TPU v7x, 32 devices: a whole 2x2x4 slice. The times are simulated.
32 devices in a mesh: dp: 16 (over z, x, core), ctx: 2 (over y).
Axes of the slice: x: 2, y: 2, z: 4, core: 2. Of those that a mesh axis runs over, the one named last changes fastest.
Arguments:
- tokens: bfloat16 [16384, 1024], P(('dp', 'ctx')), may hold values from -6 to 6
- frame_index: int32 [16384], P(('dp', 'ctx')), may hold values from 0 to 31
- row_index: int32 [16384], P(('dp', 'ctx')), may hold values from 0 to 15
- column_index: int32 [16384], P(('dp', 'ctx')), may hold values from 0 to 15
- norm1_gain: bfloat16 [1024], P(('dp', 'ctx')), may hold values from 0.5 to 1.5
- norm1_bias: bfloat16 [1024], P(('dp', 'ctx')), may hold values from -3 to 3
- qkv_weight: bfloat16 [1024, 3072], P('dp', 'ctx'), may hold values from -0.1875 to 0.1875
- qkv_bias: bfloat16 [3072], P(('dp', 'ctx')), may hold values from -0.625 to 0.625
- proj_weight: bfloat16 [1024, 1024], P('dp', 'ctx'), may hold values from -1.5 to 1.5
- proj_bias: bfloat16 [1024], P(('dp', 'ctx')), may hold values from -3 to 3
- norm2_gain: bfloat16 [1024], P(('dp', 'ctx')), may hold values from 0.5 to 1.5
- norm2_bias: bfloat16 [1024], P(('dp', 'ctx')), may hold values from -3 to 3
- up_weight: bfloat16 [1024, 4096], P('dp', 'ctx'), may hold values from -0.1875 to 0.1875
- up_bias: bfloat16 [4096], P(('dp', 'ctx')), may hold values from -3 to 3
- down_weight: bfloat16 [4096, 1024], P('dp', 'ctx'), may hold values from -0.09375 to 0.09375
- down_bias: bfloat16 [1024], P(('dp', 'ctx')), may hold values from -3 to 3
- cotangent: bfloat16 [16384, 1024], P(('dp', 'ctx')), may hold values from -6 to 6
Outputs:
- block_out: bfloat16 [16384, 1024], P(('dp', 'ctx'))
- tokens_grad: bfloat16 [16384, 1024], P(('dp', 'ctx'))
- norm1_gain_grad: float32 [1024], P(('dp', 'ctx'))
- norm1_bias_grad: float32 [1024], P(('dp', 'ctx'))
- qkv_weight_grad: float32 [1024, 3072], P('dp', 'ctx')
- qkv_bias_grad: float32 [3072], P(('dp', 'ctx'))
- proj_weight_grad: float32 [1024, 1024], P('dp', 'ctx')
- proj_bias_grad: float32 [1024], P(('dp', 'ctx'))
- norm2_gain_grad: float32 [1024], P(('dp', 'ctx'))
- norm2_bias_grad: float32 [1024], P(('dp', 'ctx'))
- up_weight_grad: float32 [1024, 4096], P('dp', 'ctx')
- up_bias_grad: float32 [4096], P(('dp', 'ctx'))
- down_weight_grad: float32 [4096, 1024], P('dp', 'ctx')
- down_bias_grad: float32 [1024], P(('dp', 'ctx'))
All inputs are finite; a program needn't handle non-finite values.
Results may differ from a plain program's by a relative error of at most 0.019.
Values may be sent and summed in bfloat16 or wider, within the bound.
No kernel may reach another device: no remote copies, remote signals or barrier semaphores. Data moves between devices by JAX's collectives and lax.ppermute only.
A program may use at most 192 MiB of HBM per device.

v0:
```python
import jax
import jax.numpy as jnp
from jax import lax
from jax.sharding import PartitionSpec as P

HEADS = 16
SPAN = 256
LEAST_LEN = 1024


EPS = 1e-06


def norm_rows(values, gain_row, shift_row):
    row_mean = jnp.mean(values, axis=-1, keepdims=True)
    centred = values - row_mean
    variance = jnp.mean(centred * centred, axis=-1, keepdims=True)
    return centred * lax.rsqrt(variance + EPS) * gain_row + shift_row


def tables(frames, patch_rows, patch_columns, head_size):
    section = 2 * (head_size // 3 // 2)
    half_size = section // 2
    frequency = 1.0 / 10000.0 ** (jnp.arange(half_size).astype(jnp.float32) / half_size)
    cosines = []
    sines = []
    for place in (frames, patch_rows, patch_columns):
        angles = place.astype(jnp.float32)[..., None] * frequency
        cosines = cosines + [jnp.cos(angles), jnp.cos(angles)]
        sines = sines + [jnp.sin(angles), jnp.sin(angles)]
    spare = head_size - 3 * section
    cosines.append(jnp.ones(frames.shape + (spare,), jnp.float32))
    sines.append(jnp.zeros(frames.shape + (spare,), jnp.float32))
    return (jnp.concatenate(cosines, axis=-1), jnp.concatenate(sines, axis=-1))


def turn_half(values):
    head_size = values.shape[-1]
    section = 2 * (head_size // 3 // 2)
    half_size = section // 2
    pieces = []
    for part_number in range(3):
        begin = part_number * section
        pieces.append(-values[..., begin + half_size : begin + section])
        pieces.append(values[..., begin : begin + half_size])
    pieces.append(jnp.zeros_like(values[..., 3 * section :]))
    return jnp.concatenate(pieces, axis=-1)


def rotary(values, cosine_table, sine_table):
    return values * cosine_table + turn_half(values) * sine_table


def rotary_back(values, cosine_table, sine_table):
    return values * cosine_table - turn_half(values * sine_table)


def shards(
    tokens,
    frame_index,
    row_index,
    column_index,
    norm1_gain,
    norm1_bias,
    qkv_weight,
    qkv_bias,
    proj_weight,
    proj_bias,
    norm2_gain,
    norm2_bias,
    up_weight,
    up_bias,
    down_weight,
    down_bias,
    cotangent,
):
    ctx_count = lax.axis_size("ctx")
    clip_length = max(LEAST_LEN, SPAN * ctx_count)
    piece_rows = clip_length // ctx_count
    rows_here, model_width = tokens.shape
    clip_count = rows_here // piece_rows
    head_size = model_width // HEADS
    score_scale = head_size ** (-0.5)
    head_shape = (clip_count, piece_rows, HEADS, head_size)
    long_shape = (clip_count, clip_length, HEADS, head_size)
    flat_shape = (clip_count, piece_rows, model_width)

    def gather_all():
        partial_value = (
            lax.all_gather(qkv_weight, "ctx", axis=1, tiled=True),
            lax.all_gather(proj_weight, "ctx", axis=1, tiled=True),
            lax.all_gather(up_weight, "ctx", axis=1, tiled=True),
            lax.all_gather(down_weight, "ctx", axis=1, tiled=True),
            lax.all_gather(norm1_gain, "ctx", axis=0, tiled=True),
            lax.all_gather(norm1_bias, "ctx", axis=0, tiled=True),
            lax.all_gather(qkv_bias, "ctx", axis=0, tiled=True),
            lax.all_gather(proj_bias, "ctx", axis=0, tiled=True),
            lax.all_gather(norm2_gain, "ctx", axis=0, tiled=True),
            lax.all_gather(norm2_bias, "ctx", axis=0, tiled=True),
            lax.all_gather(up_bias, "ctx", axis=0, tiled=True),
            lax.all_gather(down_bias, "ctx", axis=0, tiled=True),
        )
        return (
            lax.all_gather(partial_value[0], "dp", axis=0, tiled=True),
            lax.all_gather(partial_value[1], "dp", axis=0, tiled=True),
            lax.all_gather(partial_value[2], "dp", axis=0, tiled=True),
            lax.all_gather(partial_value[3], "dp", axis=0, tiled=True),
            lax.all_gather(partial_value[4], "dp", axis=0, tiled=True),
            lax.all_gather(partial_value[5], "dp", axis=0, tiled=True),
            lax.all_gather(partial_value[6], "dp", axis=0, tiled=True),
            lax.all_gather(partial_value[7], "dp", axis=0, tiled=True),
            lax.all_gather(partial_value[8], "dp", axis=0, tiled=True),
            lax.all_gather(partial_value[9], "dp", axis=0, tiled=True),
            lax.all_gather(partial_value[10], "dp", axis=0, tiled=True),
            lax.all_gather(partial_value[11], "dp", axis=0, tiled=True),
        )

    gathered = gather_all()
    (
        w_qkv,
        w_proj,
        w_up,
        w_down,
        gain_one,
        shift_one,
        bias_qkv,
        bias_proj,
        gain_two,
        shift_two,
        bias_up,
        bias_down,
    ) = gathered
    block_in = tokens.astype(jnp.float32).reshape(flat_shape)
    cosine_table, sine_table = tables(
        frame_index.reshape(clip_count, piece_rows),
        row_index.reshape(clip_count, piece_rows),
        column_index.reshape(clip_count, piece_rows),
        head_size,
    )
    cosine_table = cosine_table[:, :, None, :]
    sine_table = sine_table[:, :, None, :]
    normed = norm_rows(
        block_in, gain_one.astype(jnp.float32), shift_one.astype(jnp.float32)
    ).astype(jnp.bfloat16)
    projected = jnp.einsum(
        "spd,de->spe", normed, w_qkv, preferred_element_type=jnp.float32
    ) + bias_qkv.astype(jnp.float32)
    queries = rotary(
        projected[..., :model_width].reshape(head_shape), cosine_table, sine_table
    ).astype(jnp.bfloat16)
    keys_own = (
        rotary(
            projected[..., model_width : 2 * model_width].reshape(head_shape),
            cosine_table,
            sine_table,
        )
        .astype(jnp.bfloat16)
        .reshape(flat_shape)
    )
    values_own = projected[..., 2 * model_width :].astype(jnp.bfloat16)
    keys_all, values_all = (
        lax.all_gather(keys_own, "ctx", axis=1, tiled=True),
        lax.all_gather(values_own, "ctx", axis=1, tiled=True),
    )
    keys_all = keys_all.reshape(long_shape)
    values_all = values_all.reshape(long_shape)

    def head_forward(head_number):
        query_head = lax.dynamic_index_in_dim(queries, head_number, 2, keepdims=False)
        key_head = lax.dynamic_index_in_dim(keys_all, head_number, 2, keepdims=False)
        value_head = lax.dynamic_index_in_dim(values_all, head_number, 2, keepdims=False)
        scores = (
            jnp.einsum("sqd,skd->sqk", query_head, key_head, preferred_element_type=jnp.float32)
            * score_scale
        )
        row_top = jnp.max(scores, axis=-1, keepdims=True)
        weights = jnp.exp(scores - row_top)
        row_total = jnp.sum(weights, axis=-1, keepdims=True)
        weights_low = (weights / row_total).astype(jnp.bfloat16)
        result = jnp.einsum(
            "sqk,skd->sqd", weights_low, value_head, preferred_element_type=jnp.float32
        )
        return (result, (row_top + jnp.log(row_total))[..., 0])

    head_numbers = jnp.arange(HEADS, dtype=jnp.int32)
    attended, log_total = lax.map(head_forward, head_numbers)
    attended_low = jnp.transpose(attended, (1, 2, 0, 3)).reshape(flat_shape).astype(jnp.bfloat16)
    branch = jnp.einsum(
        "spd,de->spe", attended_low, w_proj, preferred_element_type=jnp.float32
    ) + bias_proj.astype(jnp.float32)
    middle = block_in + branch
    second = norm_rows(middle, gain_two.astype(jnp.float32), shift_two.astype(jnp.float32)).astype(
        jnp.bfloat16
    )
    hidden = jnp.einsum(
        "spd,df->spf", second, w_up, preferred_element_type=jnp.float32
    ) + bias_up.astype(jnp.float32)
    active = jax.nn.gelu(hidden, approximate=False).astype(jnp.bfloat16)
    output = jnp.einsum(
        "spf,fd->spd", active, w_down, preferred_element_type=jnp.float32
    ) + bias_down.astype(jnp.float32)
    block_out = (middle + output).astype(jnp.bfloat16).reshape(rows_here, model_width)
    backward_weights = gather_all()
    (
        w_qkv,
        w_proj,
        w_up,
        w_down,
        gain_one,
        shift_one,
        bias_qkv,
        bias_proj,
        gain_two,
        shift_two,
        bias_up,
        bias_down,
    ) = backward_weights
    out_low = cotangent.reshape(flat_shape)
    out_grad = out_low.astype(jnp.float32)
    grad_down_bias = jnp.sum(out_grad, axis=(0, 1))
    grad_down = jnp.einsum("spf,spd->fd", active, out_low, preferred_element_type=jnp.float32)
    active_grad = jnp.einsum("spd,fd->spf", out_low, w_down, preferred_element_type=jnp.float32)
    gelu_pull = jax.vjp(lambda inner: jax.nn.gelu(inner, approximate=False), hidden)[1]
    hidden_grad = gelu_pull(active_grad)[0].astype(jnp.bfloat16)
    grad_up_bias = jnp.sum(hidden_grad.astype(jnp.float32), axis=(0, 1))
    grad_up = jnp.einsum("spd,spf->df", second, hidden_grad, preferred_element_type=jnp.float32)
    second_grad = jnp.einsum("spf,df->spd", hidden_grad, w_up, preferred_element_type=jnp.float32)
    second_pull = jax.vjp(
        norm_rows, middle, gain_two.astype(jnp.float32), shift_two.astype(jnp.float32)
    )[1]
    middle_part, grad_gain_two, grad_shift_two = second_pull(second_grad)
    middle_grad = out_grad + middle_part
    branch_low = middle_grad.astype(jnp.bfloat16)
    grad_proj_bias = jnp.sum(branch_low.astype(jnp.float32), axis=(0, 1))
    grad_proj = jnp.einsum(
        "spd,spe->de", attended_low, branch_low, preferred_element_type=jnp.float32
    )
    attended_grad = (
        jnp.einsum("spe,de->spd", branch_low, w_proj, preferred_element_type=jnp.float32)
        .astype(jnp.bfloat16)
        .reshape(head_shape)
    )

    def head_backward(head_number):
        query_head = lax.dynamic_index_in_dim(queries, head_number, 2, keepdims=False)
        key_head = lax.dynamic_index_in_dim(keys_all, head_number, 2, keepdims=False)
        value_head = lax.dynamic_index_in_dim(values_all, head_number, 2, keepdims=False)
        grad_head = lax.dynamic_index_in_dim(attended_grad, head_number, 2, keepdims=False)
        log_head = lax.dynamic_index_in_dim(log_total, head_number, 0, keepdims=False)
        scores = (
            jnp.einsum("sqd,skd->sqk", query_head, key_head, preferred_element_type=jnp.float32)
            * score_scale
        )
        weights = jnp.exp(scores - log_head[..., None])
        weights_low = weights.astype(jnp.bfloat16)
        value_grad = jnp.einsum(
            "sqk,sqd->skd", weights_low, grad_head, preferred_element_type=jnp.float32
        )
        weight_grad = jnp.einsum(
            "sqd,skd->sqk", grad_head, value_head, preferred_element_type=jnp.float32
        )
        score_grad = (
            weights * (weight_grad - jnp.sum(weights * weight_grad, axis=-1, keepdims=True))
        ).astype(jnp.bfloat16)
        query_grad = (
            jnp.einsum("sqk,skd->sqd", score_grad, key_head, preferred_element_type=jnp.float32)
            * score_scale
        )
        key_grad = (
            jnp.einsum("sqk,sqd->skd", score_grad, query_head, preferred_element_type=jnp.float32)
            * score_scale
        )
        return (query_grad, key_grad, value_grad)

    query_grads, key_grads, value_grads = lax.map(head_backward, head_numbers)
    key_full = jnp.transpose(key_grads, (1, 2, 0, 3)).reshape(clip_count, clip_length, model_width)
    value_full = jnp.transpose(value_grads, (1, 2, 0, 3)).reshape(
        clip_count, clip_length, model_width
    )
    key_part, value_part = (
        lax.psum_scatter(
            key_full.astype(jnp.bfloat16), "ctx", scatter_dimension=1, tiled=True
        ).astype(jnp.float32),
        lax.psum_scatter(
            value_full.astype(jnp.bfloat16), "ctx", scatter_dimension=1, tiled=True
        ).astype(jnp.float32),
    )
    query_grads = jnp.transpose(query_grads, (1, 2, 0, 3))
    query_back = rotary_back(query_grads, cosine_table, sine_table).reshape(flat_shape)
    key_back = rotary_back(key_part.reshape(head_shape), cosine_table, sine_table).reshape(
        flat_shape
    )
    mixed_grad = jnp.concatenate([query_back, key_back, value_part], axis=-1).astype(jnp.bfloat16)
    grad_qkv_bias = jnp.sum(mixed_grad.astype(jnp.float32), axis=(0, 1))
    grad_qkv = jnp.einsum("spd,spe->de", normed, mixed_grad, preferred_element_type=jnp.float32)
    normed_grad = jnp.einsum("spe,de->spd", mixed_grad, w_qkv, preferred_element_type=jnp.float32)
    first_pull = jax.vjp(
        norm_rows, block_in, gain_one.astype(jnp.float32), shift_one.astype(jnp.float32)
    )[1]
    input_part, grad_gain_one, grad_shift_one = first_pull(normed_grad)
    tokens_grad = (middle_grad + input_part).astype(jnp.bfloat16).reshape(rows_here, model_width)
    summed = (
        lax.psum_scatter(
            grad_qkv.astype(jnp.bfloat16), "dp", scatter_dimension=0, tiled=True
        ).astype(jnp.float32),
        lax.psum_scatter(
            grad_proj.astype(jnp.bfloat16), "dp", scatter_dimension=0, tiled=True
        ).astype(jnp.float32),
        lax.psum_scatter(
            grad_up.astype(jnp.bfloat16), "dp", scatter_dimension=0, tiled=True
        ).astype(jnp.float32),
        lax.psum_scatter(
            grad_down.astype(jnp.bfloat16), "dp", scatter_dimension=0, tiled=True
        ).astype(jnp.float32),
        lax.psum_scatter(
            grad_gain_one.astype(jnp.bfloat16), "dp", scatter_dimension=0, tiled=True
        ).astype(jnp.float32),
        lax.psum_scatter(
            grad_shift_one.astype(jnp.bfloat16), "dp", scatter_dimension=0, tiled=True
        ).astype(jnp.float32),
        lax.psum_scatter(
            grad_qkv_bias.astype(jnp.bfloat16), "dp", scatter_dimension=0, tiled=True
        ).astype(jnp.float32),
        lax.psum_scatter(
            grad_proj_bias.astype(jnp.bfloat16), "dp", scatter_dimension=0, tiled=True
        ).astype(jnp.float32),
        lax.psum_scatter(
            grad_gain_two.astype(jnp.bfloat16), "dp", scatter_dimension=0, tiled=True
        ).astype(jnp.float32),
        lax.psum_scatter(
            grad_shift_two.astype(jnp.bfloat16), "dp", scatter_dimension=0, tiled=True
        ).astype(jnp.float32),
        lax.psum_scatter(
            grad_up_bias.astype(jnp.bfloat16), "dp", scatter_dimension=0, tiled=True
        ).astype(jnp.float32),
        lax.psum_scatter(
            grad_down_bias.astype(jnp.bfloat16), "dp", scatter_dimension=0, tiled=True
        ).astype(jnp.float32),
    )
    owned = (
        lax.psum_scatter(
            summed[0].astype(jnp.bfloat16), "ctx", scatter_dimension=1, tiled=True
        ).astype(jnp.float32),
        lax.psum_scatter(
            summed[1].astype(jnp.bfloat16), "ctx", scatter_dimension=1, tiled=True
        ).astype(jnp.float32),
        lax.psum_scatter(
            summed[2].astype(jnp.bfloat16), "ctx", scatter_dimension=1, tiled=True
        ).astype(jnp.float32),
        lax.psum_scatter(
            summed[3].astype(jnp.bfloat16), "ctx", scatter_dimension=1, tiled=True
        ).astype(jnp.float32),
        lax.psum_scatter(
            summed[4].astype(jnp.bfloat16), "ctx", scatter_dimension=0, tiled=True
        ).astype(jnp.float32),
        lax.psum_scatter(
            summed[5].astype(jnp.bfloat16), "ctx", scatter_dimension=0, tiled=True
        ).astype(jnp.float32),
        lax.psum_scatter(
            summed[6].astype(jnp.bfloat16), "ctx", scatter_dimension=0, tiled=True
        ).astype(jnp.float32),
        lax.psum_scatter(
            summed[7].astype(jnp.bfloat16), "ctx", scatter_dimension=0, tiled=True
        ).astype(jnp.float32),
        lax.psum_scatter(
            summed[8].astype(jnp.bfloat16), "ctx", scatter_dimension=0, tiled=True
        ).astype(jnp.float32),
        lax.psum_scatter(
            summed[9].astype(jnp.bfloat16), "ctx", scatter_dimension=0, tiled=True
        ).astype(jnp.float32),
        lax.psum_scatter(
            summed[10].astype(jnp.bfloat16), "ctx", scatter_dimension=0, tiled=True
        ).astype(jnp.float32),
        lax.psum_scatter(
            summed[11].astype(jnp.bfloat16), "ctx", scatter_dimension=0, tiled=True
        ).astype(jnp.float32),
    )
    return (
        block_out,
        tokens_grad,
        owned[4],
        owned[5],
        owned[0],
        owned[6],
        owned[1],
        owned[7],
        owned[8],
        owned[9],
        owned[2],
        owned[10],
        owned[3],
        owned[11],
    )


def solution(mesh):
    placed = (
        P(("dp", "ctx"), None),
        P(("dp", "ctx")),
        P(("dp", "ctx")),
        P(("dp", "ctx")),
        P(("dp", "ctx")),
        P(("dp", "ctx")),
        P("dp", "ctx"),
        P(("dp", "ctx")),
        P("dp", "ctx"),
        P(("dp", "ctx")),
        P(("dp", "ctx")),
        P(("dp", "ctx")),
        P("dp", "ctx"),
        P(("dp", "ctx")),
        P("dp", "ctx"),
        P(("dp", "ctx")),
        P(("dp", "ctx"), None),
    )
    return jax.shard_map(
        shards,
        mesh=mesh,
        in_specs=placed,
        out_specs=(
            P(("dp", "ctx"), None),
            P(("dp", "ctx"), None),
            P(("dp", "ctx")),
            P(("dp", "ctx")),
            P("dp", "ctx"),
            P(("dp", "ctx")),
            P("dp", "ctx"),
            P(("dp", "ctx")),
            P(("dp", "ctx")),
            P(("dp", "ctx")),
            P("dp", "ctx"),
            P(("dp", "ctx")),
            P("dp", "ctx"),
            P(("dp", "ctx")),
        ),
        check_vma=False,
    )
```

profile of v0, /device:TPU:1, one launch (start us, length us, event | category | flops | bytes accessed | tf_op | source)
XLA Modules:
  0.0 1098.7 jit_solution(12408808714704723745)
XLA Ops:
  7.2 9.3 all_gather.94
  32.4 58.2 %all-reduce.31 = (bf16[3072]{0:T(1024)(128)(2,1)S(1)}, bf16[1024]{0:T(1024)(128)(2,1)S(1)}, bf16[1024]{0:T(1024)(128)(2,1)S(1)}, bf16[1024]{0:T(1024)(128)(2,1)S...) all-reduce(bf16[3072]{0:T(1024)(128)(2,1)S(1)} %dynamic-update-slic, ...), channel_id=1, replica_groups=mesh['dp'=16,'ctx'=2] {'dp'}, use_global_device_ids=true, to_apply=%add.5 | all-reduce | flops 8192 | bytes 32768
  112.8 22.7 %concatenate.65 = f32[1,512,16,64]{1,3,2,0:T(8,128)} concatenate(f32[1,512,16,10]{1,3,2,0:T(8,128)} %get-tuple-element.212, f32[1,512,16,10]{1,3,2,0:T(8,128)} %get-tuple-element.211, f32[1,512,16,10]{1,3,2,0:T(8,128)} %get-tuple-element.210, f32[1,512,16,10]{1,3,2,0:T(8,128)} %get-tuple-element.209, f32[1,512,16,10]{1,3,2,0:T(8,128)} %get-tuple-element.208, ...), dimensions={3} | concatenate | bytes 4194304 | tf_op jit(solution)/shard_map/concatenate | solution.py:47
  151.6 10.4 all_gather.108
  162.1 14.0 %all_gather.112 = bf16[256,1024]{1,0:T(8,128)(2,1)} all-gather(bf16[256,512]{1,0:T(8,128)(2,1)S(1)} %copy-done.20), channel_id=1, replica_groups=mesh['dp'=16,'ctx'=2] {'ctx'}, dimensions={1}, use_global_device_ids=true | all-gather | bytes 786432 | tf_op jit(solution)/shard_map/all_gather | solution.py:93
  180.8 29.0 %all-gather.1 = bf16[16,1,256]{2,1,0:T(2,128)(2,1)S(1)} all-gather(bf16[1,1,256]{2,1,0:T(2,128)(2,1)S(1)} %bitcast.227), channel_id=1, replica_groups=mesh['dp'=16,'ctx'=2] {'dp'}, dimensions={0}, use_global_device_ids=true | all-gather | bytes 8704 | tf_op jit(solution)/shard_map/all_gather | solution.py:114
  214.0 22.7 %concatenate.63 = f32[1,512,16,64]{1,3,2,0:T(8,128)} concatenate(f32[1,512,16,10]{1,3,2,0:T(8,128)} %get-tuple-element.218, f32[1,512,16,10]{1,3,2,0:T(8,128)} %get-tuple-element.217, f32[1,512,16,10]{1,3,2,0:T(8,128)} %get-tuple-element.216, f32[1,512,16,10]{1,3,2,0:T(8,128)} %get-tuple-element.215, f32[1,512,16,10]{1,3,2,0:T(8,128)} %get-tuple-element.214, ...), dimensions={3} | concatenate | bytes 4194304 | tf_op jit(solution)/shard_map/concatenate | solution.py:47
  246.7 116.0 %while.28 = (s32[]{:T(128)}, bf16[16,1,512,64]{2,3,1,0:T(8,128)(2,1)}, f32[16,1,512]{2,1,0:T(1,128)}, s32[16]{0:T(128)S(1)}, bf16[1,512,16,64]{1,3,2,0:T(8,128)(...) while((s32[]{:T(128)}, bf16[16,1,512,64]{2,3,1,0:T(8,128)(2,1)}, ...), condition=%wide.region_5.6_spmd.clone, body=%wide.region_2.5_spmd.sunk.clone | while | flops 138935808 | bytes 6771855 | solution.py:186
  367.7 10.7 fusion.68
  378.3 39.5 %all-gather.19.cloned.1.call-done = bf16[4096,1024]{1,0:T(8,128)(2,1)} async-done(((bf16[256,1024]{1,0:T(8,128)(2,1)}), bf16[4096,1024]{1,0:T(8,128)(2,1)}) %all-gather.19.cloned.1.call-update) | async-done | bytes 8388624 | tf_op jit(solution)/shard_map/all_gather | solution.py:107
  417.8 28.0 %fusion.70 = (bf16[4096]{0:T(1024)(128)(2,1)S(1)}, bf16[512,4096]{1,0:T(8,128)(2,1)S(1)}, f32[512,4096]{1,0:T(8,128)}) fusion(f32[512,4096]{1,0:T(8,128)} %fusion.68, f32[4096]{0:T(1024)S(1)} %bitcast.225, bf16[512,1024]{1,0:T(8,128)(2,1)S(1)} %copy-done.6, bf16[4096,1024]{1,0:T(8,128)(2,1)} %all-gather.19.cloned.1.call-done), kind=kOutput, calls=%fused_computation.157 | convolution fusion | flops 4450152448 | bytes 30433280 | tf_op jit(solution)/shard_map/spd,fd->spf/dot_general | solution.py:222
  463.9 194.3 %while.29 = (s32[]{:T(128)}, f32[16,1,512,64]{2,3,1,0:T(8,128)}, bf16[16,1,1024,64]{2,3,1,0:T(8,128)(2,1)}, bf16[16,1,1024,64]{2,3,1,0:T(8,128)(2,1)}, s32[16]{0...) while((s32[]{:T(128)}, f32[16,1,512,64]{2,3,1,0:T(8,128)}, ...), condition=%wide.region_12.13_spmd.clone, body=%wide.region_10.12_spmd.sunk.clone | while | flops 339836416 | bytes 17051832 | solution.py:275
  659.8 10.8 convolution_convert_fusion.1
  670.6 9.8 multiply_convert_fusion.1
  693.8 22.5 %concatenate.67 = f32[1,512,16,64]{1,3,2,0:T(8,128)} concatenate(f32[1,512,16,10]{1,3,2,0:T(8,128)} %get-tuple-element.200, f32[1,512,16,10]{1,3,2,0:T(8,128)} %get-tuple-element.199, f32[1,512,16,10]{1,3,2,0:T(8,128)} %get-tuple-element.198, f32[1,512,16,10]{1,3,2,0:T(8,128)} %get-tuple-element.197, f32[1,512,16,10]{1,3,2,0:T(8,128)} %get-tuple-element.196, ...), dimensions={3} | concatenate | bytes 4194304 | tf_op jit(solution)/shard_map/concatenate | solution.py:47
  723.3 22.4 %concatenate.69 = f32[1,512,16,64]{1,3,2,0:T(8,128)} concatenate(f32[1,512,16,10]{1,3,2,0:T(8,128)} %get-tuple-element.206, f32[1,512,16,10]{1,3,2,0:T(8,128)} %get-tuple-element.205, f32[1,512,16,10]{1,3,2,0:T(8,128)} %get-tuple-element.204, f32[1,512,16,10]{1,3,2,0:T(8,128)} %get-tuple-element.203, f32[1,512,16,10]{1,3,2,0:T(8,128)} %get-tuple-element.202, ...), dimensions={3} | concatenate | bytes 4194304 | tf_op jit(solution)/shard_map/concatenate | solution.py:47
  774.3 69.6 %reduce-scatter.23.cloned.1.call-done = bf16[64,4096]{1,0:T(8,128)(2,1)} async-done(((bf16[1024,4096]{1,0:T(8,128)(2,1)}), bf16[64,4096]{1,0:T(8,128)(2,1)}) %reduce-scatter.23.cloned.1.call-update) | async-done | bytes 524304 | tf_op jit(solution)/shard_map/reduce_scatter | solution.py:309
  846.8 57.1 %all-reduce.30 = (bf16[1024]{0:T(1024)(128)(2,1)S(1)}, bf16[1024]{0:T(1024)(128)(2,1)S(1)}, bf16[1024]{0:T(1024)(128)(2,1)S(1)}, bf16[3072]{0:T(1024)(128)(2,1)S...) all-reduce(bf16[1024]{0:T(1024)(128)(2,1)S(1)} %dynamic-update-slic, ...), channel_id=1, replica_groups=mesh['dp'=16,'ctx'=2] {'dp'}, use_global_device_ids=true, to_apply=%add.13 | all-reduce | flops 14336 | bytes 57344
  912.2 40.5 %reduce-scatter.27.cloned.1.call-done = bf16[256,1024]{1,0:T(8,128)(2,1)} async-done(((bf16[4096,1024]{1,0:T(8,128)(2,1)}), bf16[256,1024]{1,0:T(8,128)(2,1)}) %reduce-scatter.27.cloned.1.call-update) | async-done | bytes 524304 | tf_op jit(solution)/shard_map/reduce_scatter | solution.py:312
  952.8 10.6 add_convert_fusion.2
  963.4 78.0 %reduce-scatter.15.cloned.1.call-done = bf16[64,3072]{1,0:T(8,128)(2,1)} async-done(((bf16[1024,3072]{1,0:T(8,128)(2,1)}), bf16[64,3072]{1,0:T(8,128)(2,1)}) %reduce-scatter.15.cloned.1.call-update) | async-done | bytes 393232 | tf_op jit(solution)/shard_map/reduce_scatter | solution.py:303
  1045.8 12.2 %reduce-scatter.25.cloned.1.call-done = bf16[64,2048]{1,0:T(8,128)(2,1)} async-done(((bf16[64,4096]{1,0:T(8,128)(2,1)}), bf16[64,2048]{1,0:T(8,128)(2,1)}) %reduce-scatter.25.cloned.1.call-update) | async-done | bytes 262160 | tf_op jit(solution)/shard_map/reduce_scatter | solution.py:347
  1059.8 15.0 %reduce-scatter.29.cloned.1.call-done = bf16[256,512]{1,0:T(8,128)(2,1)} async-done(((bf16[256,1024]{1,0:T(8,128)(2,1)}), bf16[256,512]{1,0:T(8,128)(2,1)}) %reduce-scatter.29.cloned.1.call-update) | async-done | bytes 262160 | tf_op jit(solution)/shard_map/reduce_scatter | solution.py:350
  1076.6 13.5 %reduce-scatter.17.cloned.1.call-done = bf16[64,1536]{1,0:T(8,128)(2,1)} async-done(((bf16[64,3072]{1,0:T(8,128)(2,1)}), bf16[64,1536]{1,0:T(8,128)(2,1)}) %reduce-scatter.17.cloned.1.call-update) | async-done | bytes 196624 | tf_op jit(solution)/shard_map/reduce_scatter | solution.py:341
  (463 shorter events, 408.3 us)
Async XLA Ops:
  7.2 92.0 %all-gather.9.cloned.1.call-start = ((), (), s32[]{:S(2)}) async-start(), calls=%async_computation.10 | async-start | bytes 6684672 | tf_op jit(solution)/shard_map/all_gather | solution.py:104
  16.6 223.3 %all-gather.11.cloned.1.call-start = ((), (), s32[]{:S(2)}) async-start(), calls=%async_computation.11 | async-start | bytes 3145728 | tf_op jit(solution)/shard_map/all_gather | solution.py:162
  93.7 143.0 %copy-start.11 = (f32[1,512,64]{1,2,0:T(8,128)}, f32[1,512,64]{1,2,0:T(8,128)S(1)}, u32[]{:S(2)}) copy-start(f32[1,512,64]{1,2,0:T(8,128)S(1)} %concatenate.64) | copy-start | bytes 393220
  96.3 140.4 %copy-start.13 = (f32[1,512,64]{1,2,0:T(8,128)}, f32[1,512,64]{1,2,0:T(8,128)S(1)}, u32[]{:S(2)}) copy-start(f32[1,512,64]{1,2,0:T(8,128)S(1)} %concatenate.61) | copy-start | bytes 393220
  112.8 101.2 %copy-start.15 = (f32[1,512,16,4]{1,3,2,0:T(4,128)}, f32[1,512,16,4]{1,3,2,0:T(4,128)S(1)}, u32[]{:S(2)}) copy-start(f32[1,512,16,4]{1,3,2,0:T(4,128)S(1)} %concatenate.62) | copy-start | bytes 393220
  144.7 98.0 %all-gather.13.cloned.1.call-start = ((), (), s32[]{:S(2)}) async-start(), calls=%async_computation.12 | async-start | bytes 3145728 | tf_op jit(solution)/shard_map/all_gather | solution.py:163
  147.6 29.7 %copy-start.34 = (bf16[128]{0:T(256)(128)(2,1)S(1)}, bf16[128]{0:T(256)(128)(2,1)}, u32[]{:S(2)}) copy-start(bf16[128]{0:T(256)(128)(2,1)} %param.34) | copy-start | bytes 772
  147.6 215.1 %all-gather.15.cloned.1.call-start = ((), (), s32[]{:S(2)}) async-start(), calls=%async_computation.13 | async-start | bytes 2228224 | tf_op jit(solution)/shard_map/all_gather | solution.py:105
  151.6 216.1 %all-gather.17.cloned.1.call-start = ((), (), s32[]{:S(2)}) async-start(), calls=%async_computation.14 | async-start | bytes 8912896 | tf_op jit(solution)/shard_map/all_gather | solution.py:106
  162.1 255.7 %all-gather.19.cloned.1.call-start = ((), (), s32[]{:S(2)}) async-start(), calls=%async_computation.15 | async-start | bytes 8912896 | tf_op jit(solution)/shard_map/all_gather | solution.py:107
  176.1 482.9 %reduce-scatter.19.cloned.1.call-start = ((), (), s32[]{:S(2)}) async-start(), calls=%async_computation.20 | async-start | bytes 2228224 | tf_op jit(solution)/shard_map/reduce_scatter | solution.py:306
  367.3 78.5 %copy-start.2 = (f32[512,1024]{1,0:T(8,128)}, f32[512,1024]{1,0:T(8,128)S(1)}, u32[]{:S(2)}) copy-start(f32[512,1024]{1,0:T(8,128)S(1)} %get-tuple-element.235) | copy-start | bytes 6291460
  367.6 50.2 %copy-start.6 = (bf16[512,1024]{1,0:T(8,128)(2,1)S(1)}, bf16[512,1024]{1,0:T(8,128)(2,1)}, u32[]{:S(2)}) copy-start(bf16[512,1024]{1,0:T(8,128)(2,1)} %param.37) | copy-start | bytes 3145732
  367.6 50.2 %copy-start.22 = (f32[16,1,256]{2,1,0:T(1,128)S(1)}, f32[16,1,256]{2,1,0:T(1,128)}, u32[]{:S(2)}) copy-start(f32[16,1,256]{2,1,0:T(1,128)} %convert_element_type.327) | copy-start | bytes 49156
  463.9 256.3 %reduce-scatter.11.cloned.1.call-start = ((), (), s32[]{:S(2)}) async-start(), calls=%async_computation.16 | async-start | bytes 3145728 | tf_op jit(solution)/shard_map/reduce_scatter | solution.py:281
  658.2 91.1 %reduce-scatter.13.cloned.1.call-start = ((), (), s32[]{:S(2)}) async-start(), calls=%async_computation.17 | async-start | bytes 3145728 | tf_op jit(solution)/shard_map/reduce_scatter | solution.py:284
  658.9 103.4 %reduce-scatter.21.cloned.1.call-start = ((), (), s32[]{:S(2)}) async-start(), calls=%async_computation.21 | async-start | bytes 196608 | tf_op jit(solution)/shard_map/reduce_scatter | solution.py:344
  659.5 184.3 %reduce-scatter.23.cloned.1.call-start = ((), (), s32[]{:S(2)}) async-start(), calls=%async_computation.22 | async-start | bytes 8912896 | tf_op jit(solution)/shard_map/reduce_scatter | solution.py:309
  670.6 282.1 %reduce-scatter.27.cloned.1.call-start = ((), (), s32[]{:S(2)}) async-start(), calls=%async_computation.24 | async-start | bytes 8912896 | tf_op jit(solution)/shard_map/reduce_scatter | solution.py:312
  689.5 351.9 %reduce-scatter.15.cloned.1.call-start = ((), (), s32[]{:S(2)}) async-start(), calls=%async_computation.18 | async-start | bytes 6684672 | tf_op jit(solution)/shard_map/reduce_scatter | solution.py:303
  758.1 299.9 %reduce-scatter.25.cloned.1.call-start = ((), (), s32[]{:S(2)}) async-start(), calls=%async_computation.23 | async-start | bytes 786432 | tf_op jit(solution)/shard_map/reduce_scatter | solution.py:347
  766.4 77.8 %copy-start.28 = (f32[512]{0:T(512)S(1)}, f32[512]{0:T(512)}, u32[]{:S(2)}) copy-start(f32[512]{0:T(512)} %copy-done.27) | copy-start | bytes 6148
  843.9 230.9 %reduce-scatter.29.cloned.1.call-start = ((), (), s32[]{:S(2)}) async-start(), calls=%async_computation.25 | async-start | bytes 786432 | tf_op jit(solution)/shard_map/reduce_scatter | solution.py:350
  952.7 137.3 %reduce-scatter.17.cloned.1.call-start = ((), (), s32[]{:S(2)}) async-start(), calls=%async_computation.19 | async-start | bytes 589824 | tf_op jit(solution)/shard_map/reduce_scatter | solution.py:341
  (29 other events, 168.7 us)
Sparse Core Ops, SparseCore 0:
  16.7 63.8 all-gather.8
  144.8 44.7 all-gather.10
  191.2 31.6 all-gather.12
  224.9 41.9 all-gather.14
  268.9 73.6 all-gather.16
  344.6 73.1 all-gather.18
  464.0 57.8 reduce-scatter.18
  658.3 29.6 reduce-scatter.10
  690.3 31.8 reduce-scatter.12
  724.3 10.1 reduce-scatter.20
  739.1 104.7 reduce-scatter.22
  848.3 104.3 reduce-scatter.26
  957.1 84.2 reduce-scatter.14
  1043.5 14.4 reduce-scatter.24
  1060.2 14.5 reduce-scatter.28
  1076.9 13.1 reduce-scatter.16
where the time goes:
time: 1110 us; the launch traced here: 1100 us
  matrix products  303 us (27%)
  waiting for transfers between devices  270 us (24%)
  blocking collectives  194 us (17%)
  local copies, waits for them, and re-layouts  170 us (15%)
  other arithmetic  76.8 us (7%)
  loops' own time  62.5 us (6%)
  between operations  21.5 us (2%)
    unnamed x4, blocking collectives  124 us
    concatenate x6, local copies, waits for them, and re-layouts, turn_half(): return jnp.concatenate(pieces, axis=-1)  93.4 us
    reduce_scatter x1, waiting for transfers between devices, shards(): lax.psum_scatter(grad_qkv.astype(jnp.bfloat16), 'dp', scatter_dimension=0...  78 us
    reduce_scatter x1, waiting for transfers between devices, shards(): lax.psum_scatter(grad_up.astype(jnp.bfloat16), 'dp', scatter_dimension=0,...  69.6 us
    reduce_scatter x1, waiting for transfers between devices, shards(): lax.psum_scatter(grad_down.astype(jnp.bfloat16), 'dp', scatter_dimension=...  40.5 us
    all_gather x1, waiting for transfers between devices, gather_all(): lax.all_gather(partial_value[3], 'dp', axis=0, tiled=True)  39.5 us
    dot_general x16, matrix products, head_forward(): jnp.einsum('sqk,skd->sqd', weights_low, value_head, preferred_element_typ...  35.5 us
    dot_general x16, matrix products, head_backward(): jnp.einsum('sqk,skd->sqd', score_grad, key_head, preferred_element_type=j...  32.1 us
  transfers between devices with their start and end apart: 16, of which 7 were waited for; matrix products, arithmetic and copies ran while one was open for 41% of the time, Pallas kernels for 0%

commit v1 on v0

--- a/solution.py
+++ b/solution.py
@@ -1,6 +1,12 @@
+import functools
+import math
+
 import jax
 import jax.numpy as jnp
 from jax import lax
+from jax.experimental import pallas as pl
+from jax.experimental.pallas import tpu as pltpu
+from jax.sharding import Mesh
 from jax.sharding import PartitionSpec as P
 
 HEADS = 16
@@ -393,45 +399,1189 @@
     )
 
 
+LOG2E = 1.4426950408889634
+COST = 0.1
+NT = (((1,), (1,)), ((), ()))
+NN = (((1,), (0,)), ((), ()))
+TN = (((0,), (0,)), ((), ()))
+F32 = jnp.float32
+BF16 = jnp.bfloat16
+SWAP = [(0, 1), (1, 0)]
+DIAGONAL = [(0, 0), (1, 2), (2, 1), (3, 3)]
+ANYWHERE = pl.BlockSpec(memory_space=pl.ANY)
+WHOLE = pl.BlockSpec(memory_space=pltpu.VMEM)
+SCALARS = pl.BlockSpec(memory_space=pltpu.SMEM)
+
+
+def shape_of(shape, kind):
+    return jax.ShapeDtypeStruct(shape, kind)
+
+
+def half_lanes(number, shape):
+    lane = lax.broadcasted_iota(jnp.int32, shape, 1)
+    width = shape[1] // 2
+    return (lane < width) if number == 0 else (lane >= width)
+
+
+def keep(mask, values):
+    return jnp.where(mask, values, jnp.zeros_like(values))
+
+
+def dot(first, second, dims, to=F32):
+    return lax.dot_general(first, second, dims, preferred_element_type=F32).astype(to)
+
+
+def kernel_call(
+    body, inputs, in_specs, out_shapes, scratch=(), grid=None, out_specs=None, flops=0, exps=0, room=8
+):
+    def size(item):
+        return item.size * item.dtype.itemsize
+
+    total = sum(size(a) for a in inputs) + sum(size(s) for s in out_shapes)
+    if out_specs is None:
+        out_specs = [WHOLE] * len(out_shapes)
+    need = room << 20
+    if grid is None:
+        need += sum(size(a) for a, spec in zip(inputs, in_specs) if spec is WHOLE)
+        need += sum(size(a) for a, spec in zip(out_shapes, out_specs) if spec is WHOLE)
+    for item in scratch:
+        if getattr(item, "memory_space", None) == pltpu.VMEM:
+            need += math.prod(item.shape) * jnp.dtype(item.dtype).itemsize
+    extra = {} if grid is None else {"grid": grid}
+    return pl.pallas_call(
+        body,
+        in_specs=in_specs,
+        out_specs=out_specs,
+        out_shape=out_shapes,
+        scratch_shapes=list(scratch),
+        compiler_params=pltpu.CompilerParams(vmem_limit_bytes=min(need, 56 << 20)),
+        cost_estimate=pl.CostEstimate(
+            flops=int(flops * COST),
+            bytes_accessed=int(total * COST),
+            transcendentals=int(exps * COST),
+        ),
+        **extra,
+    )(*inputs)
+
+
+def after(values, *others):
+    return lax.optimization_barrier((values,) + others)[0]
+
+
+def swap(values, axis):
+    return lax.ppermute(values, axis, SWAP)
+
+
+def ring(values, depth):
+    return lax.ppermute(values, "z", [(i, (i + 1) % depth) for i in range(depth)])
+
+
+def gather_first(block, depth):
+    hops = [block]
+    for _ in range(depth - 1):
+        hops.append(ring(hops[-1], depth))
+    one = jnp.stack([hop[0] for hop in hops])
+    two = jnp.stack([hop[1] for hop in hops])
+    one_x = swap(one, "x")
+    two_y = swap(two, "y")
+    one_y = swap(one, "y")
+    two_x = swap(two, "x")
+    one_xy = swap(one_x, "y")
+    two_xy = swap(two_y, "x")
+    arrays = [one, two, one_x, two_y, one_y, two_x, one_xy, two_xy]
+    marks = [(0, 0, 0), (1, 0, 0), (0, 1, 0), (1, 0, 1), (0, 0, 1), (1, 1, 0), (0, 1, 1), (1, 1, 1)]
+    parts = [
+        (n, z, half, z, x, y)
+        for n, (half, x, y) in enumerate(marks)
+        for z in range(depth)
+    ]
+    return arrays, parts, hops[-1], (one_xy, two_xy)
+
+
+def gather_middle(block, depth, hop_gate, swap_gate):
+    one, two = block[0], block[1]
+    hop = jnp.stack([one, swap(one, "x"), two, swap(two, "y")])
+    hops = [hop]
+    for _ in range(depth - 1):
+        hops.append(ring(after(hops[-1], hop_gate), depth))
+    arrays = []
+    parts = []
+    for z in range(depth):
+        parts += [
+            (len(arrays), 0, 0, z, 0, 0),
+            (len(arrays), 1, 0, z, 1, 0),
+            (len(arrays), 2, 1, z, 0, 0),
+            (len(arrays), 3, 1, z, 0, 1),
+        ]
+        arrays.append(hops[z])
+    step = max(depth // 2, 1)
+    for begin in range(0, depth, step):
+        group = hops[begin : begin + step]
+        ones = swap(after(jnp.concatenate([hop[:2] for hop in group]), swap_gate[0]), "y")
+        twos = swap(after(jnp.concatenate([hop[2:] for hop in group]), swap_gate[1]), "x")
+        swap_gate = (ones, twos)
+        for k in range(step):
+            z = begin + k
+            parts += [
+                (len(arrays), 2 * k, 0, z, 0, 1),
+                (len(arrays), 2 * k + 1, 0, z, 1, 1),
+                (len(arrays) + 1, 2 * k, 1, z, 1, 0),
+                (len(arrays) + 1, 2 * k + 1, 1, z, 1, 1),
+            ]
+        arrays += [ones, twos]
+    return arrays, parts, hops[-1], swap_gate
+
+
+def gather_single(block, depth, first, last, hop_gate, swap_gate):
+    hops = [jnp.stack([block, swap(block, first)])]
+    for _ in range(depth - 1):
+        hops.append(ring(after(hops[-1], hop_gate), depth))
+    arrays = []
+    parts = []
+
+    def part(array, index, z, near, far):
+        x, y = (near, far) if first == "x" else (far, near)
+        return (array, index, 0, z, x, y)
+
+    for z in range(depth):
+        parts += [part(len(arrays), k, z, k, 0) for k in range(2)]
+        arrays.append(hops[z])
+    step = max(depth // 2, 1)
+    for begin in range(0, depth, step):
+        group = jnp.concatenate(hops[begin : begin + step])
+        for k in range(2 * step):
+            parts.append(part(len(arrays), k, begin + k // 2, k % 2, 1))
+        arrays.append(swap(after(group, swap_gate), last))
+        swap_gate = arrays[-1]
+    return arrays, parts
+
+
+def place(where_ref, depth, z, x):
+    z_number = lax.rem(where_ref[0] + (depth - z), depth)
+    return 2 * z_number + lax.rem(where_ref[1] + x, 2)
+
+
+def start_copies(pairs, sems):
+    copies = [pltpu.make_async_copy(a, b, sems.at[n]) for n, (a, b) in enumerate(pairs)]
+    for copy in copies:
+        copy.start()
+    return copies
+
+
+def add_low(*terms):
+    total = terms[0].astype(F32)
+    for term in terms[1:]:
+        total = total + term.astype(F32)
+    return total.astype(BF16)
+
+
+def near_first(depth):
+    order = [i % depth for i in range(1, depth + 1)]
+    split = max(depth // 2, 1)
+    return order[:split], order[split:]
+
+
+class Scatter:
+    def __init__(self, sends, first, last, depth):
+        self.arrived = [swap(send, first) for send in sends]
+        self.last = last
+        self.depth = depth
+        self.spots = [(g, k) for g, group in enumerate(near_first(depth)) for k in range(len(group))]
+        self.moving = None
+
+    def terms(self, step):
+        g, k = self.spots[step]
+        found = [self.keeps[g][k], self.arrived[g][k]]
+        if self.moving is not None:
+            found.append(self.moving)
+        return found
+
+    def hop(self, step, gate):
+        terms = self.terms(step)
+        terms[0] = after(terms[0], gate)
+        total = add_low(*terms)
+        self.moving = ring(total, self.depth)
+        return total
+
+    def finish(self, gate):
+        terms = self.terms(self.depth - 1)
+        terms[0] = after(terms[0], gate)
+        far = add_low(*[term[1] for term in terms])
+        self.near = [term[0] for term in terms]
+        self.other = swap(far, self.last)
+        return far
+
+    def result(self):
+        return add_low(*self.near, self.other)
+
+
+def turned(values, cosine, before, after):
+    wide = cosine.shape[1]
+    pieces = []
+    for begin in range(0, values.shape[1], wide):
+        piece = values[:, begin : begin + wide]
+        pieces.append(
+            piece * cosine
+            + pltpu.roll(piece, wide - HALF, 1) * before
+            + pltpu.roll(piece, HALF, 1) * after
+        )
+    return pieces
+
+
+def turned_back(piece, cosine, before, after):
+    wide = cosine.shape[1]
+    return (
+        piece * cosine
+        + pltpu.roll(piece * before, HALF, 1)
+        + pltpu.roll(piece * after, wide - HALF, 1)
+    )
+
+
+def normal(values):
+    mean = jnp.mean(values, axis=-1, keepdims=True)
+    centred = values - mean
+    variance = jnp.mean(centred * centred, axis=-1, keepdims=True)
+    inverse = lax.rsqrt(variance + EPS)
+    return centred * inverse, inverse
+
+
+def qkv_kernel(depth, parts, where_ref, own_ref, other_ref, gain_ref, shift_ref, bias_ref,
+               cosine_ref, before_ref, after_ref, *rest):
+    count = 1 + max(p[0] for p in parts)
+    arrays = rest[:count]
+    normed_ref, query_ref, key_ref, value_ref, weight, sems = rest[count:]
+    y_own = where_ref[2]
+    pairs = []
+    rows = arrays[0].shape[1]
+    wide = query_ref.shape[1]
+    thin = wide // 2
+    for n, i, half, z, x, y in parts:
+        spot = pl.ds(pl.multiple_of(place(where_ref, depth, z, x) * rows, rows), rows)
+        y_spot = lax.rem(y_own + y, 2)
+        if half == 0:
+            pairs.append((arrays[n].at[i], weight.at[y_spot, spot, pl.ds(0, wide)]))
+        else:
+            pairs.append((arrays[n].at[i, :, pl.ds(0, thin)], weight.at[y_spot, spot, pl.ds(wide, thin)]))
+    copies = start_copies(pairs, sems)
+    piece = own_ref.shape[0]
+    for ref, base in ((own_ref, 0), (other_ref, piece)):
+        for begin in range(0, piece, 256):
+            hat, _ = normal(ref[pl.ds(begin, 256), :].astype(F32))
+            normed_ref[pl.ds(base + begin, 256), :] = (hat * gain_ref[...] + shift_ref[...]).astype(BF16)
+    for copy in copies:
+        copy.wait()
+    outs = [(query_ref, 0), (query_ref, thin), (key_ref, 0), (key_ref, thin), (value_ref, 0), (value_ref, thin)]
+    for number, (ref, column) in enumerate(outs):
+        y, spot = divmod(number, 3)
+        for begin in range(0, 2 * piece, piece):
+            lines = pl.ds(begin, piece)
+            result = dot(normed_ref[lines, :], weight[y, :, pl.ds(spot * thin, thin)], NN)
+            result = result + bias_ref[:, pl.ds(number * thin, thin)]
+            if ref is value_ref:
+                ref[lines, pl.ds(column, thin)] = result.astype(BF16)
+            else:
+                pieces = turned(result, cosine_ref[lines, :], before_ref[lines, :], after_ref[lines, :])
+                for k, item in enumerate(pieces):
+                    ref[lines, pl.ds(column + k * 128, 128)] = item.astype(BF16)
+
+
+def attend_kernel(query_ref, key_ref, value_ref, out_ref, log_ref, *, block, scale):
+    length, width = key_ref.shape
+    keys = key_ref[...]
+    values = value_ref[...]
+    for number in range(2):
+        mask = half_lanes(number, (length, width))
+        key_half = keep(mask, keys)
+        value_half = keep(mask, values)
+        for start in range(0, length, block):
+            rows = pl.ds(start, block)
+            scores = dot(query_ref[rows, :], key_half, NT)
+            top = jnp.max(scores, axis=1, keepdims=True)
+            weights = jnp.exp2((scores - top) * scale)
+            total = jnp.sum(weights, axis=1, keepdims=True)
+            part = (dot(weights.astype(BF16), value_half, NN) / total).astype(BF16)
+            if number == 0:
+                out_ref[rows, :] = part
+            else:
+                out_ref[rows, :] = out_ref[rows, :] + part
+            logs = top * scale + jnp.log2(total)
+            turned_logs = jnp.transpose(jnp.broadcast_to(logs, (block, 128)))
+            log_ref[0, number : number + 1, rows] = turned_logs[0:1, :]
+
+
+def attend(queries, keys, values, head_size):
+    length, width = queries.shape
+    wide = 2 * head_size
+    pairs = width // wide
+    spec = pl.BlockSpec((length, wide), lambda i: (0, i))
+    return kernel_call(
+        functools.partial(attend_kernel, block=512, scale=LOG2E * head_size**-0.5),
+        [queries, keys, values],
+        [spec] * 3,
+        [shape_of((length, width), BF16), shape_of((pairs, 2, length), F32)],
+        grid=(pairs,),
+        out_specs=[spec, pl.BlockSpec((1, 2, length), lambda i: (i, 0, 0))],
+        flops=16 * length * length * width,
+        exps=2 * pairs * length * length,
+        room=28,
+    )
+
+
+def attend_back_kernel(
+    query_ref, key_ref, value_ref, grad_ref, log_ref, cosine_ref, before_ref, after_ref,
+    query_out, key_out, value_out, sum_out, key_sum, value_sum, query_sum, *, block, scale,
+):
+    length, width = key_ref.shape
+    keys = key_ref[...]
+    values = value_ref[...]
+    for number in range(2):
+        mask = half_lanes(number, (length, width))
+        key_half = keep(mask, keys)
+        value_half = keep(mask, values)
+        block_mask = half_lanes(number, (block, width))
+        for start in range(0, length, block):
+            rows = pl.ds(start, block)
+            query = query_ref[rows, :]
+            grad = grad_ref[rows, :]
+            scores = dot(key_half, query, NT)
+            probs = jnp.exp2(scores * (scale * LOG2E) - log_ref[0, number : number + 1, rows])
+            prob_grad = dot(value_half, grad, NT)
+            mean = jnp.sum(probs * prob_grad, axis=0, keepdims=True)
+            score_grad = (probs * (prob_grad - mean)).astype(BF16)
+            value_part = dot(probs.astype(BF16), keep(block_mask, grad), NN)
+            key_part = dot(score_grad, keep(block_mask, query), NN)
+            query_part = dot(score_grad, key_half, TN)
+            if number == 0 and start == 0:
+                value_sum[...] = value_part
+                key_sum[...] = key_part
+            else:
+                value_sum[...] += value_part
+                key_sum[...] += key_part
+            if number == 0:
+                query_sum[rows, :] = query_part
+            else:
+                query_sum[rows, :] += query_part
+    tables_here = (cosine_ref[...], before_ref[...], after_ref[...])
+    for slot, (ref, value) in enumerate(
+        (
+            (query_out, turned_back(query_sum[...] * scale, *tables_here)),
+            (key_out, turned_back(key_sum[...] * scale, *tables_here)),
+            (value_out, value_sum[...]),
+        )
+    ):
+        low = value.astype(BF16)
+        ref[...] = low
+        sum_out[slot : slot + 1, :] = jnp.sum(low.astype(F32), axis=0, keepdims=True)
+
+
+def attend_back(queries, keys, values, grads, logs, turn, head_size, begin, end):
+    length = queries.shape[0]
+    wide = 2 * head_size
+    width = (end - begin) * wide
+    spec = pl.BlockSpec((length, wide), lambda i: (0, begin + i))
+    out_spec = pl.BlockSpec((length, wide), lambda i: (0, i))
+    whole = pl.BlockSpec((length, wide), lambda i: (0, 0))
+    return kernel_call(
+        functools.partial(attend_back_kernel, block=512, scale=head_size**-0.5),
+        [queries, keys, values, grads, logs, *turn],
+        [spec] * 4 + [pl.BlockSpec((1, 2, length), lambda i: (begin + i, 0, 0))] + [whole] * 3,
+        [shape_of((length, width), BF16)] * 3 + [shape_of((8, width), F32)],
+        grid=(end - begin,),
+        out_specs=[out_spec] * 3 + [pl.BlockSpec((8, wide), lambda i: (0, i))],
+        scratch=[pltpu.VMEM((length, wide), F32)] * 3,
+        flops=40 * length * length * width,
+        exps=(end - begin) * 2 * length * length,
+        room=28,
+    )
+
+
+def load_proj(where_ref, depth, parts, arrays, weight, sems):
+    pairs = []
+    group = arrays[0].shape[1] // 2
+    thin = weight.shape[2] // 2
+    for n, i, half, z, x, y in parts:
+        if half == 0:
+            continue
+        spot = pl.ds(pl.multiple_of(place(where_ref, depth, z, x) * group, group), group)
+        y_spot = lax.rem(where_ref[2] + y, 2)
+        for k in range(2):
+            pairs.append(
+                (
+                    arrays[n].at[i, pl.ds(k * group, group), pl.ds(2 * thin - thin, thin)],
+                    weight.at[y_spot, spot, pl.ds(k * thin, thin)],
+                )
+            )
+    return start_copies(pairs, sems)
+
+
+def proj_kernel(depth, parts, where_ref, attended_ref, *rest):
+    count = 1 + max(p[0] for p in parts)
+    arrays = rest[:count]
+    keep_ref, send_ref, weight, sems = rest[count:]
+    piece, width = keep_ref.shape
+    for copy in load_proj(where_ref, depth, parts, arrays, weight, sems):
+        copy.wait()
+    half = width // 2
+    for y in range(2):
+        columns = pl.ds(y * half, half)
+        send_ref[:, columns] = dot(attended_ref[pl.ds(piece, piece), :], weight[y], NN, BF16)
+    for y in range(2):
+        columns = pl.ds(y * half, half)
+        keep_ref[:, columns] = dot(attended_ref[pl.ds(0, piece), :], weight[y], NN)
+
+
+def proj_back_kernel(depth, parts, where_ref, own_ref, other_ref, *rest):
+    count = 1 + max(p[0] for p in parts)
+    arrays = rest[:count]
+    out_ref, weight, sems = rest[count:]
+    piece, width = own_ref.shape
+    for copy in load_proj(where_ref, depth, parts, arrays, weight, sems):
+        copy.wait()
+    half = width // 2
+    for ref, begin in ((own_ref, 0), (other_ref, piece)):
+        total = dot(ref[:, pl.ds(0, half)], weight[0], NT) + dot(ref[:, pl.ds(half, half)], weight[1], NT)
+        out_ref[pl.ds(begin, piece), :] = total.astype(BF16)
+
+
+def middle_kernel(own_ref, keep_ref, other_ref, bias_ref, gain_ref, shift_ref, middle_ref, second_ref):
+    for begin in range(0, own_ref.shape[0], 128):
+        rows = pl.ds(begin, 128)
+        middle = own_ref[rows, :].astype(F32) + keep_ref[rows, :] + other_ref[rows, :].astype(F32) + bias_ref[...]
+        middle_ref[rows, :] = middle
+        hat, _ = normal(middle)
+        second_ref[rows, :] = (hat * gain_ref[...] + shift_ref[...]).astype(BF16)
+
+
+def load_up(where_ref, depth, parts, arrays, weight, sems):
+    pairs = []
+    rows, wide = arrays[0].shape[1:]
+    for n, i, half, z, x, y in parts:
+        spot = pl.ds(pl.multiple_of(place(where_ref, depth, z, x) * rows, rows), rows)
+        y_spot = lax.rem(where_ref[2] + y, 2)
+        pairs.append((arrays[n].at[i], weight.at[y_spot, spot, pl.ds(half * wide, wide)]))
+    return start_copies(pairs, sems)
+
+
+def up_kernel(depth, parts, where_ref, own_ref, other_ref, bias_ref, *rest):
+    count = 1 + max(p[0] for p in parts)
+    arrays = rest[:count]
+    second_ref, active_ref, slope_ref, weight, sems = rest[count:]
+    copies = load_up(where_ref, depth, parts, arrays, weight, sems)
+    piece = own_ref.shape[0]
+    second_ref[pl.ds(0, piece), :] = own_ref[...]
+    second_ref[pl.ds(piece, piece), :] = other_ref[...]
+    for copy in copies:
+        copy.wait()
+    wide = weight.shape[2]
+    for y in range(2):
+        for column in range(0, wide, 256):
+            for begin in range(0, 2 * piece, piece):
+                rows = pl.ds(begin, piece)
+                columns = pl.ds(y * wide + column, 256)
+                hidden = dot(second_ref[rows, :], weight[y, :, pl.ds(column, 256)], NN) + bias_ref[:, columns]
+                gate = 0.5 + 0.5 * lax.erf(hidden * 0.7071067811865476)
+                active_ref[rows, columns] = (hidden * gate).astype(BF16)
+                bell = jnp.exp2(hidden * hidden * (-0.5 * LOG2E)) * 0.3989422804014327
+                slope_ref[rows, columns] = (gate + hidden * bell).astype(BF16)
+
+
+def hidden_kernel(depth, parts, where_ref, grad_ref, slope_ref, *rest):
+    count = 1 + max(p[0] for p in parts)
+    arrays = rest[:count]
+    out_ref, sum_ref, weight, sems = rest[count:]
+    for copy in load_up(where_ref, depth, parts, arrays, weight, sems):
+        copy.wait()
+    half = grad_ref.shape[1] // 2
+    for column in range(0, out_ref.shape[1], 512):
+        columns = pl.ds(column, 512)
+        total = dot(grad_ref[:, pl.ds(0, half)], weight[0, columns, :], NT)
+        total = total + dot(grad_ref[:, pl.ds(half, half)], weight[1, columns, :], NT)
+        low = (total * slope_ref[:, columns].astype(F32)).astype(BF16)
+        out_ref[:, columns] = low
+        sum_ref[0:1, columns] = jnp.sum(low.astype(F32), axis=0, keepdims=True)
+
+
+def down_kernel(depth, parts, where_ref, active_ref, *rest):
+    count = 1 + max(p[0] for p in parts)
+    arrays = rest[:count]
+    keep_ref, send_ref, weight, sems = rest[count:]
+    piece, width = keep_ref.shape
+    for copy in load_up(where_ref, depth, parts, arrays, weight, sems):
+        copy.wait()
+    half = width // 2
+    for y in range(2):
+        columns = pl.ds(y * half, half)
+        send_ref[:, columns] = dot(active_ref[pl.ds(piece, piece), :], weight[y], NN, BF16)
+        keep_ref[:, columns] = dot(active_ref[pl.ds(0, piece), :], weight[y], NN)
+
+
+def up_back_kernel(depth, parts, where_ref, grad_ref, *rest):
+    count = 1 + max(p[0] for p in parts)
+    arrays = rest[:count]
+    keep_ref, send_ref, weight, sems = rest[count:]
+    piece, width = keep_ref.shape
+    for copy in load_up(where_ref, depth, parts, arrays, weight, sems):
+        copy.wait()
+    wide = weight.shape[2]
+    for ref, begin in ((send_ref, piece), (keep_ref, 0)):
+        rows = pl.ds(begin, piece)
+        for column in range(0, width, 512):
+            columns = pl.ds(column, 512)
+            total = dot(grad_ref[rows, pl.ds(0, wide)], weight[0, columns, :], NT)
+            total = total + dot(grad_ref[rows, pl.ds(wide, wide)], weight[1, columns, :], NT)
+            ref[:, columns] = total.astype(ref.dtype)
+
+
+def middle_back_kernel(keep_ref, other_ref, middle_ref, grad_ref, gain_ref, middle_out, branch_out, sum_out):
+    totals = [jnp.zeros((1, keep_ref.shape[1]), F32) for _ in range(4)]
+    for begin in range(0, keep_ref.shape[0], 128):
+        rows = pl.ds(begin, 128)
+        grad = keep_ref[rows, :] + other_ref[rows, :].astype(F32)
+        hat, inverse = normal(middle_ref[rows, :])
+        scaled = grad * gain_ref[...]
+        first = jnp.mean(scaled, axis=-1, keepdims=True)
+        second = jnp.mean(scaled * hat, axis=-1, keepdims=True)
+        outer = grad_ref[rows, :].astype(F32)
+        result = outer + inverse * (scaled - first - hat * second)
+        middle_out[rows, :] = result
+        low = result.astype(BF16)
+        branch_out[rows, :] = low
+        for n, value in enumerate((grad * hat, grad, low.astype(F32), outer)):
+            totals[n] = totals[n] + jnp.sum(value, axis=0, keepdims=True)
+    for n in range(4):
+        sum_out[n : n + 1, :] = totals[n]
+
+
+def tokens_back_kernel(keep_ref, other_ref, own_ref, grad_ref, gain_ref, out_ref, sum_out):
+    totals = [jnp.zeros((1, keep_ref.shape[1]), F32) for _ in range(2)]
+    for begin in range(0, keep_ref.shape[0], 128):
+        rows = pl.ds(begin, 128)
+        grad = keep_ref[rows, :] + other_ref[rows, :].astype(F32)
+        hat, inverse = normal(own_ref[rows, :].astype(F32))
+        scaled = grad * gain_ref[...]
+        first = jnp.mean(scaled, axis=-1, keepdims=True)
+        second = jnp.mean(scaled * hat, axis=-1, keepdims=True)
+        result = grad_ref[rows, :] + inverse * (scaled - first - hat * second)
+        out_ref[rows, :] = result.astype(BF16)
+        for n, value in enumerate((grad * hat, grad)):
+            totals[n] = totals[n] + jnp.sum(value, axis=0, keepdims=True)
+    for n in range(2):
+        sum_out[n : n + 1, :] = totals[n]
+
+
+def load_columns(where_ref, depth, source, scratch, rows, sems):
+    pairs = []
+    for x in range(2):
+        for z in range(depth):
+            spot = pl.ds(pl.multiple_of(place(where_ref, depth, z, x) * rows, rows), rows)
+            pairs.append((source.at[:, spot], scratch.at[:, pl.ds((x * depth + z) * rows, rows)]))
+    return start_copies(pairs, sems)
+
+
+def rows_grad_kernel(depth, rows, sent, where_ref, act_ref, grad_ref, *rest):
+    outs, scratch, sems = rest[:-2], rest[-2], rest[-1]
+    pairs = []
+    order = [z for group in near_first(depth) for z in group]
+    for n, z in enumerate(order):
+        spot = pl.ds(pl.multiple_of(place(where_ref, depth, z, sent) * rows, rows), rows)
+        pairs.append((act_ref.at[:, spot], scratch.at[:, pl.ds(n * rows, rows)]))
+    for copy in start_copies(pairs, sems):
+        copy.wait()
+    part = grad_ref.shape[1] // 2
+    begin = 0
+    for ref in outs:
+        size = ref.shape[0]
+        for y_near in range(2):
+            y = lax.rem(where_ref[2] + y_near, 2)
+            columns = pl.ds(pl.multiple_of(y * part, 128), part)
+            result = dot(scratch[:, pl.ds(begin * rows, size * rows)], grad_ref[:, columns], TN, BF16)
+            for k in range(size):
+                ref[k, y_near] = result[k * rows : (k + 1) * rows]
+        begin += size
+
+
+def rows_grad(where, act, grad, depth, rows, sent):
+    length, total = act.shape
+    part = grad.shape[1] // 2
+    return kernel_call(
+        functools.partial(rows_grad_kernel, depth, rows, sent),
+        [where, act, grad],
+        [SCALARS, ANYWHERE, WHOLE],
+        [shape_of((len(group), 2, rows, part), BF16) for group in near_first(depth)],
+        scratch=[pltpu.VMEM((length, depth * rows), BF16), pltpu.SemaphoreType.DMA((depth,))],
+        flops=length * total * grad.shape[1],
+    )
+
+
+def columns_grad_kernel(depth, rows, sent, where_ref, act_ref, grad_ref, *rest):
+    outs, scratch, sems = rest[:-2], rest[-2], rest[-1]
+    pairs = []
+    order = [z for group in near_first(depth) for z in group]
+    for n, z in enumerate(order):
+        for x in range(2):
+            spot = pl.ds(pl.multiple_of(place(where_ref, depth, z, x) * rows, rows), rows)
+            pairs.append((act_ref.at[:, spot], scratch.at[:, pl.ds((2 * n + x) * rows, rows)]))
+    for copy in start_copies(pairs, sems):
+        copy.wait()
+    part = grad_ref.shape[1] // 2
+    begin = 0
+    half = part // 2
+    y = lax.rem(where_ref[2] + sent, 2)
+    for ref in outs:
+        size = ref.shape[0]
+        for column in range(0, part, half):
+            columns = pl.ds(pl.multiple_of(y * part + column, 128), half)
+            result = dot(scratch[:, pl.ds(begin * rows, 2 * size * rows)], grad_ref[:, columns], TN, BF16)
+            for k in range(size):
+                for x in range(2):
+                    line = (2 * k + x) * rows
+                    ref[k, x, :, pl.ds(column, half)] = result[line : line + rows]
+        begin += 2 * size
+
+
+def columns_grad(where, act, grad, depth, rows, sent):
+    length, total = act.shape
+    part = grad.shape[1] // 2
+    return kernel_call(
+        functools.partial(columns_grad_kernel, depth, rows, sent),
+        [where, act, grad],
+        [SCALARS, ANYWHERE, WHOLE],
+        [shape_of((len(group), 2, rows, part), BF16) for group in near_first(depth)],
+        scratch=[pltpu.VMEM((length, total), BF16), pltpu.SemaphoreType.DMA((2 * depth,))],
+        flops=length * total * grad.shape[1],
+    )
+
+
+def own_half(core, mine, other):
+    first = core == 0
+    return jnp.where(first, mine, other), jnp.where(first, other, mine)
+
+
+def split_kernel(hidden_block, core_ref, qkv_ref, up_ref, qkv_mine, qkv_other, up_mine, up_other):
+    core = core_ref[0]
+    rows = qkv_ref.shape[0]
+    low = lax.broadcasted_iota(jnp.int32, (rows, 128), 1) < 64
+    for tile in range(qkv_ref.shape[1] // 256):
+        one = qkv_ref[:, pl.ds(tile * 256, 128)].astype(F32)
+        two = qkv_ref[:, pl.ds(tile * 256 + 128, 128)].astype(F32)
+        even = jnp.where(low, one, pltpu.roll(two, 64, 1)).astype(BF16)
+        odd = jnp.where(low, pltpu.roll(one, 64, 1), two).astype(BF16)
+        mine, other = own_half(core, even, odd)
+        qkv_mine[:, pl.ds(tile * 128, 128)] = mine
+        qkv_other[:, pl.ds(tile * 128, 128)] = other
+    for tile in range(up_ref.shape[1] // (2 * hidden_block)):
+        even = up_ref[:, pl.ds(tile * 2 * hidden_block, hidden_block)]
+        odd = up_ref[:, pl.ds((tile * 2 + 1) * hidden_block, hidden_block)]
+        mine, other = own_half(core, even, odd)
+        up_mine[:, pl.ds(tile * hidden_block, hidden_block)] = mine
+        up_other[:, pl.ds(tile * hidden_block, hidden_block)] = other
+
+
+def pack_kernel(core_ref, mine_ref, other_ref, *rest):
+    extra, out_ref = rest[:-1], rest[-1]
+    rows, columns = mine_ref.shape
+    half = out_ref.shape[2]
+    for ref, number in ((mine_ref, core_ref[0]), (other_ref, 1 - core_ref[0])):
+        lines = pl.ds(pl.multiple_of(number * rows, rows), rows)
+        out_ref[0, lines, :] = ref[:, pl.ds(0, half)]
+        out_ref[1, lines, pl.ds(0, columns - half)] = ref[:, pl.ds(half, columns - half)]
+    for ref in extra:
+        thin = ref.shape[1] // 2
+        for k in range(2):
+            out_ref[1, pl.ds(k * rows, rows), pl.ds(half - thin, thin)] = ref[:, pl.ds(k * thin, thin)]
+
+
+def join_heads_kernel(core_ref, mine_ref, other_ref, out_ref):
+    rows = mine_ref.shape[0]
+    low = lax.broadcasted_iota(jnp.int32, (rows, 128), 1) < 64
+    for tile in range(mine_ref.shape[1] // 128):
+        columns = pl.ds(tile * 128, 128)
+        even, odd = own_half(core_ref[0], mine_ref[:, columns].astype(F32), other_ref[:, columns].astype(F32))
+        out_ref[:, pl.ds(tile * 256, 128)] = jnp.where(low, even, pltpu.roll(odd, 64, 1))
+        out_ref[:, pl.ds(tile * 256 + 128, 128)] = jnp.where(low, pltpu.roll(even, 64, 1), odd)
+
+
+def join_blocks_kernel(block, core_ref, mine_ref, other_ref, out_ref):
+    for tile in range(mine_ref.shape[1] // block):
+        columns = pl.ds(tile * block, block)
+        even, odd = own_half(core_ref[0], mine_ref[:, columns].astype(F32), other_ref[:, columns].astype(F32))
+        out_ref[:, pl.ds(2 * tile * block, block)] = even
+        out_ref[:, pl.ds((2 * tile + 1) * block, block)] = odd
+
+
+def proj_grad_kernel(depth, where_ref, attended_ref, own_ref, other_ref, out_ref, scratch):
+    piece = own_ref.shape[0]
+    group = out_ref.shape[3] // 2
+    thin = out_ref.shape[4]
+    for y_near in range(2):
+        y = lax.rem(where_ref[2] + y_near, 2)
+        columns = pl.ds(pl.multiple_of(y * 2 * thin, 128), 2 * thin)
+        result = dot(attended_ref[pl.ds(0, piece), :], own_ref[:, columns], TN)
+        scratch[...] = result + dot(attended_ref[pl.ds(piece, piece), :], other_ref[:, columns], TN)
+        for x in range(2):
+            for z in range(depth):
+                spot = pl.ds(pl.multiple_of(place(where_ref, depth, z, x) * group, group), group)
+                block = scratch[spot, :].astype(BF16)
+                for k in range(2):
+                    out_ref[x, y_near, z, pl.ds(k * group, group), :] = block[:, k * thin : (k + 1) * thin]
+
+
+def mixed_grad_kernel(depth, sent, where_ref, act_ref, *rest):
+    count = len(rest) - 7
+    pieces, (proj_ref, one_ref, two_ref, scratch, mixed, sems, mixed_sems) = rest[:count], rest[count:]
+    rows = one_ref.shape[2]
+    copies = load_columns(where_ref, depth, act_ref, scratch, rows, sems)
+    size = pieces[0].shape[1]
+    wide = size * count // 3
+    thin = wide // 2
+    copies += start_copies(
+        [(ref, mixed.at[:, pl.ds(n * size, size)]) for n, ref in enumerate(pieces)],
+        mixed_sems,
+    )
+    for copy in copies:
+        copy.wait()
+    part = wide + thin
+    half = depth * rows
+    y = lax.rem(where_ref[2] + sent, 2)
+    columns = pl.ds(pl.multiple_of(y * part, 128), wide)
+    for x in range(2):
+        result = dot(scratch[:, pl.ds(x * half, half)], mixed[:, columns], TN, BF16)
+        for z in range(depth):
+            one_ref[x, z] = result[z * rows : (z + 1) * rows]
+    for y_near in range(2):
+        y = lax.rem(where_ref[2] + y_near, 2)
+        columns = pl.ds(pl.multiple_of(y * part + wide, 128), thin)
+        result = dot(scratch[:, pl.ds(sent * half, half)], mixed[:, columns], TN, BF16)
+        for z in range(depth):
+            two_ref[y_near, z, :, pl.ds(0, thin)] = result[z * rows : (z + 1) * rows]
+            two_ref[y_near, z, :, pl.ds(thin, thin)] = proj_ref[sent, y_near, z]
+
+
+def mixed_back_kernel(depth, parts, count, where_ref, *rest):
+    pieces, rest = rest[:count], rest[count:]
+    arrays = rest[: 1 + max(p[0] for p in parts)]
+    keep_ref, send_ref, weight, sems = rest[len(arrays) :]
+    pairs = []
+    rows = arrays[0].shape[1]
+    size = pieces[0].shape[1]
+    wide = size * count // 3
+    thin = wide // 2
+    for n, i, half, z, x, y in parts:
+        spot = pl.ds(pl.multiple_of(place(where_ref, depth, z, x) * rows, rows), rows)
+        y_spot = lax.rem(where_ref[2] + y, 2)
+        if half == 0:
+            pairs.append((arrays[n].at[i], weight.at[y_spot, spot, pl.ds(0, wide)]))
+        else:
+            pairs.append((arrays[n].at[i, :, pl.ds(0, thin)], weight.at[y_spot, spot, pl.ds(wide, thin)]))
+    for copy in start_copies(pairs, sems):
+        copy.wait()
+    piece, width = keep_ref.shape
+    for ref, begin in ((send_ref, piece), (keep_ref, 0)):
+        lines = pl.ds(begin, piece)
+        for column in range(0, width, 512):
+            columns = pl.ds(column, 512)
+            total = None
+            for n, item in enumerate(pieces):
+                y, spot = divmod(n * size, wide + thin)
+                term = dot(item[lines, :], weight[y, columns, pl.ds(spot, size)], NT)
+                total = term if total is None else total + term
+            ref[:, columns] = total.astype(ref.dtype)
+
+
+HALF = 10
+
+
+def turn_tables(places, head_size, wide):
+    section = 2 * (head_size // 3 // 2)
+    half_size = section // 2
+    lane = jnp.arange(wide) % head_size
+    number = lane // section
+    spot = lane % section
+    frequency = 1.0 / 10000.0 ** ((spot % half_size).astype(F32) / half_size)
+    place_of = jnp.where(
+        number[None, :] == 0,
+        places[:, 0:1],
+        jnp.where(number[None, :] == 1, places[:, 1:2], places[:, 2:3]),
+    )
+    angles = place_of.astype(F32) * frequency[None, :]
+    live = (number < 3)[None, :]
+    cosine = jnp.where(live, jnp.cos(angles), 1.0)
+    sine = jnp.where(live, jnp.sin(angles), 0.0)
+    low = (spot < half_size)[None, :]
+    return cosine, jnp.where(low, -sine, 0.0), jnp.where(low, 0.0, sine)
+
+
+def ordered(index, first, second, axis=0):
+    low = jnp.where(index == 0, first, second)
+    high = jnp.where(index == 0, second, first)
+    return jnp.stack([low, high], axis=axis)
+
+
+def taken(values, index, axis):
+    return lax.dynamic_index_in_dim(values, index, axis, keepdims=False)
+
+
+def fast_shards(
+    tokens,
+    frame_index,
+    row_index,
+    column_index,
+    norm1_gain,
+    norm1_bias,
+    qkv_weight,
+    qkv_bias,
+    proj_weight,
+    proj_bias,
+    norm2_gain,
+    norm2_bias,
+    up_weight,
+    up_bias,
+    down_weight,
+    down_bias,
+    cotangent,
+):
+    core = lax.axis_index("core")
+    depth = lax.axis_size("z")
+    where = jnp.stack([lax.axis_index("z"), lax.axis_index("x"), lax.axis_index("y")]).astype(jnp.int32)
+    everyone = ("z", "x", "core", "y")
+    count = 8 * depth
+    piece, width = tokens.shape
+    length = 2 * piece
+    head_size = width // HEADS
+    local = width // 2
+    hidden_block = down_weight.shape[0]
+
+    cores = jnp.stack([core]).astype(jnp.int32)
+    up_rows = width // (2 * depth)
+    shard_rows = qkv_weight.shape[0]
+    part_qkv = 3 * local // 2
+    part_up = up_weight.shape[1] // 2
+    block_kind = shape_of((2, up_rows, local), BF16)
+
+    qkv_mine, qkv_other, up_mine, up_other = kernel_call(
+        functools.partial(split_kernel, hidden_block),
+        [cores, qkv_weight, up_weight],
+        [SCALARS, WHOLE, WHOLE],
+        [shape_of((shard_rows, part_qkv), BF16)] * 2 + [shape_of((shard_rows, part_up), BF16)] * 2,
+    )
+    (first_block,) = kernel_call(
+        pack_kernel,
+        [cores, qkv_mine, swap(qkv_other, "core"), proj_weight],
+        [SCALARS] + [WHOLE] * 3,
+        [block_kind],
+    )
+    (up_block,) = kernel_call(
+        pack_kernel, [cores, up_mine, swap(up_other, "core")], [SCALARS] + [WHOLE] * 2, [block_kind]
+    )
+    first_arrays, first_parts, hop_gate, swap_gate = gather_first(first_block, depth)
+    tokens_own = lax.ppermute(tokens, ("core", "y"), DIAGONAL)
+    grad_own = lax.ppermute(after(cotangent, tokens_own), ("core", "y"), DIAGONAL)
+    up_arrays, up_parts, hop_gate, swap_gate = gather_middle(up_block, depth, hop_gate, swap_gate)
+    down_arrays, down_parts = gather_single(down_weight, depth, "y", "x", hop_gate, swap_gate[1])
+
+    small = jnp.concatenate(
+        [norm1_gain, norm1_bias, norm2_gain, norm2_bias, proj_bias, down_bias, qkv_bias, up_bias]
+    )
+    small = after(small, first_block)
+    used = small.shape[0]
+    small = jnp.broadcast_to(
+        jnp.concatenate([small.astype(F32), jnp.zeros((512 - used,), F32)]), (count, 512)
+    )
+    small = lax.all_to_all(small, everyone, split_axis=0, concat_axis=0, tiled=True)
+    each = norm1_gain.shape[0]
+    gain_one, shift_one, gain_two, shift_two, bias_proj, bias_down = [
+        small[:, i * each : (i + 1) * each].reshape(1, width) for i in range(6)
+    ]
+    spot = 6 * each
+    bias_qkv = small[:, spot : spot + qkv_bias.shape[0]].reshape(-1, 2, head_size)
+    spot += qkv_bias.shape[0]
+    bias_up = small[:, spot : spot + up_bias.shape[0]].reshape(-1, 2, hidden_block)
+    bias_qkv = taken(bias_qkv, core, 1).reshape(1, -1)
+    bias_up = taken(bias_up, core, 1).reshape(1, -1)
+
+    places = jnp.stack([frame_index, row_index, column_index], axis=0)
+    places = lax.ppermute(places, ("core", "y"), DIAGONAL)
+    places = jnp.concatenate([places, swap(places, "core")], axis=1).T
+    tokens_other = swap(tokens_own, "core")
+    grad_full = jnp.concatenate([grad_own, swap(grad_own, "core")])
+    turn = turn_tables(places, head_size, 2 * head_size)
+
+    part_count = len(first_parts)
+    dma = pltpu.SemaphoreType.DMA
+    normed, queries, keys, values = kernel_call(
+        functools.partial(qkv_kernel, depth, first_parts),
+        [where, tokens_own, tokens_other, gain_one, shift_one, bias_qkv, *turn, *first_arrays],
+        [SCALARS] + [WHOLE] * 8 + [ANYWHERE] * len(first_arrays),
+        [shape_of((length, width), BF16)] + [shape_of((length, local), BF16)] * 3,
+        scratch=[pltpu.VMEM((2, width, 3 * local // 2), BF16), dma((part_count,))],
+        flops=2 * length * width * 3 * local,
+    )
+    attended, logs = attend(queries, keys, values, head_size)
+    proj_scratch = [pltpu.VMEM((2, local, width // 2), BF16), dma((part_count,))]
+    partial = [shape_of((piece, width), F32), shape_of((piece, width), BF16)]
+    kept, sent = kernel_call(
+        functools.partial(proj_kernel, depth, first_parts),
+        [where, attended, *first_arrays],
+        [SCALARS, WHOLE] + [ANYWHERE] * len(first_arrays),
+        partial,
+        scratch=proj_scratch,
+        flops=2 * length * width * local,
+    )
+    middle, second_own = kernel_call(
+        middle_kernel,
+        [tokens_own, kept, swap(sent, "core"), bias_proj, gain_two, shift_two],
+        [WHOLE] * 6,
+        partial,
+    )
+    hidden_size = bias_up.shape[1]
+    up_scratch = [pltpu.VMEM((2, width, hidden_size // 2), BF16), dma((len(up_parts),))]
+    second, active, slope = kernel_call(
+        functools.partial(up_kernel, depth, up_parts),
+        [where, second_own, swap(second_own, "core"), bias_up, *up_arrays],
+        [SCALARS] + [WHOLE] * 3 + [ANYWHERE] * len(up_arrays),
+        [shape_of((length, width), BF16)] + [shape_of((length, hidden_size), BF16)] * 2,
+        scratch=up_scratch,
+        flops=2 * length * width * hidden_size,
+        exps=length * hidden_size,
+    )
+    sends = rows_grad(where, active, grad_full, depth, hidden_block, 1)
+    down_sum = Scatter(sends, "x", "y", depth)
+    down_scratch = [pltpu.VMEM((2, hidden_size, width // 2), BF16), dma((len(down_parts),))]
+    hidden_grad, up_sums = kernel_call(
+        functools.partial(hidden_kernel, depth, down_parts),
+        [where, grad_full, after(slope, *sends), *down_arrays],
+        [SCALARS] + [WHOLE] * 2 + [ANYWHERE] * len(down_arrays),
+        [shape_of((length, hidden_size), BF16), shape_of((8, hidden_size), F32)],
+        scratch=down_scratch,
+        flops=2 * length * width * hidden_size,
+    )
+    sends = columns_grad(where, second, hidden_grad, depth, up_rows, 1)
+    up_sum = Scatter(sends, "y", "x", depth)
+    down_sum.keeps = rows_grad(where, after(active, *sends), grad_full, depth, hidden_block, 0)
+    kept, sent = kernel_call(
+        functools.partial(up_back_kernel, depth, up_parts),
+        [where, after(hidden_grad, *down_sum.keeps), *up_arrays],
+        [SCALARS, WHOLE] + [ANYWHERE] * len(up_arrays),
+        partial,
+        scratch=up_scratch,
+        flops=2 * length * width * hidden_size,
+    )
+    up_sum.keeps = columns_grad(where, after(second, sent), hidden_grad, depth, up_rows, 0)
+    gate = down_sum.hop(0, up_sum.keeps[0])
+    middle_grad, branch_own, middle_sums = kernel_call(
+        middle_back_kernel,
+        [after(kept, gate), swap(sent, "core"), middle, grad_own, gain_two],
+        [WHOLE] * 5,
+        partial + [shape_of((8, width), F32)],
+    )
+    branch_other = swap(branch_own, "core")
+    (attended_grad,) = kernel_call(
+        functools.partial(proj_back_kernel, depth, first_parts),
+        [where, branch_own, branch_other, *first_arrays],
+        [SCALARS] + [WHOLE] * 2 + [ANYWHERE] * len(first_arrays),
+        [shape_of((length, local), BF16)],
+        scratch=proj_scratch,
+        flops=2 * length * width * local,
+    )
+    (proj_blocks,) = kernel_call(
+        functools.partial(proj_grad_kernel, depth),
+        [where, attended, after(branch_own, attended_grad), branch_other],
+        [SCALARS] + [WHOLE] * 3,
+        [shape_of((2, 2, depth, up_rows, width // 4), BF16)],
+        scratch=[pltpu.VMEM((local, width // 2), F32)],
+        flops=2 * length * width * local,
+    )
+    pairs = local // (2 * head_size)
+    gate = down_sum.hop(1, proj_blocks)
+    first_grads = attend_back(
+        queries, keys, values, after(attended_grad, gate), logs, turn, head_size, 0, pairs // 2
+    )
+    gate = (down_sum.hop(2, first_grads[0]), up_sum.hop(0, first_grads[0]))
+    second_grads = attend_back(
+        queries, keys, values, after(attended_grad, *gate), logs, turn, head_size, pairs // 2, pairs
+    )
+    mixed_pieces = [group[n] for n in range(3) for group in (first_grads, second_grads)]
+    mixed_sums = jnp.concatenate([first_grads[3][:3], second_grads[3][:3]], axis=1)
+
+    def mixed_weight_grad(sent_number, gate):
+        block = (2, depth, up_rows, local)
+        return kernel_call(
+            functools.partial(mixed_grad_kernel, depth, sent_number),
+            [where, after(normed, gate), *mixed_pieces, proj_blocks],
+            [SCALARS] + [ANYWHERE] * (1 + len(mixed_pieces)) + [WHOLE],
+            [shape_of(block, BF16)] * 2,
+            scratch=[
+                pltpu.VMEM((length, width), BF16),
+                pltpu.VMEM((length, 3 * local), BF16),
+                dma((2 * depth,)),
+                dma((len(mixed_pieces),)),
+            ],
+            flops=length * width * 3 * local,
+        )
+
+    one_send, two_send = mixed_weight_grad(1, second_grads[0])
+    one_near = swap(one_send, "y")
+    two_near = swap(two_send, "x")
+    gate = (up_sum.hop(1, two_send), down_sum.finish(two_send))
+    kept, sent = kernel_call(
+        functools.partial(mixed_back_kernel, depth, first_parts, len(mixed_pieces)),
+        [where, after(mixed_pieces[0], *gate), *mixed_pieces[1:], *first_arrays],
+        [SCALARS] + [WHOLE] * len(mixed_pieces) + [ANYWHERE] * len(first_arrays),
+        partial,
+        scratch=[pltpu.VMEM((2, width, 3 * local // 2), BF16), dma((part_count,))],
+        flops=2 * length * width * 3 * local,
+    )
+    sent_other = swap(sent, "core")
+    one_keep, two_keep = mixed_weight_grad(0, sent)
+    gate = up_sum.hop(2, two_keep)
+    tokens_grad, first_sums = kernel_call(
+        tokens_back_kernel,
+        [after(kept, gate), sent_other, tokens_own, middle_grad, gain_one],
+        [WHOLE] * 5,
+        [shape_of((piece, width), BF16), shape_of((8, width), F32)],
+    )
+    one_far = add_low(after(one_keep[1], tokens_grad), one_near[1])
+    two_far = add_low(after(two_keep[1], tokens_grad), two_near[1])
+    one_last = swap(one_far, "x")
+    two_last = swap(two_far, "y")
+    kept, sent = kernel_call(
+        functools.partial(down_kernel, depth, down_parts),
+        [where, after(active, one_far, two_far), *down_arrays],
+        [SCALARS, WHOLE] + [ANYWHERE] * len(down_arrays),
+        partial,
+        scratch=down_scratch,
+        flops=2 * length * width * hidden_size,
+    )
+    up_sum.finish(sent)
+    block_out = (middle + (kept + swap(sent, "core").astype(F32)) + bias_down).astype(BF16)
+    block_out = lax.ppermute(block_out, ("core", "y"), DIAGONAL)
+    tokens_grad = lax.ppermute(tokens_grad, ("core", "y"), DIAGONAL)
+    one = add_low(one_keep[0], one_near[0], one_last)
+    two = add_low(two_keep[0], two_near[0], two_last)
+    both = jnp.stack([one, two], axis=1)
+    moving = both[1 % depth]
+    for step in range(1, depth):
+        moving = add_low(both[(step + 1) % depth], ring(moving, depth))
+    grad_first = moving
+    grad_down = down_sum.result()
+    grad_up = up_sum.result()
+
+    def spread(vector, group):
+        parts = vector.reshape(-1, 1, group)
+        pair = jnp.arange(2).reshape(1, 2, 1) == core
+        return jnp.where(pair, parts, 0.0).reshape(-1)
+
+    vectors = [
+        first_sums[0],
+        first_sums[1],
+        middle_sums[0],
+        middle_sums[1],
+        middle_sums[2],
+        middle_sums[3],
+        spread(mixed_sums[:3].reshape(-1), head_size),
+        spread(up_sums[0], hidden_block),
+    ]
+    packed = jnp.concatenate([v.reshape(count, -1) for v in vectors], axis=1)
+    packed = jnp.pad(packed, ((0, 0), (0, 512 - packed.shape[1])))
+    packed = lax.all_to_all(packed, everyone, split_axis=0, concat_axis=0, tiled=True)
+    packed = jnp.sum(packed, axis=0)
+    pieces = []
+    spot = 0
+    for v in vectors:
+        size = v.shape[0] // count
+        pieces.append(packed[spot : spot + size])
+        spot += size
+
+    def joined(body, block):
+        rows = block.shape[0] // 2
+        pair = block.reshape(2, rows, -1)
+        (whole,) = kernel_call(
+            body,
+            [cores, taken(pair, core, 0), swap(taken(pair, 1 - core, 0), "core")],
+            [SCALARS, WHOLE, WHOLE],
+            [shape_of((rows, 2 * block.shape[1]), F32)],
+        )
+        return whole
+
+    grad_proj = grad_first[1][:, part_qkv - local :].astype(F32)
+    group = grad_proj.shape[0] // 2
+    grad_proj = jnp.concatenate([grad_proj[:group], grad_proj[group:]], axis=1)
+    grad_qkv = jnp.concatenate([grad_first[0], grad_first[1][:, : part_qkv - local]], axis=1)
+    grad_qkv = joined(join_heads_kernel, grad_qkv)
+    grad_up = joined(functools.partial(join_blocks_kernel, hidden_block), grad_up)
+    return (
+        block_out,
+        tokens_grad,
+        pieces[0],
+        pieces[1],
+        grad_qkv,
+        pieces[6],
+        grad_proj,
+        pieces[4],
+        pieces[2],
+        pieces[3],
+        grad_up,
+        pieces[7],
+        grad_down.astype(F32),
+        pieces[5],
+    )
+
+
 def solution(mesh):
-    placed = (
-        P(("dp", "ctx"), None),
-        P(("dp", "ctx")),
-        P(("dp", "ctx")),
-        P(("dp", "ctx")),
-        P(("dp", "ctx")),
-        P(("dp", "ctx")),
-        P("dp", "ctx"),
-        P(("dp", "ctx")),
-        P("dp", "ctx"),
-        P(("dp", "ctx")),
-        P(("dp", "ctx")),
-        P(("dp", "ctx")),
-        P("dp", "ctx"),
-        P(("dp", "ctx")),
-        P("dp", "ctx"),
-        P(("dp", "ctx")),
-        P(("dp", "ctx"), None),
-    )
+    ctx_count = mesh.shape["ctx"]
+    dp_count = mesh.shape["dp"]
+    if ctx_count == 2 and dp_count % 4 == 0:
+        mesh = Mesh(
+            mesh.devices.reshape(dp_count // 4, 2, 2, 2), ("z", "x", "core", "y")
+        )
+        dp = ("z", "x", "core")
+        ctx = "y"
+        every = P(dp + (ctx,))
+        body = fast_shards
+    else:
+        dp = "dp"
+        ctx = "ctx"
+        every = P((dp, ctx))
+        body = shards
+    rows = P(every[0], None)
+    matrix = P(dp, ctx)
     return jax.shard_map(
-        shards,
+        body,
         mesh=mesh,
-        in_specs=placed,
+        in_specs=(
+            rows,
+            every,
+            every,
+            every,
+            every,
+            every,
+            matrix,
+            every,
+            matrix,
+            every,
+            every,
+            every,
+            matrix,
+            every,
+            matrix,
+            every,
+            rows,
+        ),
         out_specs=(
-            P(("dp", "ctx"), None),
-            P(("dp", "ctx"), None),
-            P(("dp", "ctx")),
-            P(("dp", "ctx")),
-            P("dp", "ctx"),
-            P(("dp", "ctx")),
-            P("dp", "ctx"),
-            P(("dp", "ctx")),
-            P(("dp", "ctx")),
-            P(("dp", "ctx")),
-            P("dp", "ctx"),
-            P(("dp", "ctx")),
-            P("dp", "ctx"),
-            P(("dp", "ctx")),
+            rows,
+            rows,
+            every,
+            every,
+            matrix,
+            every,
+            matrix,
+            every,
+            every,
+            every,
+            matrix,
+            every,
+            matrix,
+            every,
         ),
         check_vma=False,
     )

time: 1110 us -> 448 us (0.40)
  matrix products: 303 us -> 0 us
  blocking collectives: 194 us -> 0 us
  waiting for transfers between devices: 270 us -> 106 us
  Pallas kernels: 0 us -> 133 us
  local copies, waits for them, and re-layouts: 170 us -> 70.4 us
  starting transfers between devices: 1.29 us -> 82.5 us
  loops' own time: 62.5 us -> 0 us
  other arithmetic: 76.8 us -> 46.7 us
  between operations: 21.5 us -> 2.25 us
    dot_general x124 -> x0, matrix products: 303 us -> none  [the longest x16 35.5 us: head_forward(): jnp.einsum('sqk,skd->sqd', weights_low, value_head, preferred_element_typ...]
    reduce_scatter x10 -> x0, waiting for transfers between devices: 229 us -> none  [the longest x1 78 us: shards(): lax.psum_scatter(grad_qkv.astype(jnp.bfloat16), 'dp', scatter_dimension=0...]
    pallas_call x0 -> x26, Pallas kernels: none -> 133 us  [kernel_call(): pl.pallas_call(body, in_specs=in_specs, out_specs=out_specs, out_shape=ou...]
    unnamed x4 -> x0, blocking collectives: 124 us -> none
    ppermute x0 -> x61, waiting for transfers between devices: none -> 101 us  [the longest x18 54.5 us: ring(): lax.ppermute(values, 'z', [(i, (i + 1) % depth) for i in range(depth)])]
    concatenate x8 -> x3, local copies, waits for them, and re-layouts: 94.4 us -> 6.83 us  [the longest x1 5.43 us: fast_shards(): jnp.concatenate([norm1_gain, norm1_bias, norm2_gain, norm2_bias, proj_bia...]
    all_gather x6 -> x0, blocking collectives: 70.1 us -> none  [the longest x1 29 us: gather_all(): lax.all_gather(partial_value[10], 'dp', axis=0, tiled=True)]
    ppermute x0 -> x61, starting transfers between devices: none -> 66.4 us  [the longest x38 37.1 us: swap(): return lax.ppermute(values, axis, SWAP)]
  transfers between devices with their start and end apart: 16 -> 63, of which waited for: 7 -> 18; matrix products, arithmetic and copies ran while one was open for 41% -> 17% of each run, Pallas kernels for 0% -> 29%
where the time goes in v1:
time: 448 us; the launch traced here: 441 us
  Pallas kernels  133 us (30%)
  waiting for transfers between devices  106 us (24%)
  starting transfers between devices  82.5 us (18%)
  local copies, waits for them, and re-layouts  70.4 us (16%)
  other arithmetic  46.7 us (10%)
    pallas_call x26, Pallas kernels, kernel_call(): pl.pallas_call(body, in_specs=in_specs, out_specs=out_specs, out_shape=ou...  133 us
    ppermute x18, waiting for transfers between devices, ring(): lax.ppermute(values, 'z', [(i, (i + 1) % depth) for i in range(depth)])  54.5 us
    unnamed x206, local copies, waits for them, and re-layouts  44.2 us
    ppermute x38, waiting for transfers between devices, swap(): return lax.ppermute(values, axis, SWAP)  40.2 us
    ppermute x38, starting transfers between devices, swap(): return lax.ppermute(values, axis, SWAP)  37.1 us
    convert_element_type x14, other arithmetic, add_low(): return total.astype(BF16)  21.7 us
    all_to_all x1, starting transfers between devices, fast_shards(): lax.all_to_all(small, everyone, split_axis=0, concat_axis=0, tiled=True)  10.7 us
  transfers between devices with their start and end apart: 63, of which 18 were waited for; matrix products, arithmetic and copies ran while one was open for 17% of the time, Pallas kernels for 29%

profile of v1, /device:TPU:1, one launch (start us, length us, event | category | flops | bytes accessed | tf_op | source)
XLA Modules:
  0.0 440.7 jit_solution(305768250560386324)
XLA Ops:
  12.2 5.4 %concatenate.54 = bf16[416]{0:T(512)(128)(2,1)S(1)} concatenate(bf16[32]{0:T(256)(128)(2,1)} %param.21, bf16[32]{0:T(256)(128)(2,1)} %param.22, bf16[32]{0:T(256)(128)(2,1)} %param.27, bf16[32]{0:T(256)(128)(2,1)} %param.28, bf16[32]{0:T(256)(128)(2,1)} %param.26, bf16[32]{0:T(256)(128)(2,1)} %param.32, bf16[96]{0:T(256)(128)(2,1)} %param.24, bf16[128]{0:T(256)(128)(2,1)} %param.30), dimensions={0} | concatenate | bytes 1664 | tf_op jit(solution)/shard_map/concatenate | solution.py:1282
  21.6 6.2 %collective-permute-done.5 = bf16[2,128,512]{2,1,0:T(8,128)(2,1)S(1)} collective-permute-done((bf16[2,128,512]{2,1,0:T(8,128)(2,1)S(1)}, bf16[2,128,512]{2,1,0:T(8,128)(2,1)S(1)}, u32[]{:S(2)}, u32[]{:S(2)}) %collective-permute-start.5) | collective-permute-done | bytes 262176 | tf_op jit(solution)/shard_map/ppermute | solution.py:476
  28.6 7.5 %collective-permute-done.6 = bf16[2,128,512]{2,1,0:T(8,128)(2,1)S(1)} collective-permute-done((bf16[2,128,512]{2,1,0:T(8,128)(2,1)S(1)}, bf16[2,128,512]{2,1,0:T(8,128)(2,1)S(1)}, u32[]{:S(2)}, u32[]{:S(2)}) %collective-permute-start.6) | collective-permute-done | bytes 262176 | tf_op jit(solution)/shard_map/ppermute | solution.py:476
  37.5 6.1 %collective-permute-done.7 = bf16[2,128,512]{2,1,0:T(8,128)(2,1)S(1)} collective-permute-done((bf16[2,128,512]{2,1,0:T(8,128)(2,1)S(1)}, bf16[2,128,512]{2,1,0:T(8,128)(2,1)S(1)}, u32[]{:S(2)}, u32[]{:S(2)}) %collective-permute-start.7) | collective-permute-done | bytes 262176 | tf_op jit(solution)/shard_map/ppermute | solution.py:476
  46.4 9.3 %collective-permute-done.19.rest_1_ = bf16[4,128,512]{2,1,0:T(8,128)(2,1)} collective-permute-done((bf16[4,128,512]{2,1,0:T(8,128)(2,1)S(1)}, bf16[4,128,512]{2,1,0:T(8,128)(2,1)}, u32[]{:S(2)}, u32[]{:S(2)}) %collective-permute-start.19) | collective-permute-done | bytes 524320 | tf_op jit(solution)/shard_map/ppermute | solution.py:476
  56.4 10.7 %all-to-all-start = ((f32[32,1,512]{2,1,0:T(1,128)}), f32[32,1,512]{2,1,0:T(1,128)}, u32[]{:S(2)}, u32[]{:S(2)}) async-start(f32[32,1,512]{2,1,0:T(1,128)} %broadcast_in_dim.135), calls=%async_computation | async-start | bytes 131072 | tf_op jit(solution)/shard_map/all_to_all | solution.py:1290
  70.7 5.4 %all-to-all-done = f32[32,1,512]{2,1,0:T(1,128)} async-done(((f32[32,1,512]{2,1,0:T(1,128)}), f32[32,1,512]{2,1,0:T(1,128)}, u32[]{:S(2)}, u32[]{:S(2)}) %all-to-all-start) | async-done | bytes 65568 | tf_op jit(solution)/shard_map/all_to_all | solution.py:1290
  92.3 9.3 %collective-permute-done.8.rest_2_.rest_8_ = bf16[4,128,512]{2,1,0:T(8,128)(2,1)} collective-permute-done((bf16[4,128,512]{2,1,0:T(8,128)(2,1)S(1)}, bf16[4,128,512]{2,1,0:T(8,128)(2,1)}, u32[]{:S(2)}, u32[]{:S(2)}) %collective-permute-start.8) | collective-permute-done | bytes 524320 | tf_op jit(solution)/shard_map/ppermute | solution.py:472
  103.6 9.2 %collective-permute-done.23.rest_5_ = bf16[4,128,512]{2,1,0:T(8,128)(2,1)S(1)} collective-permute-done((bf16[4,128,512]{2,1,0:T(8,128)(2,1)S(1)}, bf16[4,128,512]{2,1,0:T(8,128)(2,1)S(1)}, u32[]{:S(2)}, u32[]{:S(2)}) %collective-permute-start.23) | collective-permute-done | bytes 524320 | tf_op jit(solution)/shard_map/ppermute | solution.py:472
  116.0 8.1 %collective-permute-done.11.rest_5_.rest_11_ = bf16[4,128,512]{2,1,0:T(8,128)(2,1)} collective-permute-done((bf16[4,128,512]{2,1,0:T(8,128)(2,1)S(1)}, bf16[4,128,512]{2,1,0:T(8,128)(2,1)}, u32[]{:S(2)}, u32[]{:S(2)}) %collective-permute-start.11) | collective-permute-done | bytes 524320 | tf_op jit(solution)/shard_map/ppermute | solution.py:472
  132.0 6.9 %shard_map.274 = (bf16[1024,1024]{1,0:T(8,128)(2,1)S(1)}, bf16[1024,512]{1,0:T(8,128)(2,1)S(1)}, bf16[1024,512]{1,0:T(8,128)(2,1)S(1)}, bf16[1024,512]{1,0:T(8,128)(2,1)S(1)}) custom-call(s32[3]{0:T(128)S(1)} %pad_add_fusion.1.where_ref, bf16[512,1024]{1,0:T(8,128)(2,1)S(1)} %collective-permute-done.own_ref, ...), custom_call_target="tpu_custom_call" | custom-call | flops 322122560 | bytes 1312154 | tf_op jit(solution)/shard_map/pallas_call | solution.py:451
  140.3 13.9 %shard_map.275 = (bf16[1024,512]{1,0:T(8,128)(2,1)S(1)}, f32[4,2,1024]{2,1,0:T(2,128)S(1)}) custom-call(bf16[1024,512]{1,0:T(8,128)(2,1)S(1)} %get-tuple-element.104.query_ref, bf16[1024,512]{1,0:T(8,128)(2,1)S(1)} %get-tuple-element.105.key_ref, bf16[1024,512]{1,0:T(8,128)(2,1)S(1)} %get-tuple-element.106.value_ref), custom_call_target="tpu_custom_call" | custom-call | flops 858993472 | bytes 422707 | tf_op jit(solution)/shard_map/pallas_call | solution.py:451
  159.2 7.2 %collective-permute-start.14 = (bf16[512,1024]{1,0:T(8,128)(2,1)}, bf16[512,1024]{1,0:T(8,128)(2,1)}, u32[]{:S(2)}, u32[]{:S(2)}) collective-permute-start(bf16[512,1024]{1,0:T(8,128)(2,1)} %get-tuple-element.109), channel_id=1, source_target_pairs={{0,2},{2,0},{1,3},{3,1},{4,6},{6,4},{5,7},{7,5},{8,10},{10,8},{9,1... | collective-permute-start | bytes 3145736 | tf_op jit(solution)/shard_map/ppermute | solution.py:472
  169.5 12.5 %collective-permute-done.30.rest_2_ = bf16[2,256,512]{2,1,0:T(8,128)(2,1)} collective-permute-done((bf16[2,256,512]{2,1,0:T(8,128)(2,1)}, bf16[2,256,512]{2,1,0:T(8,128)(2,1)}, u32[]{:S(2)}, u32[]{:S(2)}) %collective-permute-start.30) | collective-permute-done | bytes 524320 | tf_op jit(solution)/shard_map/ppermute | solution.py:476
  203.4 8.8 %collective-permute-done.24.rest_6_ = bf16[4,128,512]{2,1,0:T(8,128)(2,1)} collective-permute-done((bf16[4,128,512]{2,1,0:T(8,128)(2,1)}, bf16[4,128,512]{2,1,0:T(8,128)(2,1)}, u32[]{:S(2)}, u32[]{:S(2)}) %collective-permute-start.24) | collective-permute-done | bytes 524320 | tf_op jit(solution)/shard_map/ppermute | solution.py:472
  212.3 10.9 %shard_map.279 = (bf16[1024,1024]{1,0:T(8,128)(2,1)S(1)}, bf16[1024,2048]{1,0:T(8,128)(2,1)S(1)}, bf16[1024,2048]{1,0:T(8,128)(2,1)S(1)}) custom-call(s32[3]{0:T(128)S(1)} %pad_add_fusion.1.where_ref, bf16[512,1024]{1,0:T(8,128)(2,1)} %get-tuple-element.111.own_ref, bf16[512,1024]{1,0:T(8,128)(2,1)} %collective-permute-done.15.other_ref, ...), custom_call_target="tpu_custom_call" | custom-call | flops 429496736 | bytes 1678542 | tf_op jit(solution)/shard_map/pallas_call | solution.py:451
  227.9 7.8 %shard_map.281 = (bf16[1024,2048]{1,0:T(8,128)(2,1)S(1)}, f32[8,2048]{1,0:T(8,128)S(1)}) custom-call(s32[3]{0:T(128)S(1)} %pad_add_fusion.1.where_ref, bf16[1024,1024]{1,0:T(8,128)(2,1)S(1)} %constant_dynamic-update-slice_fusion.grad_ref, bf16[1024,2048]{1,0:T(8,128)(2,1)S(1)} %get-tuple-element.127.slope_ref, ...), custom_call_target="tpu_custom_call" | custom-call | flops 429496736 | bytes 1474561 | tf_op jit(solution)/shard_map/pallas_call | solution.py:451
  244.7 7.3 %shard_map.284 = (f32[512,1024]{1,0:T(8,128)S(1)}, bf16[512,1024]{1,0:T(8,128)(2,1)S(1)}) custom-call(s32[3]{0:T(128)S(1)} %pad_add_fusion.1.where_ref, bf16[1024,2048]{1,0:T(8,128)(2,1)S(1)} %get-tuple-element.140.grad_ref, bf16[4,128,512]{2,1,0:T(8,128)(2,1)S(1)} %copy-done.28, bf16[4,128,512]{2,1,0:T(8,128)(2,1)} %collective-permute-done.19.rest_1_, ...), custom_call_target="tpu_custom_call" | custom-call | flops 429496736 | bytes 1153434 | tf_op jit(solution)/shard_map/pallas_call | solution.py:451
  285.8 13.1 %shard_map.289 = (bf16[1024,256]{1,0:T(8,128)(2,1)S(1)}, bf16[1024,256]{1,0:T(8,128)(2,1)S(1)}, bf16[1024,256]{1,0:T(8,128)(2,1)S(1)}, f32[8,256]{1,0:T(8,128)S(1)}) custom-call(bf16[1024,512]{1,0:T(8,128)(2,1)S(1)} %copy-done.49, bf16[1024,512]{1,0:T(8,128)(2,1)S(1)} %copy-done.52, bf16[1024,512]{1,0:T(8,128)(2,1)S(1)} %copy-done.55, ...), custom_call_target="tpu_custom_call" | custom-call | flops 1073741824 | bytes 738099 | tf_op jit(solution)/shard_map/pallas_call | solution.py:451
  315.8 13.3 %shard_map.290 = (bf16[1024,256]{1,0:T(8,128)(2,1)S(1)}, bf16[1024,256]{1,0:T(8,128)(2,1)S(1)}, bf16[1024,256]{1,0:T(8,128)(2,1)S(1)}, f32[8,256]{1,0:T(8,128)S(1)}) custom-call(bf16[1024,512]{1,0:T(8,128)(2,1)S(1)} %copy-done.50, bf16[1024,512]{1,0:T(8,128)(2,1)S(1)} %copy-done.53, bf16[1024,512]{1,0:T(8,128)(2,1)S(1)} %copy-done.56, ...), custom_call_target="tpu_custom_call" | custom-call | flops 1073741824 | bytes 738099 | tf_op jit(solution)/shard_map/pallas_call | solution.py:451
  341.7 6.7 %shard_map.292 = (f32[512,1024]{1,0:T(8,128)S(1)}, bf16[512,1024]{1,0:T(8,128)(2,1)}) custom-call(s32[3]{0:T(128)S(1)} %pad_add_fusion.1.where_ref, bf16[1024,256]{1,0:T(8,128)(2,1)S(1)} %copy-done.32, bf16[1024,256]{1,0:T(8,128)(2,1)S(1)} %get-tuple-element.156.rest_1_, bf16[1024,256]{1,0:T(8,128)(2,1)S(1)} %copy-done.35, ...), custom_call_target="tpu_custom_call" | custom-call | flops 322122560 | bytes 1048577 | tf_op jit(solution)/shard_map/pallas_call | solution.py:451
  376.6 5.4 %all-to-all-start.1 = ((f32[32,1,512]{2,1,0:T(1,128)}), f32[32,1,512]{2,1,0:T(1,128)S(1)}, u32[]{:S(2)}, u32[]{:S(2)}) async-start(f32[32,1,512]{2,1,0:T(1,128)} %all_to_all.14), calls=%async_computation.1 | async-start | bytes 131072 | tf_op jit(solution)/shard_map/all_to_all | solution.py:1486
  384.2 7.4 %shard_map.295 = (f32[512,1024]{1,0:T(8,128)S(1)}, bf16[512,1024]{1,0:T(8,128)(2,1)}) custom-call(s32[3]{0:T(128)S(1)} %pad_add_fusion.1.where_ref, bf16[1024,2048]{1,0:T(8,128)(2,1)S(1)} %copy-done.1, bf16[2,256,512]{2,1,0:T(8,128)(2,1)} %pad_maximum_fusion.10.rest_0_, bf16[2,256,512]{2,1,0:T(8,128)(2,1)} %collective-permute-done.29.rest_1_, ...), custom_call_target="tpu_custom_call" | custom-call | flops 429496736 | bytes 1153434 | tf_op jit(solution)/shard_map/pallas_call | solution.py:451
  431.2 6.0 %collective-permute-done.49 = bf16[512,1024]{1,0:T(8,128)(2,1)S(1)} collective-permute-done((bf16[512,1024]{1,0:T(8,128)(2,1)S(1)}, bf16[512,1024]{1,0:T(8,128)(2,1)S(1)}, u32[]{:S(2)}, u32[]{:S(2)}) %collective-permute-start.49) | collective-permute-done | bytes 1048608 | tf_op jit(solution)/shard_map/ppermute | solution.py:1457
  (435 shorter events, 233.9 us)
Async XLA Ops:
  5.9 71.3 %collective-permute-start.28 = (bf16[256,512]{1,0:T(8,128)(2,1)}, bf16[256,512]{1,0:T(8,128)(2,1)}, u32[]{:S(2)}, u32[]{:S(2)}) collective-permute-start(bf16[256,512]{1,0:T(8,128)(2,1)} %param.31), channel_id=1, source_target_pairs={{0,1},{1,0},{2,3},{3,2},{4,5},{5,4},{6,7},{7,6},{8,9},{9,8},{10,11... | collective-permute-start | bytes 786440 | tf_op jit(solution)/shard_map/ppermute | solution.py:472
  8.6 73.0 %collective-permute-start = (bf16[512,1024]{1,0:T(8,128)(2,1)}, bf16[512,1024]{1,0:T(8,128)(2,1)S(1)}, u32[]{:S(2)}, u32[]{:S(2)}) collective-permute-start(bf16[512,1024]{1,0:T(8,128)(2,1)} %param.17), channel_id=1, source_target_pairs={{0,0},{1,2},{2,1},{3,3},{4,4},{5,6},{6,5},{7,7},{8,8},{9,10},{10,9... | collective-permute-start | bytes 3145736 | tf_op jit(solution)/shard_map/ppermute | solution.py:1277
  44.3 32.6 %collective-permute-start.9 = (bf16[4,128,512]{2,1,0:T(8,128)(2,1)S(1)}, bf16[4,128,512]{2,1,0:T(8,128)(2,1)}, u32[]{:S(2)}, u32[]{:S(2)}) collective-permute-start(bf16[4,128,512]{2,1,0:T(8,128)(2,1)S(1)} %pad_maximum_fusion.3.rest_1_.rest_7_), channel_id=1, source_target_pairs={{0,1},{1,0},{2,3},{3,2},{4,5},{5,4},{6,7},{7,6},{8,9},{9,8},{10,11... | collective-permute-start | bytes 1572872 | tf_op jit(solution)/shard_map/ppermute | solution.py:472
  55.8 27.4 %collective-permute-start.20 = (bf16[4,128,512]{2,1,0:T(8,128)(2,1)}, bf16[4,128,512]{2,1,0:T(8,128)(2,1)}, u32[]{:S(2)}, u32[]{:S(2)}) collective-permute-start(bf16[4,128,512]{2,1,0:T(8,128)(2,1)} %collective-permute-done.19.rest_1_), channel_id=1, source_target_pairs={{0,8},{8,16},{16,24},{24,0},{1,9},{9,17},{17,25},{25,1},{2,10},{10... | collective-permute-start | bytes 1572872 | tf_op jit(solution)/shard_map/ppermute | solution.py:476
  80.3 34.0 %collective-permute-start.10 = (bf16[4,128,512]{2,1,0:T(8,128)(2,1)S(1)}, bf16[4,128,512]{2,1,0:T(8,128)(2,1)S(1)}, u32[]{:S(2)}, u32[]{:S(2)}) collective-permute-start(bf16[4,128,512]{2,1,0:T(8,128)(2,1)S(1)} %pad_maximum_fusion.2.rest_0_.rest_6_), channel_id=1, source_target_pairs={{0,1},{1,0},{2,3},{3,2},{4,5},{5,4},{6,7},{7,6},{8,9},{9,8},{10,11... | collective-permute-start | bytes 1572872 | tf_op jit(solution)/shard_map/ppermute | solution.py:472
  81.6 47.2 %collective-permute-start.1 = (bf16[512,1024]{1,0:T(8,128)(2,1)S(1)}, bf16[512,1024]{1,0:T(8,128)(2,1)}, u32[]{:S(2)}, u32[]{:S(2)}) collective-permute-start(bf16[512,1024]{1,0:T(8,128)(2,1)S(1)} %collective-permute-done.own_ref), channel_id=1, source_target_pairs={{0,2},{2,0},{1,3},{3,1},{4,6},{6,4},{5,7},{7,5},{8,10},{10,8},{9,1... | collective-permute-start | bytes 3145736 | tf_op jit(solution)/shard_map/ppermute | solution.py:472
  101.7 27.1 %collective-permute-start.12 = (bf16[4,128,512]{2,1,0:T(8,128)(2,1)}, bf16[4,128,512]{2,1,0:T(8,128)(2,1)}, u32[]{:S(2)}, u32[]{:S(2)}) collective-permute-start(bf16[4,128,512]{2,1,0:T(8,128)(2,1)} %collective-permute-done.8.rest_2_.rest_8_), channel_id=1, source_target_pairs={{0,1},{1,0},{2,3},{3,2},{4,5},{5,4},{6,7},{7,6},{8,9},{9,8},{10,11... | collective-permute-start | bytes 1572872 | tf_op jit(solution)/shard_map/ppermute | solution.py:472
  113.6 52.7 %collective-permute-start.29 = (bf16[2,256,512]{2,1,0:T(8,128)(2,1)}, bf16[2,256,512]{2,1,0:T(8,128)(2,1)}, u32[]{:S(2)}, u32[]{:S(2)}) collective-permute-start(bf16[2,256,512]{2,1,0:T(8,128)(2,1)} %pad_maximum_fusion.10.rest_0_), channel_id=1, source_target_pairs={{0,8},{8,16},{16,24},{24,0},{1,9},{9,17},{17,25},{25,1},{2,10},{10... | collective-permute-start | bytes 1572872 | tf_op jit(solution)/shard_map/ppermute | solution.py:476
  115.2 53.4 %collective-permute-start.25 = (bf16[4,128,512]{2,1,0:T(8,128)(2,1)}, bf16[4,128,512]{2,1,0:T(8,128)(2,1)}, u32[]{:S(2)}, u32[]{:S(2)}) collective-permute-start(bf16[4,128,512]{2,1,0:T(8,128)(2,1)} %pad_maximum_fusion.9), channel_id=1, source_target_pairs={{0,4},{4,0},{1,5},{5,1},{2,6},{6,2},{3,7},{7,3},{8,12},{12,8},{9,1... | collective-permute-start | bytes 1572872 | tf_op jit(solution)/shard_map/ppermute | solution.py:472
  124.1 58.1 %collective-permute-start.26 = (bf16[512,1024]{1,0:T(8,128)(2,1)}, bf16[512,1024]{1,0:T(8,128)(2,1)}, u32[]{:S(2)}, u32[]{:S(2)}) collective-permute-start(bf16[512,1024]{1,0:T(8,128)(2,1)} %param.33), channel_id=1, source_target_pairs={{0,0},{1,2},{2,1},{3,3},{4,4},{5,6},{6,5},{7,7},{8,8},{9,10},{10,9... | collective-permute-start | bytes 3145736 | tf_op jit(solution)/shard_map/ppermute | solution.py:1278
  159.2 27.4 %collective-permute-start.14 = (bf16[512,1024]{1,0:T(8,128)(2,1)}, bf16[512,1024]{1,0:T(8,128)(2,1)}, u32[]{:S(2)}, u32[]{:S(2)}) collective-permute-start(bf16[512,1024]{1,0:T(8,128)(2,1)} %get-tuple-element.109), channel_id=1, source_target_pairs={{0,2},{2,0},{1,3},{3,1},{4,6},{6,4},{5,7},{7,5},{8,10},{10,8},{9,1... | collective-permute-start | bytes 3145736 | tf_op jit(solution)/shard_map/ppermute | solution.py:472
  168.5 30.6 %collective-permute-start.32 = (bf16[4,256,512]{2,1,0:T(8,128)(2,1)}, bf16[4,256,512]{2,1,0:T(8,128)(2,1)}, u32[]{:S(2)}, u32[]{:S(2)}) collective-permute-start(bf16[4,256,512]{2,1,0:T(8,128)(2,1)} %pad_maximum_fusion), channel_id=1, source_target_pairs={{0,4},{4,0},{1,5},{5,1},{2,6},{6,2},{3,7},{7,3},{8,12},{12,8},{9,1... | collective-permute-start | bytes 3145736 | tf_op jit(solution)/shard_map/ppermute | solution.py:472
  199.1 28.8 %collective-permute-start.33 = (bf16[4,256,512]{2,1,0:T(8,128)(2,1)}, bf16[4,256,512]{2,1,0:T(8,128)(2,1)}, u32[]{:S(2)}, u32[]{:S(2)}) collective-permute-start(bf16[4,256,512]{2,1,0:T(8,128)(2,1)} %pad_maximum_fusion.1), channel_id=1, source_target_pairs={{0,4},{4,0},{1,5},{5,1},{2,6},{6,2},{3,7},{7,3},{8,12},{12,8},{9,1... | collective-permute-start | bytes 3145736 | tf_op jit(solution)/shard_map/ppermute | solution.py:472
  226.9 32.9 %collective-permute-start.34 = (bf16[2,2,256,512]{3,2,1,0:T(8,128)(2,1)S(1)}, bf16[2,2,256,512]{3,2,1,0:T(8,128)(2,1)S(1)}, u32[]{:S(2)}, u32[]{:S(2)}) collective-permute-start(bf16[2,2,256,512]{3,2,1,0:T(8,128)(2,1)S(1)} %get-tuple-element.125), channel_id=1, source_target_pairs={{0,4},{4,0},{1,5},{5,1},{2,6},{6,2},{3,7},{7,3},{8,12},{12,8},{9,1... | collective-permute-start | bytes 3145736 | tf_op jit(solution)/shard_map/ppermute | solution.py:472
  267.8 37.2 %collective-permute-start.38 = (bf16[2,2,256,512]{3,2,1,0:T(8,128)(2,1)}, bf16[2,2,256,512]{3,2,1,0:T(8,128)(2,1)}, u32[]{:S(2)}, u32[]{:S(2)}) collective-permute-start(bf16[2,2,256,512]{3,2,1,0:T(8,128)(2,1)} %copy-done.79), channel_id=1, source_target_pairs={{0,4},{4,0},{1,5},{5,1},{2,6},{6,2},{3,7},{7,3},{8,12},{12,8},{9,1... | collective-permute-start | bytes 3145736 | tf_op jit(solution)/shard_map/ppermute | solution.py:472
  268.4 32.9 %collective-permute-start.40 = (bf16[2,2,128,1024]{3,2,1,0:T(8,128)(2,1)}, bf16[2,2,128,1024]{3,2,1,0:T(8,128)(2,1)}, u32[]{:S(2)}, u32[]{:S(2)}) collective-permute-start(bf16[2,2,128,1024]{3,2,1,0:T(8,128)(2,1)} %copy-done.80), channel_id=1, source_target_pairs={{0,1},{1,0},{2,3},{3,2},{4,5},{5,4},{6,7},{7,6},{8,9},{9,8},{10,11... | collective-permute-start | bytes 3145736 | tf_op jit(solution)/shard_map/ppermute | solution.py:472
  271.7 93.1 %collective-permute-start.43 = (bf16[2,2,128,1024]{3,2,1,0:T(8,128)(2,1)}, bf16[2,2,128,1024]{3,2,1,0:T(8,128)(2,1)}, u32[]{:S(2)}, u32[]{:S(2)}) collective-permute-start(bf16[2,2,128,1024]{3,2,1,0:T(8,128)(2,1)} %get-tuple-element.136), channel_id=1, source_target_pairs={{0,1},{1,0},{2,3},{3,2},{4,5},{5,4},{6,7},{7,6},{8,9},{9,8},{10,11... | collective-permute-start | bytes 3145736 | tf_op jit(solution)/shard_map/ppermute | solution.py:472
  303.4 31.0 %collective-permute-start.41 = (bf16[2,128,1024]{2,1,0:T(8,128)(2,1)}, bf16[2,128,1024]{2,1,0:T(8,128)(2,1)}, u32[]{:S(2)}, u32[]{:S(2)}) collective-permute-start(bf16[2,128,1024]{2,1,0:T(8,128)(2,1)} %fusion.6), channel_id=1, source_target_pairs={{0,8},{8,16},{16,24},{24,0},{1,9},{9,17},{17,25},{25,1},{2,10},{10... | collective-permute-start | bytes 1572872 | tf_op jit(solution)/shard_map/ppermute | solution.py:476
  307.1 32.7 %collective-permute-start.42 = (bf16[2,256,512]{2,1,0:T(8,128)(2,1)}, bf16[2,256,512]{2,1,0:T(8,128)(2,1)}, u32[]{:S(2)}, u32[]{:S(2)}) collective-permute-start(bf16[2,256,512]{2,1,0:T(8,128)(2,1)} %fusion.8), channel_id=1, source_target_pairs={{0,8},{8,16},{16,24},{24,0},{1,9},{9,17},{17,25},{25,1},{2,10},{10... | collective-permute-start | bytes 1572872 | tf_op jit(solution)/shard_map/ppermute | solution.py:476
  333.7 38.9 %collective-permute-start.47 = (bf16[2,4,128,512]{3,2,1,0:T(8,128)(2,1)}, bf16[2,4,128,512]{3,2,1,0:T(8,128)(2,1)}, u32[]{:S(2)}, u32[]{:S(2)}) collective-permute-start(bf16[2,4,128,512]{3,2,1,0:T(8,128)(2,1)} %get-tuple-element.162), channel_id=1, source_target_pairs={{0,4},{4,0},{1,5},{5,1},{2,6},{6,2},{3,7},{7,3},{8,12},{12,8},{9,1... | collective-permute-start | bytes 3145736 | tf_op jit(solution)/shard_map/ppermute | solution.py:472
  336.7 28.3 %collective-permute-start.44 = (bf16[2,128,1024]{2,1,0:T(8,128)(2,1)}, bf16[2,128,1024]{2,1,0:T(8,128)(2,1)}, u32[]{:S(2)}, u32[]{:S(2)}) collective-permute-start(bf16[2,128,1024]{2,1,0:T(8,128)(2,1)} %fusion.5), channel_id=1, source_target_pairs={{0,8},{8,16},{16,24},{24,0},{1,9},{9,17},{17,25},{25,1},{2,10},{10... | collective-permute-start | bytes 1572872 | tf_op jit(solution)/shard_map/ppermute | solution.py:476
  338.4 31.7 %collective-permute-start.46 = (bf16[2,4,128,512]{3,2,1,0:T(8,128)(2,1)}, bf16[2,4,128,512]{3,2,1,0:T(8,128)(2,1)}, u32[]{:S(2)}, u32[]{:S(2)}) collective-permute-start(bf16[2,4,128,512]{3,2,1,0:T(8,128)(2,1)} %get-tuple-element.177), channel_id=1, source_target_pairs={{0,1},{1,0},{2,3},{3,2},{4,5},{5,4},{6,7},{7,6},{8,9},{9,8},{10,11... | collective-permute-start | bytes 3145736 | tf_op jit(solution)/shard_map/ppermute | solution.py:472
  364.9 35.0 %collective-permute-start.60 = (bf16[256,512]{1,0:T(8,128)(2,1)}, bf16[256,512]{1,0:T(8,128)(2,1)}, u32[]{:S(2)}, u32[]{:S(2)}) collective-permute-start(bf16[256,512]{1,0:T(8,128)(2,1)} %fusion.24), channel_id=1, source_target_pairs={{0,1},{1,0},{2,3},{3,2},{4,5},{5,4},{6,7},{7,6},{8,9},{9,8},{10,11... | collective-permute-start | bytes 786440 | tf_op jit(solution)/shard_map/ppermute | solution.py:472
  376.6 29.3 %all-to-all-start.1 = ((f32[32,1,512]{2,1,0:T(1,128)}), f32[32,1,512]{2,1,0:T(1,128)S(1)}, u32[]{:S(2)}, u32[]{:S(2)}) async-start(f32[32,1,512]{2,1,0:T(1,128)} %all_to_all.14), calls=%async_computation.1 | async-start | bytes 131072 | tf_op jit(solution)/shard_map/all_to_all | solution.py:1486
  (140 other events, 1356.7 us)

commit v2 on v1

--- a/solution.py
+++ b/solution.py
@@ -400,16 +400,18 @@
 
 
 LOG2E = 1.4426950408889634
-COST = 0.1
+COST = 0.001
 NT = (((1,), (1,)), ((), ()))
 NN = (((1,), (0,)), ((), ()))
 TN = (((0,), (0,)), ((), ()))
 F32 = jnp.float32
 BF16 = jnp.bfloat16
 SWAP = [(0, 1), (1, 0)]
-DIAGONAL = [(0, 0), (1, 2), (2, 1), (3, 3)]
+DIAGONAL = [(1, 2), (2, 1)]
 ANYWHERE = pl.BlockSpec(memory_space=pl.ANY)
 WHOLE = pl.BlockSpec(memory_space=pltpu.VMEM)
+SHARES = 1
+LINES = 128
 SCALARS = pl.BlockSpec(memory_space=pltpu.SMEM)
 
 
@@ -464,6 +466,32 @@
     )(*inputs)
 
 
+def merged_call(*steps, room=8):
+    counts = [(len(a), len(o), len(c)) for _, a, _, o, c in steps]
+    inputs = sum(c[0] for c in counts)
+    outs = sum(c[1] for c in counts)
+
+    def body(*refs):
+        i, o, c = 0, inputs, inputs + outs
+        for (step_body, *_), (ni, no, nc) in zip(steps, counts):
+            step_body(*refs[i : i + ni], *refs[o : o + no], *refs[c : c + nc])
+            i, o, c = i + ni, o + no, c + nc
+
+    found = kernel_call(
+        body,
+        [a for step in steps for a in step[1]],
+        [a for step in steps for a in step[2]],
+        [a for step in steps for a in step[3]],
+        scratch=[a for step in steps for a in step[4]],
+        room=room,
+    )
+    results = []
+    for _, no, _ in counts:
+        results.append(found[:no])
+        found = found[no:]
+    return results
+
+
 def after(values, *others):
     return lax.optimization_barrier((values,) + others)[0]
 
@@ -472,93 +500,27 @@
     return lax.ppermute(values, axis, SWAP)
 
 
+def swap_each(pieces):
+    return [swap(piece, "core") for piece in pieces]
+
+
+def put_rows(refs, columns, value):
+    rows = refs[0].shape[0]
+    for k, ref in enumerate(refs):
+        ref[:, columns] = value[k * rows : (k + 1) * rows].astype(ref.dtype)
+
+
 def ring(values, depth):
     return lax.ppermute(values, "z", [(i, (i + 1) % depth) for i in range(depth)])
 
 
-def gather_first(block, depth):
-    hops = [block]
-    for _ in range(depth - 1):
-        hops.append(ring(hops[-1], depth))
-    one = jnp.stack([hop[0] for hop in hops])
-    two = jnp.stack([hop[1] for hop in hops])
-    one_x = swap(one, "x")
-    two_y = swap(two, "y")
-    one_y = swap(one, "y")
-    two_x = swap(two, "x")
-    one_xy = swap(one_x, "y")
-    two_xy = swap(two_y, "x")
-    arrays = [one, two, one_x, two_y, one_y, two_x, one_xy, two_xy]
-    marks = [(0, 0, 0), (1, 0, 0), (0, 1, 0), (1, 0, 1), (0, 0, 1), (1, 1, 0), (0, 1, 1), (1, 1, 1)]
-    parts = [
-        (n, z, half, z, x, y)
-        for n, (half, x, y) in enumerate(marks)
-        for z in range(depth)
-    ]
-    return arrays, parts, hops[-1], (one_xy, two_xy)
-
-
-def gather_middle(block, depth, hop_gate, swap_gate):
-    one, two = block[0], block[1]
-    hop = jnp.stack([one, swap(one, "x"), two, swap(two, "y")])
-    hops = [hop]
-    for _ in range(depth - 1):
-        hops.append(ring(after(hops[-1], hop_gate), depth))
-    arrays = []
-    parts = []
-    for z in range(depth):
-        parts += [
-            (len(arrays), 0, 0, z, 0, 0),
-            (len(arrays), 1, 0, z, 1, 0),
-            (len(arrays), 2, 1, z, 0, 0),
-            (len(arrays), 3, 1, z, 0, 1),
-        ]
-        arrays.append(hops[z])
-    step = max(depth // 2, 1)
-    for begin in range(0, depth, step):
-        group = hops[begin : begin + step]
-        ones = swap(after(jnp.concatenate([hop[:2] for hop in group]), swap_gate[0]), "y")
-        twos = swap(after(jnp.concatenate([hop[2:] for hop in group]), swap_gate[1]), "x")
-        swap_gate = (ones, twos)
-        for k in range(step):
-            z = begin + k
-            parts += [
-                (len(arrays), 2 * k, 0, z, 0, 1),
-                (len(arrays), 2 * k + 1, 0, z, 1, 1),
-                (len(arrays) + 1, 2 * k, 1, z, 1, 0),
-                (len(arrays) + 1, 2 * k + 1, 1, z, 1, 1),
-            ]
-        arrays += [ones, twos]
-    return arrays, parts, hops[-1], swap_gate
-
-
-def gather_single(block, depth, first, last, hop_gate, swap_gate):
-    hops = [jnp.stack([block, swap(block, first)])]
-    for _ in range(depth - 1):
-        hops.append(ring(after(hops[-1], hop_gate), depth))
-    arrays = []
-    parts = []
-
-    def part(array, index, z, near, far):
-        x, y = (near, far) if first == "x" else (far, near)
-        return (array, index, 0, z, x, y)
-
-    for z in range(depth):
-        parts += [part(len(arrays), k, z, k, 0) for k in range(2)]
-        arrays.append(hops[z])
-    step = max(depth // 2, 1)
-    for begin in range(0, depth, step):
-        group = jnp.concatenate(hops[begin : begin + step])
-        for k in range(2 * step):
-            parts.append(part(len(arrays), k, begin + k // 2, k % 2, 1))
-        arrays.append(swap(after(group, swap_gate), last))
-        swap_gate = arrays[-1]
-    return arrays, parts
-
-
-def place(where_ref, depth, z, x):
-    z_number = lax.rem(where_ref[0] + (depth - z), depth)
-    return 2 * z_number + lax.rem(where_ref[1] + x, 2)
+def place(depth, z, x):
+    z_number = lax.rem(lax.axis_index("z") + (depth - z), depth)
+    return 2 * z_number + lax.rem(lax.axis_index("x") + x, 2)
+
+
+def y_place(y):
+    return lax.rem(lax.axis_index("y") + y, 2)
 
 
 def start_copies(pairs, sems):
@@ -568,11 +530,85 @@
     return copies
 
 
-def add_low(*terms):
-    total = terms[0].astype(F32)
-    for term in terms[1:]:
-        total = total + term.astype(F32)
-    return total.astype(BF16)
+def join_kernel(spans, *refs):
+    out_ref, sems = refs[-2:]
+    pairs = []
+    spot = 0
+    for n, begin, count in spans:
+        pairs.append((refs[n].at[pl.ds(begin, count)], out_ref.at[pl.ds(spot, count)]))
+        spot += count
+    for copy in start_copies(pairs, sems):
+        copy.wait()
+
+
+def join(arrays, spans):
+    total = sum(span[2] for span in spans)
+    (out,) = kernel_call(
+        functools.partial(join_kernel, spans),
+        arrays,
+        [ANYWHERE] * len(arrays),
+        [shape_of((total,) + arrays[0].shape[1:], arrays[0].dtype)],
+        out_specs=[ANYWHERE],
+        scratch=[pltpu.SemaphoreType.DMA((len(spans),))],
+    )
+    return out
+
+
+def choose_kernel(own_ref, other_ref, out_ref, sem):
+    stays = lax.axis_index("core") == lax.axis_index("y")
+
+    @pl.when(stays)
+    def _():
+        copy = pltpu.make_async_copy(own_ref, out_ref, sem)
+        copy.start()
+        copy.wait()
+
+    @pl.when(jnp.logical_not(stays))
+    def _():
+        copy = pltpu.make_async_copy(other_ref, out_ref, sem)
+        copy.start()
+        copy.wait()
+
+
+def trade(values):
+    return lax.ppermute(values, ("core", "y"), DIAGONAL)
+
+
+def choose(own, other):
+    (out,) = kernel_call(
+        choose_kernel,
+        [own, other],
+        [ANYWHERE] * 2,
+        [shape_of(own.shape, own.dtype)],
+        scratch=[pltpu.SemaphoreType.DMA],
+    )
+    return out
+
+
+def add_kernel(*refs):
+    total = None
+    for ref in refs[:-1]:
+        value = ref[(0,) * (len(ref.shape) - 2)].astype(F32)
+        total = value if total is None else total + value
+    refs[-1][0] = total.astype(refs[-1].dtype)
+
+
+def add_blocks(terms, kind=BF16):
+    array, prefix = terms[0]
+    number, rows, columns = array.shape[len(prefix) :]
+
+    def spec(prefix):
+        return pl.BlockSpec((1,) * len(prefix) + (1, rows, columns), lambda i: prefix + (i, 0, 0))
+
+    (out,) = kernel_call(
+        add_kernel,
+        [array for array, _ in terms],
+        [spec(tuple(prefix)) for _, prefix in terms],
+        [shape_of((number, rows, columns), kind)],
+        grid=(number,),
+        out_specs=[spec(())],
+    )
+    return out
 
 
 def near_first(depth):
@@ -583,36 +619,53 @@
 
 class Scatter:
     def __init__(self, sends, first, last, depth):
-        self.arrived = [swap(send, first) for send in sends]
+        self.sends = sends
+        self.arrived = []
+        self.first = first
         self.last = last
         self.depth = depth
         self.spots = [(g, k) for g, group in enumerate(near_first(depth)) for k in range(len(group))]
         self.moving = None
 
+    def send(self, *gates):
+        block = after(self.sends[len(self.arrived)], *gates)
+        self.arrived.append(swap(block, self.first))
+        return self.arrived[-1]
+
     def terms(self, step):
         g, k = self.spots[step]
-        found = [self.keeps[g][k], self.arrived[g][k]]
+        found = [(self.keeps[g], (k,)), (self.arrived[g], (k,))]
         if self.moving is not None:
-            found.append(self.moving)
+            found.append((self.moving, ()))
         return found
 
-    def hop(self, step, gate):
+    def hop(self, step, *gates):
         terms = self.terms(step)
-        terms[0] = after(terms[0], gate)
-        total = add_low(*terms)
+        terms[0] = (after(terms[0][0], *gates), terms[0][1])
+        total = add_blocks(terms)
         self.moving = ring(total, self.depth)
         return total
 
-    def finish(self, gate):
-        terms = self.terms(self.depth - 1)
-        terms[0] = after(terms[0], gate)
-        far = add_low(*[term[1] for term in terms])
-        self.near = [term[0] for term in terms]
-        self.other = swap(far, self.last)
-        return far
-
-    def result(self):
-        return add_low(*self.near, self.other)
+    def finish(self, *gates):
+        found = self.terms(self.depth - 1)
+        found[0] = (after(found[0][0], *gates), found[0][1])
+        far, near = [], []
+        for array, prefix in found:
+            rows, columns = array.shape[-2:]
+            lead = 1
+            for size in array.shape[:-2]:
+                lead *= size
+            begin = prefix[0] * 2 if prefix else 0
+            flat = array.reshape(lead, 1, rows, columns)
+            far.append((flat, (begin + 1,)))
+            near.append((flat, (begin,)))
+        total = add_blocks(far)
+        self.near = near
+        self.other = swap(total, self.last)
+        return total
+
+    def rest(self):
+        return self.near + [(self.other, ())]
 
 
 def turned(values, cosine, before, after):
@@ -645,19 +698,18 @@
     return centred * inverse, inverse
 
 
-def qkv_kernel(depth, parts, where_ref, own_ref, other_ref, gain_ref, shift_ref, bias_ref,
+def qkv_kernel(depth, parts, own_ref, other_ref, rows_ref, bias_ref,
                cosine_ref, before_ref, after_ref, *rest):
     count = 1 + max(p[0] for p in parts)
     arrays = rest[:count]
     normed_ref, query_ref, key_ref, value_ref, weight, sems = rest[count:]
-    y_own = where_ref[2]
     pairs = []
     rows = arrays[0].shape[1]
     wide = query_ref.shape[1]
     thin = wide // 2
     for n, i, half, z, x, y in parts:
-        spot = pl.ds(pl.multiple_of(place(where_ref, depth, z, x) * rows, rows), rows)
-        y_spot = lax.rem(y_own + y, 2)
+        spot = pl.ds(pl.multiple_of(place(depth, z, x) * rows, rows), rows)
+        y_spot = y_place(y)
         if half == 0:
             pairs.append((arrays[n].at[i], weight.at[y_spot, spot, pl.ds(0, wide)]))
         else:
@@ -667,7 +719,7 @@
     for ref, base in ((own_ref, 0), (other_ref, piece)):
         for begin in range(0, piece, 256):
             hat, _ = normal(ref[pl.ds(begin, 256), :].astype(F32))
-            normed_ref[pl.ds(base + begin, 256), :] = (hat * gain_ref[...] + shift_ref[...]).astype(BF16)
+            normed_ref[pl.ds(base + begin, 256), :] = (hat * rows_ref[0:1, :] + rows_ref[1:2, :]).astype(BF16)
     for copy in copies:
         copy.wait()
     outs = [(query_ref, 0), (query_ref, thin), (key_ref, 0), (key_ref, thin), (value_ref, 0), (value_ref, thin)]
@@ -795,15 +847,15 @@
     )
 
 
-def load_proj(where_ref, depth, parts, arrays, weight, sems):
+def load_proj(depth, parts, arrays, weight, sems):
     pairs = []
     group = arrays[0].shape[1] // 2
     thin = weight.shape[2] // 2
     for n, i, half, z, x, y in parts:
         if half == 0:
             continue
-        spot = pl.ds(pl.multiple_of(place(where_ref, depth, z, x) * group, group), group)
-        y_spot = lax.rem(where_ref[2] + y, 2)
+        spot = pl.ds(pl.multiple_of(place(depth, z, x) * group, group), group)
+        y_spot = y_place(y)
         for k in range(2):
             pairs.append(
                 (
@@ -814,62 +866,86 @@
     return start_copies(pairs, sems)
 
 
-def proj_kernel(depth, parts, where_ref, attended_ref, *rest):
+def proj_kernel(depth, parts, attended_ref, *rest):
     count = 1 + max(p[0] for p in parts)
     arrays = rest[:count]
-    keep_ref, send_ref, weight, sems = rest[count:]
+    keep_ref, *sends = rest[count:-2]
+    weight, sems = rest[-2:]
     piece, width = keep_ref.shape
-    for copy in load_proj(where_ref, depth, parts, arrays, weight, sems):
+    for copy in load_proj(depth, parts, arrays, weight, sems):
         copy.wait()
     half = width // 2
     for y in range(2):
         columns = pl.ds(y * half, half)
-        send_ref[:, columns] = dot(attended_ref[pl.ds(piece, piece), :], weight[y], NN, BF16)
+        put_rows(sends, columns, dot(attended_ref[pl.ds(piece, piece), :], weight[y], NN))
     for y in range(2):
         columns = pl.ds(y * half, half)
         keep_ref[:, columns] = dot(attended_ref[pl.ds(0, piece), :], weight[y], NN)
 
 
-def proj_back_kernel(depth, parts, where_ref, own_ref, other_ref, *rest):
+def proj_back_kernel(depth, parts, attended_ref, *rest):
+    halves, rest = rest[: 2 * SHARES], rest[2 * SHARES :]
     count = 1 + max(p[0] for p in parts)
     arrays = rest[:count]
-    out_ref, weight, sems = rest[count:]
-    piece, width = own_ref.shape
-    for copy in load_proj(where_ref, depth, parts, arrays, weight, sems):
+    out_ref, blocks_ref, weight, scratch, branch, sems, branch_sems = rest[count:]
+    copies = start_copies(
+        [(ref, branch.at[pl.ds(n * ref.shape[0], ref.shape[0])]) for n, ref in enumerate(halves)], branch_sems
+    )
+    copies += load_proj(depth, parts, arrays, weight, sems)
+    for copy in copies:
         copy.wait()
+    length, width = branch.shape
+    group = blocks_ref.shape[3] // 2
+    thin = blocks_ref.shape[4]
+    for y_near in range(2):
+        columns = pl.ds(pl.multiple_of(y_place(y_near) * 2 * thin, 128), 2 * thin)
+        scratch[...] = dot(attended_ref[...], branch[:, columns], TN)
+        for x in range(2):
+            for z in range(depth):
+                spot = pl.ds(pl.multiple_of(place(depth, z, x) * group, group), group)
+                block = scratch[spot, :].astype(BF16)
+                for k in range(2):
+                    blocks_ref[x, y_near, z, pl.ds(k * group, group), :] = block[:, k * thin : (k + 1) * thin]
     half = width // 2
-    for ref, begin in ((own_ref, 0), (other_ref, piece)):
-        total = dot(ref[:, pl.ds(0, half)], weight[0], NT) + dot(ref[:, pl.ds(half, half)], weight[1], NT)
-        out_ref[pl.ds(begin, piece), :] = total.astype(BF16)
-
-
-def middle_kernel(own_ref, keep_ref, other_ref, bias_ref, gain_ref, shift_ref, middle_ref, second_ref):
-    for begin in range(0, own_ref.shape[0], 128):
-        rows = pl.ds(begin, 128)
-        middle = own_ref[rows, :].astype(F32) + keep_ref[rows, :] + other_ref[rows, :].astype(F32) + bias_ref[...]
+    for begin in range(0, length, length // 2):
+        rows = pl.ds(begin, length // 2)
+        total = dot(branch[rows, pl.ds(0, half)], weight[0], NT) + dot(branch[rows, pl.ds(half, half)], weight[1], NT)
+        out_ref[rows, :] = total.astype(BF16)
+
+
+def middle_kernel(own_ref, keep_ref, rows_ref, *rest):
+    others, (middle_ref, *seconds) = rest[:SHARES], rest[SHARES:]
+    size = others[0].shape[0]
+    for begin in range(0, SHARES * size, LINES):
+        k = begin // size
+        rows = pl.ds(begin, LINES)
+        lines = pl.ds(begin % size, LINES)
+        middle = own_ref[rows, :].astype(F32) + keep_ref[rows, :] + others[k][lines, :].astype(F32) + rows_ref[4:5, :]
         middle_ref[rows, :] = middle
         hat, _ = normal(middle)
-        second_ref[rows, :] = (hat * gain_ref[...] + shift_ref[...]).astype(BF16)
-
-
-def load_up(where_ref, depth, parts, arrays, weight, sems):
+        seconds[k][lines, :] = (hat * rows_ref[2:3, :] + rows_ref[3:4, :]).astype(BF16)
+
+
+def load_up(depth, parts, arrays, weight, sems):
     pairs = []
     rows, wide = arrays[0].shape[1:]
     for n, i, half, z, x, y in parts:
-        spot = pl.ds(pl.multiple_of(place(where_ref, depth, z, x) * rows, rows), rows)
-        y_spot = lax.rem(where_ref[2] + y, 2)
+        spot = pl.ds(pl.multiple_of(place(depth, z, x) * rows, rows), rows)
+        y_spot = y_place(y)
         pairs.append((arrays[n].at[i], weight.at[y_spot, spot, pl.ds(half * wide, wide)]))
     return start_copies(pairs, sems)
 
 
-def up_kernel(depth, parts, where_ref, own_ref, other_ref, bias_ref, *rest):
+def up_kernel(depth, parts, bias_ref, *rest):
+    halves, rest = rest[: 2 * SHARES], rest[2 * SHARES :]
     count = 1 + max(p[0] for p in parts)
     arrays = rest[:count]
     second_ref, active_ref, slope_ref, weight, sems = rest[count:]
-    copies = load_up(where_ref, depth, parts, arrays, weight, sems)
-    piece = own_ref.shape[0]
-    second_ref[pl.ds(0, piece), :] = own_ref[...]
-    second_ref[pl.ds(piece, piece), :] = other_ref[...]
+    copies = load_up(depth, parts, arrays, weight, sems)
+    size = halves[0].shape[0]
+    piece = size * SHARES
+    for n, ref in enumerate(halves):
+        second_ref[pl.ds(n * size, size), :] = ref[...]
     for copy in copies:
         copy.wait()
     wide = weight.shape[2]
@@ -885,80 +961,118 @@
                 slope_ref[rows, columns] = (gate + hidden * bell).astype(BF16)
 
 
-def hidden_kernel(depth, parts, where_ref, grad_ref, slope_ref, *rest):
+def load_down(depth, parts, arrays, weight, sems):
+    pairs = []
+    rows = arrays[0].shape[1]
+    for n, i, half, z, x, y in parts:
+        line = place(depth, z, x) * (2 * rows) + half * rows
+        spot = pl.ds(pl.multiple_of(line, rows), rows)
+        pairs.append((arrays[n].at[i], weight.at[y_place(y), spot]))
+    return start_copies(pairs, sems)
+
+
+def hidden_kernel(depth, parts, rows, own_ref, other_ref, slope_ref, act_ref, *rest):
     count = 1 + max(p[0] for p in parts)
     arrays = rest[:count]
-    out_ref, sum_ref, weight, sems = rest[count:]
-    for copy in load_up(where_ref, depth, parts, arrays, weight, sems):
+    out_ref, sum_ref, *blocks = rest[count:-6]
+    weight, grad, scratch, sems, grad_sems, act_sems = rest[-6:]
+    piece = own_ref.shape[0]
+    copies = start_copies(
+        [(own_ref, grad.at[pl.ds(0, piece)]), (other_ref, grad.at[pl.ds(piece, piece)])], grad_sems
+    )
+    copies += load_down(depth, parts, arrays, weight, sems)
+    for copy in copies:
         copy.wait()
-    half = grad_ref.shape[1] // 2
+    half = own_ref.shape[1] // 2
     for column in range(0, out_ref.shape[1], 512):
         columns = pl.ds(column, 512)
-        total = dot(grad_ref[:, pl.ds(0, half)], weight[0, columns, :], NT)
-        total = total + dot(grad_ref[:, pl.ds(half, half)], weight[1, columns, :], NT)
+        total = dot(grad[:, pl.ds(0, half)], weight[0, columns, :], NT)
+        total = total + dot(grad[:, pl.ds(half, half)], weight[1, columns, :], NT)
         low = (total * slope_ref[:, columns].astype(F32)).astype(BF16)
         out_ref[:, columns] = low
         sum_ref[0:1, columns] = jnp.sum(low.astype(F32), axis=0, keepdims=True)
-
-
-def down_kernel(depth, parts, where_ref, active_ref, *rest):
+    columns_grad_kernel(depth, rows, 1, act_ref, out_ref, *blocks, scratch, act_sems)
+
+
+def down_kernel(depth, parts, active_ref, *rest):
     count = 1 + max(p[0] for p in parts)
     arrays = rest[:count]
-    keep_ref, send_ref, weight, sems = rest[count:]
+    keep_ref, *sends = rest[count:-2]
+    weight, sems = rest[-2:]
     piece, width = keep_ref.shape
-    for copy in load_up(where_ref, depth, parts, arrays, weight, sems):
+    for copy in load_down(depth, parts, arrays, weight, sems):
         copy.wait()
     half = width // 2
     for y in range(2):
         columns = pl.ds(y * half, half)
-        send_ref[:, columns] = dot(active_ref[pl.ds(piece, piece), :], weight[y], NN, BF16)
+        put_rows(sends, columns, dot(active_ref[pl.ds(piece, piece), :], weight[y], NN))
         keep_ref[:, columns] = dot(active_ref[pl.ds(0, piece), :], weight[y], NN)
 
 
-def up_back_kernel(depth, parts, where_ref, grad_ref, *rest):
+def up_back_kernel(depth, parts, grad_ref, *rest):
     count = 1 + max(p[0] for p in parts)
     arrays = rest[:count]
-    keep_ref, send_ref, weight, sems = rest[count:]
+    keep_ref, *sends = rest[count:-2]
+    weight, sems = rest[-2:]
     piece, width = keep_ref.shape
-    for copy in load_up(where_ref, depth, parts, arrays, weight, sems):
+    for copy in load_up(depth, parts, arrays, weight, sems):
         copy.wait()
     wide = weight.shape[2]
-    for ref, begin in ((send_ref, piece), (keep_ref, 0)):
+    for refs, begin in ((sends, piece), ([keep_ref], 0)):
         rows = pl.ds(begin, piece)
         for column in range(0, width, 512):
             columns = pl.ds(column, 512)
             total = dot(grad_ref[rows, pl.ds(0, wide)], weight[0, columns, :], NT)
             total = total + dot(grad_ref[rows, pl.ds(wide, wide)], weight[1, columns, :], NT)
-            ref[:, columns] = total.astype(ref.dtype)
-
-
-def middle_back_kernel(keep_ref, other_ref, middle_ref, grad_ref, gain_ref, middle_out, branch_out, sum_out):
+            put_rows(refs, columns, total)
+
+
+def middle_back_kernel(keep_ref, middle_ref, grad_ref, rows_ref, *rest):
+    others, (middle_out, *branches, sum_out) = rest[:SHARES], rest[SHARES:]
     totals = [jnp.zeros((1, keep_ref.shape[1]), F32) for _ in range(4)]
-    for begin in range(0, keep_ref.shape[0], 128):
-        rows = pl.ds(begin, 128)
-        grad = keep_ref[rows, :] + other_ref[rows, :].astype(F32)
+    size = others[0].shape[0]
+    for begin in range(0, SHARES * size, LINES):
+        k = begin // size
+        rows = pl.ds(begin, LINES)
+        lines = pl.ds(begin % size, LINES)
+        grad = keep_ref[rows, :] + others[k][lines, :].astype(F32)
         hat, inverse = normal(middle_ref[rows, :])
-        scaled = grad * gain_ref[...]
+        scaled = grad * rows_ref[2:3, :]
         first = jnp.mean(scaled, axis=-1, keepdims=True)
         second = jnp.mean(scaled * hat, axis=-1, keepdims=True)
         outer = grad_ref[rows, :].astype(F32)
         result = outer + inverse * (scaled - first - hat * second)
         middle_out[rows, :] = result
         low = result.astype(BF16)
-        branch_out[rows, :] = low
+        branches[k][lines, :] = low
         for n, value in enumerate((grad * hat, grad, low.astype(F32), outer)):
             totals[n] = totals[n] + jnp.sum(value, axis=0, keepdims=True)
     for n in range(4):
         sum_out[n : n + 1, :] = totals[n]
 
 
-def tokens_back_kernel(keep_ref, other_ref, own_ref, grad_ref, gain_ref, out_ref, sum_out):
+def out_kernel(middle_ref, keep_ref, rows_ref, *rest):
+    others, (out_ref,) = rest[:SHARES], rest[SHARES:]
+    size = others[0].shape[0]
+    for begin in range(0, SHARES * size, LINES):
+        k = begin // size
+        rows = pl.ds(begin, LINES)
+        lines = pl.ds(begin % size, LINES)
+        total = middle_ref[rows, :] + (keep_ref[rows, :] + others[k][lines, :].astype(F32)) + rows_ref[5:6, :]
+        out_ref[rows, :] = total.astype(BF16)
+
+
+def tokens_back_kernel(keep_ref, own_ref, grad_ref, rows_ref, *rest):
+    others, (out_ref, sum_out) = rest[:SHARES], rest[SHARES:]
     totals = [jnp.zeros((1, keep_ref.shape[1]), F32) for _ in range(2)]
-    for begin in range(0, keep_ref.shape[0], 128):
-        rows = pl.ds(begin, 128)
-        grad = keep_ref[rows, :] + other_ref[rows, :].astype(F32)
+    size = others[0].shape[0]
+    for begin in range(0, SHARES * size, LINES):
+        k = begin // size
+        rows = pl.ds(begin, LINES)
+        lines = pl.ds(begin % size, LINES)
+        grad = keep_ref[rows, :] + others[k][lines, :].astype(F32)
         hat, inverse = normal(own_ref[rows, :].astype(F32))
-        scaled = grad * gain_ref[...]
+        scaled = grad * rows_ref[0:1, :]
         first = jnp.mean(scaled, axis=-1, keepdims=True)
         second = jnp.mean(scaled * hat, axis=-1, keepdims=True)
         result = grad_ref[rows, :] + inverse * (scaled - first - hat * second)
@@ -969,64 +1083,72 @@
         sum_out[n : n + 1, :] = totals[n]
 
 
-def load_columns(where_ref, depth, source, scratch, rows, sems):
+def load_columns(depth, source, scratch, rows, sems):
     pairs = []
     for x in range(2):
         for z in range(depth):
-            spot = pl.ds(pl.multiple_of(place(where_ref, depth, z, x) * rows, rows), rows)
+            spot = pl.ds(pl.multiple_of(place(depth, z, x) * rows, rows), rows)
             pairs.append((source.at[:, spot], scratch.at[:, pl.ds((x * depth + z) * rows, rows)]))
     return start_copies(pairs, sems)
 
 
-def rows_grad_kernel(depth, rows, sent, where_ref, act_ref, grad_ref, *rest):
-    outs, scratch, sems = rest[:-2], rest[-2], rest[-1]
+def rows_grad_kernel(depth, rows, sent, act_ref, own_ref, other_ref, *rest):
+    outs, (scratch, grad, sems, grad_sems) = rest[:-4], rest[-4:]
+    piece = own_ref.shape[0]
+    copies = start_copies(
+        [(own_ref, grad.at[pl.ds(0, piece)]), (other_ref, grad.at[pl.ds(piece, piece)])], grad_sems
+    )
     pairs = []
     order = [z for group in near_first(depth) for z in group]
     for n, z in enumerate(order):
-        spot = pl.ds(pl.multiple_of(place(where_ref, depth, z, sent) * rows, rows), rows)
+        spot = pl.ds(pl.multiple_of(place(depth, z, sent) * rows, rows), rows)
         pairs.append((act_ref.at[:, spot], scratch.at[:, pl.ds(n * rows, rows)]))
-    for copy in start_copies(pairs, sems):
+    copies += start_copies(pairs, sems)
+    for copy in copies:
         copy.wait()
-    part = grad_ref.shape[1] // 2
+    part = grad.shape[1] // 2
     begin = 0
     for ref in outs:
         size = ref.shape[0]
         for y_near in range(2):
-            y = lax.rem(where_ref[2] + y_near, 2)
-            columns = pl.ds(pl.multiple_of(y * part, 128), part)
-            result = dot(scratch[:, pl.ds(begin * rows, size * rows)], grad_ref[:, columns], TN, BF16)
+            columns = pl.ds(pl.multiple_of(y_place(y_near) * part, 128), part)
+            result = dot(scratch[:, pl.ds(begin * rows, size * rows)], grad[:, columns], TN, BF16)
             for k in range(size):
                 ref[k, y_near] = result[k * rows : (k + 1) * rows]
         begin += size
 
 
-def rows_grad(where, act, grad, depth, rows, sent):
-    length, total = act.shape
-    part = grad.shape[1] // 2
-    return kernel_call(
+def rows_grad(act, grad_own, grad_other, depth, rows, sent):
+    length = act.shape[0]
+    width = grad_own.shape[1]
+    return (
         functools.partial(rows_grad_kernel, depth, rows, sent),
-        [where, act, grad],
-        [SCALARS, ANYWHERE, WHOLE],
-        [shape_of((len(group), 2, rows, part), BF16) for group in near_first(depth)],
-        scratch=[pltpu.VMEM((length, depth * rows), BF16), pltpu.SemaphoreType.DMA((depth,))],
-        flops=length * total * grad.shape[1],
-    )
-
-
-def columns_grad_kernel(depth, rows, sent, where_ref, act_ref, grad_ref, *rest):
+        [act, grad_own, grad_other],
+        [ANYWHERE] * 3,
+        [shape_of((len(group), 2, rows, width // 2), BF16) for group in near_first(depth)],
+        [
+            pltpu.VMEM((length, depth * rows), BF16),
+            pltpu.VMEM((length, width), BF16),
+            pltpu.SemaphoreType.DMA((depth,)),
+            pltpu.SemaphoreType.DMA((2,)),
+        ],
+    )
+
+
+def columns_grad_kernel(depth, rows, sent, act_ref, grad_ref, *rest):
     outs, scratch, sems = rest[:-2], rest[-2], rest[-1]
     pairs = []
     order = [z for group in near_first(depth) for z in group]
     for n, z in enumerate(order):
         for x in range(2):
-            spot = pl.ds(pl.multiple_of(place(where_ref, depth, z, x) * rows, rows), rows)
+            spot = pl.ds(pl.multiple_of(place(depth, z, x) * rows, rows), rows)
             pairs.append((act_ref.at[:, spot], scratch.at[:, pl.ds((2 * n + x) * rows, rows)]))
     for copy in start_copies(pairs, sems):
         copy.wait()
     part = grad_ref.shape[1] // 2
     begin = 0
     half = part // 2
-    y = lax.rem(where_ref[2] + sent, 2)
+    y = y_place(sent)
     for ref in outs:
         size = ref.shape[0]
         for column in range(0, part, half):
@@ -1039,16 +1161,15 @@
         begin += 2 * size
 
 
-def columns_grad(where, act, grad, depth, rows, sent):
+def columns_grad(act, grad, depth, rows, sent):
     length, total = act.shape
     part = grad.shape[1] // 2
-    return kernel_call(
+    return (
         functools.partial(columns_grad_kernel, depth, rows, sent),
-        [where, act, grad],
-        [SCALARS, ANYWHERE, WHOLE],
+        [act, grad],
+        [ANYWHERE, WHOLE],
         [shape_of((len(group), 2, rows, part), BF16) for group in near_first(depth)],
-        scratch=[pltpu.VMEM((length, total), BF16), pltpu.SemaphoreType.DMA((2 * depth,))],
-        flops=length * total * grad.shape[1],
+        [pltpu.VMEM((length, total), BF16), pltpu.SemaphoreType.DMA((2 * depth,))],
     )
 
 
@@ -1057,8 +1178,8 @@
     return jnp.where(first, mine, other), jnp.where(first, other, mine)
 
 
-def split_kernel(hidden_block, core_ref, qkv_ref, up_ref, qkv_mine, qkv_other, up_mine, up_other):
-    core = core_ref[0]
+def split_kernel(hidden_block, qkv_ref, up_ref, qkv_mine, qkv_other, up_mine, up_other):
+    core = lax.axis_index("core")
     rows = qkv_ref.shape[0]
     low = lax.broadcasted_iota(jnp.int32, (rows, 128), 1) < 64
     for tile in range(qkv_ref.shape[1] // 256):
@@ -1077,11 +1198,11 @@
         up_other[:, pl.ds(tile * hidden_block, hidden_block)] = other
 
 
-def pack_kernel(core_ref, mine_ref, other_ref, *rest):
+def pack_kernel(mine_ref, other_ref, *rest):
     extra, out_ref = rest[:-1], rest[-1]
     rows, columns = mine_ref.shape
     half = out_ref.shape[2]
-    for ref, number in ((mine_ref, core_ref[0]), (other_ref, 1 - core_ref[0])):
+    for ref, number in ((mine_ref, lax.axis_index("core")), (other_ref, 1 - lax.axis_index("core"))):
         lines = pl.ds(pl.multiple_of(number * rows, rows), rows)
         out_ref[0, lines, :] = ref[:, pl.ds(0, half)]
         out_ref[1, lines, pl.ds(0, columns - half)] = ref[:, pl.ds(half, columns - half)]
@@ -1091,46 +1212,30 @@
             out_ref[1, pl.ds(k * rows, rows), pl.ds(half - thin, thin)] = ref[:, pl.ds(k * thin, thin)]
 
 
-def join_heads_kernel(core_ref, mine_ref, other_ref, out_ref):
+def join_heads_kernel(mine_ref, other_ref, out_ref):
     rows = mine_ref.shape[0]
     low = lax.broadcasted_iota(jnp.int32, (rows, 128), 1) < 64
     for tile in range(mine_ref.shape[1] // 128):
         columns = pl.ds(tile * 128, 128)
-        even, odd = own_half(core_ref[0], mine_ref[:, columns].astype(F32), other_ref[:, columns].astype(F32))
+        even, odd = own_half(lax.axis_index("core"), mine_ref[:, columns].astype(F32), other_ref[:, columns].astype(F32))
         out_ref[:, pl.ds(tile * 256, 128)] = jnp.where(low, even, pltpu.roll(odd, 64, 1))
         out_ref[:, pl.ds(tile * 256 + 128, 128)] = jnp.where(low, pltpu.roll(even, 64, 1), odd)
 
 
-def join_blocks_kernel(block, core_ref, mine_ref, other_ref, out_ref):
+def join_blocks_kernel(block, mine_ref, other_ref, out_ref):
     for tile in range(mine_ref.shape[1] // block):
         columns = pl.ds(tile * block, block)
-        even, odd = own_half(core_ref[0], mine_ref[:, columns].astype(F32), other_ref[:, columns].astype(F32))
+        even, odd = own_half(lax.axis_index("core"), mine_ref[:, columns].astype(F32), other_ref[:, columns].astype(F32))
         out_ref[:, pl.ds(2 * tile * block, block)] = even
         out_ref[:, pl.ds((2 * tile + 1) * block, block)] = odd
 
 
-def proj_grad_kernel(depth, where_ref, attended_ref, own_ref, other_ref, out_ref, scratch):
-    piece = own_ref.shape[0]
-    group = out_ref.shape[3] // 2
-    thin = out_ref.shape[4]
-    for y_near in range(2):
-        y = lax.rem(where_ref[2] + y_near, 2)
-        columns = pl.ds(pl.multiple_of(y * 2 * thin, 128), 2 * thin)
-        result = dot(attended_ref[pl.ds(0, piece), :], own_ref[:, columns], TN)
-        scratch[...] = result + dot(attended_ref[pl.ds(piece, piece), :], other_ref[:, columns], TN)
-        for x in range(2):
-            for z in range(depth):
-                spot = pl.ds(pl.multiple_of(place(where_ref, depth, z, x) * group, group), group)
-                block = scratch[spot, :].astype(BF16)
-                for k in range(2):
-                    out_ref[x, y_near, z, pl.ds(k * group, group), :] = block[:, k * thin : (k + 1) * thin]
-
-
-def mixed_grad_kernel(depth, sent, where_ref, act_ref, *rest):
-    count = len(rest) - 7
-    pieces, (proj_ref, one_ref, two_ref, scratch, mixed, sems, mixed_sems) = rest[:count], rest[count:]
-    rows = one_ref.shape[2]
-    copies = load_columns(where_ref, depth, act_ref, scratch, rows, sems)
+def mixed_grad_kernel(depth, sent, act_ref, *rest):
+    count = len(rest) - 9
+    pieces, (proj_ref, *outs) = rest[:count], rest[count : count + 5]
+    scratch, mixed, sems, mixed_sems = rest[count + 5 :]
+    rows = outs[0].shape[1]
+    copies = load_columns(depth, act_ref, scratch, rows, sems)
     size = pieces[0].shape[1]
     wide = size * count // 3
     thin = wide // 2
@@ -1142,50 +1247,207 @@
         copy.wait()
     part = wide + thin
     half = depth * rows
-    y = lax.rem(where_ref[2] + sent, 2)
-    columns = pl.ds(pl.multiple_of(y * part, 128), wide)
+    columns = pl.ds(pl.multiple_of(y_place(sent) * part, 128), wide)
     for x in range(2):
         result = dot(scratch[:, pl.ds(x * half, half)], mixed[:, columns], TN, BF16)
         for z in range(depth):
-            one_ref[x, z] = result[z * rows : (z + 1) * rows]
+            outs[1 - x][z] = result[z * rows : (z + 1) * rows]
     for y_near in range(2):
-        y = lax.rem(where_ref[2] + y_near, 2)
-        columns = pl.ds(pl.multiple_of(y * part + wide, 128), thin)
+        columns = pl.ds(pl.multiple_of(y_place(y_near) * part + wide, 128), thin)
         result = dot(scratch[:, pl.ds(sent * half, half)], mixed[:, columns], TN, BF16)
         for z in range(depth):
-            two_ref[y_near, z, :, pl.ds(0, thin)] = result[z * rows : (z + 1) * rows]
-            two_ref[y_near, z, :, pl.ds(thin, thin)] = proj_ref[sent, y_near, z]
-
-
-def mixed_back_kernel(depth, parts, count, where_ref, *rest):
+            outs[3 - y_near][z, :, pl.ds(0, thin)] = result[z * rows : (z + 1) * rows]
+            outs[3 - y_near][z, :, pl.ds(thin, thin)] = proj_ref[sent, y_near, z]
+
+
+def mixed_back_kernel(depth, parts, count, *rest):
     pieces, rest = rest[:count], rest[count:]
     arrays = rest[: 1 + max(p[0] for p in parts)]
-    keep_ref, send_ref, weight, sems = rest[len(arrays) :]
+    keep_ref, *sends = rest[len(arrays) : -4]
+    weight, mixed, sems, mixed_sems = rest[-4:]
     pairs = []
     rows = arrays[0].shape[1]
     size = pieces[0].shape[1]
     wide = size * count // 3
     thin = wide // 2
+    copies = start_copies(
+        [(ref, mixed.at[:, pl.ds(n * size, size)]) for n, ref in enumerate(pieces)], mixed_sems
+    )
     for n, i, half, z, x, y in parts:
-        spot = pl.ds(pl.multiple_of(place(where_ref, depth, z, x) * rows, rows), rows)
-        y_spot = lax.rem(where_ref[2] + y, 2)
+        spot = pl.ds(pl.multiple_of(place(depth, z, x) * rows, rows), rows)
+        y_spot = y_place(y)
         if half == 0:
             pairs.append((arrays[n].at[i], weight.at[y_spot, spot, pl.ds(0, wide)]))
         else:
             pairs.append((arrays[n].at[i, :, pl.ds(0, thin)], weight.at[y_spot, spot, pl.ds(wide, thin)]))
-    for copy in start_copies(pairs, sems):
+    copies += start_copies(pairs, sems)
+    for copy in copies:
         copy.wait()
     piece, width = keep_ref.shape
-    for ref, begin in ((send_ref, piece), (keep_ref, 0)):
+    part = wide + thin
+    for refs, begin in ((sends, piece), ([keep_ref], 0)):
         lines = pl.ds(begin, piece)
         for column in range(0, width, 512):
             columns = pl.ds(column, 512)
-            total = None
-            for n, item in enumerate(pieces):
-                y, spot = divmod(n * size, wide + thin)
-                term = dot(item[lines, :], weight[y, columns, pl.ds(spot, size)], NT)
-                total = term if total is None else total + term
-            ref[:, columns] = total.astype(ref.dtype)
+            total = dot(mixed[lines, pl.ds(0, part)], weight[0, columns, :], NT)
+            total = total + dot(mixed[lines, pl.ds(part, part)], weight[1, columns, :], NT)
+            put_rows(refs, columns, total)
+
+
+def sum_of(refs):
+    total = None
+    for ref in refs:
+        value = ref[(0,) * (len(ref.shape) - 2)].astype(F32)
+        total = value if total is None else total + value
+    return total
+
+
+def core_rows(values_ref, rows, mine_ref, send_ref):
+    core = lax.axis_index("core")
+    mine_ref[...] = values_ref[pl.ds(pl.multiple_of(core * rows, rows), rows), :]
+    send_ref[...] = values_ref[pl.ds(pl.multiple_of((1 - core) * rows, rows), rows), :].astype(BF16)
+
+
+def finish_up_kernel(*refs):
+    mine_ref, send_ref, total = refs[-3:]
+    total[...] = sum_of(refs[:-3])
+    core_rows(total, mine_ref.shape[0], mine_ref, send_ref)
+
+
+def finish_down_kernel(*refs):
+    refs[-1][...] = sum_of(refs[:-1])
+
+
+def hop_first_kernel(*refs):
+    out_ref = refs[-1]
+    ones, twos = refs[0:3], refs[3:6]
+    for half, group in ((0, ones), (1, twos)):
+        total = sum_of(group)
+        if len(refs) > 7:
+            total = total + refs[6][half].astype(F32)
+        out_ref[half] = total.astype(BF16)
+
+
+def finish_first_kernel(*refs):
+    moving = refs[6]
+    mine_ref, send_ref, proj_ref, total = refs[7:]
+    one = sum_of(refs[0:3]) + moving[0].astype(F32)
+    two = sum_of(refs[3:6]) + moving[1].astype(F32)
+    wide = one.shape[1]
+    thin = total.shape[1] - wide
+    total[:, pl.ds(0, wide)] = one
+    total[:, pl.ds(wide, thin)] = two[:, :thin]
+    core_rows(total, mine_ref.shape[0], mine_ref, send_ref)
+    group = proj_ref.shape[0]
+    for k in range(2):
+        proj_ref[:, pl.ds(k * (wide - thin), wide - thin)] = two[k * group : (k + 1) * group, thin:]
+
+
+def first_terms(keeps, nears, lasts, z):
+    arrays, specs = [], []
+    for keep_one, near, last in zip(keeps, nears, lasts):
+        rows, columns = last.shape[-2:]
+        arrays += [keep_one, near, last]
+        specs += [pl.BlockSpec((1, rows, columns), lambda i: (z, 0, 0))] * 3
+    return arrays, specs
+
+
+def same(shape):
+    return pl.BlockSpec(shape, lambda i: (0,) * len(shape))
+
+
+EACH = 32
+ROW = 512
+
+
+def params_kernel(count, head_size, hidden_block, in_ref, rows_ref, qkv_ref, up_ref):
+    core = lax.axis_index("core")
+    row = lax.broadcasted_iota(jnp.int32, (count, 128), 0)
+    lane = lax.broadcasted_iota(jnp.int32, (count, 128), 1)
+    per = 128 // EACH
+    for i in range(6):
+        tile = in_ref[:, pl.ds(i // per * 128, 128)]
+        shift = (128 - i % per * EACH) % 128
+        first = jnp.where(lane < EACH, pltpu.roll(tile, shift, 1) if shift else tile, 0.0)
+        wide = first
+        for k in range(1, per):
+            wide = wide + pltpu.roll(first, k * EACH, 1)
+        for k in range(count // per):
+            picked = jnp.where(row == k * per + lane // EACH, wide, 0.0)
+            rows_ref[i : i + 1, pl.ds(k * 128, 128)] = jnp.sum(picked, axis=0, keepdims=True)
+    one_lane = lax.broadcasted_iota(jnp.int32, (1, 128), 1)
+    size = 3 * EACH
+    low = one_lane < head_size
+    for t in range(qkv_ref.shape[1] // 128):
+        pair = []
+        for k in (2 * t, 2 * t + 1):
+            tile = jnp.zeros((1, 128), F32)
+            for d in range(k * 128 // size, (k * 128 + 127) // size + 1):
+                offset = d * size - k * 128
+                value = in_ref[d : d + 1, pl.ds(256, 128)]
+                value = pltpu.roll(value, offset % 128, 1) if offset % 128 else value
+                tile = jnp.where((one_lane >= offset) & (one_lane < offset + size), value, tile)
+            pair.append(tile)
+        even = jnp.where(low, pair[0], pltpu.roll(pair[1], head_size, 1))
+        odd = jnp.where(low, pltpu.roll(pair[0], head_size, 1), pair[1])
+        qkv_ref[:, pl.ds(t * 128, 128)] = jnp.where(core == 0, even, odd)
+    tiles = hidden_block // 128
+    for t in range(up_ref.shape[1] // 128):
+        m, q = divmod(t, tiles)
+        spots = [2 * m * tiles + q, (2 * m + 1) * tiles + q]
+        even, odd = [in_ref[d : d + 1, pl.ds(384, 128)] for d in spots]
+        up_ref[:, pl.ds(t * 128, 128)] = jnp.where(core == 0, even, odd)
+
+
+def small_kernel(count, head_size, hidden_block, mixed_count, *refs):
+    first_ref, middle_ref, up_ref = refs[:3]
+    mixed_refs = refs[3 : 3 + mixed_count]
+    out_ref = refs[-1]
+    core = lax.axis_index("core")
+    row = lax.broadcasted_iota(jnp.int32, (count, 128), 0)
+    lane = lax.broadcasted_iota(jnp.int32, (count, 128), 1)
+    per = 128 // EACH
+    vectors = [(first_ref, 0), (first_ref, 1), (middle_ref, 0), (middle_ref, 1), (middle_ref, 2), (middle_ref, 3)]
+    tiles = [jnp.zeros((count, 128), F32) for _ in range(2)]
+    for i, (ref, line) in enumerate(vectors):
+        spread = jnp.zeros((count, 128), F32)
+        for k in range(count // per):
+            spread = jnp.where(row // per == k, ref[line : line + 1, pl.ds(k * 128, 128)], spread)
+        moved = spread
+        for k in range(per):
+            shift = (i % per - k) * EACH % 128
+            if shift:
+                moved = jnp.where(row % per == k, pltpu.roll(spread, shift, 1), moved)
+        tiles[i // per] = jnp.where(lane // EACH == i % per, moved, tiles[i // per])
+    for n, tile in enumerate(tiles):
+        out_ref[:, pl.ds(n * 128, 128)] = tile
+    one_lane = lax.broadcasted_iota(jnp.int32, (1, 128), 1)
+    low = one_lane < head_size
+    size = 3 * EACH
+    globals_ = []
+    for line in range(3):
+        for ref in mixed_refs:
+            for k in range(ref.shape[1] // 128):
+                value = ref[line : line + 1, pl.ds(k * 128, 128)]
+                other = pltpu.roll(value, head_size, 1)
+                even = core == 0
+                globals_.append(jnp.where(low == even, jnp.where(even, value, other), 0.0))
+                globals_.append(jnp.where(low == even, jnp.where(even, other, value), 0.0))
+    for d in range(count):
+        total = jnp.zeros((1, 128), F32)
+        for k in range(d * size // 128, (d * size + size - 1) // 128 + 1):
+            offset = k * 128 - d * size
+            value = pltpu.roll(globals_[k], offset % 128, 1) if offset % 128 else globals_[k]
+            inside = (one_lane >= offset) & (one_lane < offset + 128) & (one_lane < size)
+            total = jnp.where(inside, value, total)
+        out_ref[d : d + 1, pl.ds(256, 128)] = total
+    steps = hidden_block // 128
+    for t in range(up_ref.shape[1] // 128):
+        m, q = divmod(t, steps)
+        value = up_ref[0:1, pl.ds(t * 128, 128)]
+        for p in range(2):
+            d = (2 * m + p) * steps + q
+            out_ref[d : d + 1, pl.ds(384, 128)] = jnp.where(core == p, value, 0.0)
 
 
 HALF = 10
@@ -1209,16 +1471,6 @@
     sine = jnp.where(live, jnp.sin(angles), 0.0)
     low = (spot < half_size)[None, :]
     return cosine, jnp.where(low, -sine, 0.0), jnp.where(low, 0.0, sine)
-
-
-def ordered(index, first, second, axis=0):
-    low = jnp.where(index == 0, first, second)
-    high = jnp.where(index == 0, second, first)
-    return jnp.stack([low, high], axis=axis)
-
-
-def taken(values, index, axis):
-    return lax.dynamic_index_in_dim(values, index, axis, keepdims=False)
 
 
 def fast_shards(
@@ -1240,9 +1492,7 @@
     down_bias,
     cotangent,
 ):
-    core = lax.axis_index("core")
     depth = lax.axis_size("z")
-    where = jnp.stack([lax.axis_index("z"), lax.axis_index("x"), lax.axis_index("y")]).astype(jnp.int32)
     everyone = ("z", "x", "core", "y")
     count = 8 * depth
     piece, width = tokens.shape
@@ -1250,280 +1500,431 @@
     head_size = width // HEADS
     local = width // 2
     hidden_block = down_weight.shape[0]
-
-    cores = jnp.stack([core]).astype(jnp.int32)
+    hidden_size = up_weight.shape[1]
     up_rows = width // (2 * depth)
     shard_rows = qkv_weight.shape[0]
     part_qkv = 3 * local // 2
     part_up = up_weight.shape[1] // 2
     block_kind = shape_of((2, up_rows, local), BF16)
+    step = max(depth // 2, 1)
+    dma = pltpu.SemaphoreType.DMA
+    shares = [shape_of((piece // SHARES, width), BF16)] * SHARES
+    partial = [shape_of((piece, width), F32)] + shares
 
     qkv_mine, qkv_other, up_mine, up_other = kernel_call(
         functools.partial(split_kernel, hidden_block),
-        [cores, qkv_weight, up_weight],
-        [SCALARS, WHOLE, WHOLE],
+        [qkv_weight, up_weight],
+        [WHOLE, WHOLE],
         [shape_of((shard_rows, part_qkv), BF16)] * 2 + [shape_of((shard_rows, part_up), BF16)] * 2,
     )
     (first_block,) = kernel_call(
-        pack_kernel,
-        [cores, qkv_mine, swap(qkv_other, "core"), proj_weight],
-        [SCALARS] + [WHOLE] * 3,
-        [block_kind],
-    )
-    (up_block,) = kernel_call(
-        pack_kernel, [cores, up_mine, swap(up_other, "core")], [SCALARS] + [WHOLE] * 2, [block_kind]
-    )
-    first_arrays, first_parts, hop_gate, swap_gate = gather_first(first_block, depth)
-    tokens_own = lax.ppermute(tokens, ("core", "y"), DIAGONAL)
-    grad_own = lax.ppermute(after(cotangent, tokens_own), ("core", "y"), DIAGONAL)
-    up_arrays, up_parts, hop_gate, swap_gate = gather_middle(up_block, depth, hop_gate, swap_gate)
-    down_arrays, down_parts = gather_single(down_weight, depth, "y", "x", hop_gate, swap_gate[1])
-
-    small = jnp.concatenate(
-        [norm1_gain, norm1_bias, norm2_gain, norm2_bias, proj_bias, down_bias, qkv_bias, up_bias]
-    )
-    small = after(small, first_block)
-    used = small.shape[0]
-    small = jnp.broadcast_to(
-        jnp.concatenate([small.astype(F32), jnp.zeros((512 - used,), F32)]), (count, 512)
-    )
+        pack_kernel, [qkv_mine, swap(qkv_other, "core"), proj_weight], [WHOLE] * 3, [block_kind]
+    )
+    now = (first_block,)
+
+    def at(values):
+        return after(values, *now)
+
+    def packed_small():
+        return jnp.concatenate(
+            [
+                at(item)
+                for item in (norm1_gain, norm1_bias, norm2_gain, norm2_bias, proj_bias, down_bias)
+            ]
+            + [jnp.zeros((256 - 6 * EACH,), BF16), qkv_bias, jnp.zeros((EACH,), BF16), up_bias]
+        )
+
+    hops = [first_block, ring(first_block, depth)]
+    tokens_traded = trade(at(tokens))
+    places = jnp.stack([frame_index, row_index, column_index], axis=0)
+    places_traded = trade(at(places))
+    small = packed_small()
+    up_other = swap(at(up_other), "core")
+    now = (hops[1], up_other, small)
+    hops.append(ring(at(hops[1]), depth))
+    grad_traded = trade(at(cotangent))
+    (up_block,) = kernel_call(pack_kernel, [at(up_mine), up_other], [WHOLE] * 2, [block_kind])
+    now = (hops[2], up_block, tokens_traded)
+    while len(hops) < depth:
+        hops.append(ring(at(hops[-1]), depth))
+
+    def far_halves(block):
+        block = at(block)
+        return [block, swap(block[0], "x")[None], swap(block[1], "y")[None]]
+
+    def doubled(parts):
+        return join([at(parts[0])] + parts[1:], [(0, 0, 1), (1, 0, 1), (0, 1, 1), (2, 0, 1)])
+
+    def two_halves(hops):
+        return [join([at(hops[0])] + hops[1:], [(n, half, 1) for n in range(depth)]) for half in range(2)]
+
+    small = jnp.broadcast_to(at(small).astype(F32), (count, ROW))
     small = lax.all_to_all(small, everyone, split_axis=0, concat_axis=0, tiled=True)
-    each = norm1_gain.shape[0]
-    gain_one, shift_one, gain_two, shift_two, bias_proj, bias_down = [
-        small[:, i * each : (i + 1) * each].reshape(1, width) for i in range(6)
+    places = choose(at(places), places_traded)
+    places = jnp.concatenate([places, swap(places, "core")], axis=1).T
+    grad_own = choose(at(cotangent), grad_traded)
+    tokens_own = choose(at(tokens), tokens_traded)
+    tokens_other = swap(tokens_own, "core")
+    now = (hops[-1], tokens_other, places, grad_own, small)
+
+    one, two = two_halves(hops)
+    one_x = swap(one, "x")
+    two_y = swap(two, "y")
+    one_y = swap(one, "y")
+    two_x = swap(two, "x")
+    up_hops = [up_block, ring(at(up_block), depth)]
+    turn = turn_tables(at(places), head_size, 2 * head_size)
+    grad_other = swap(at(grad_own), "core")
+    now = (one_x, two_y, up_hops[-1], grad_other, *turn)
+    one_xy = swap(at(one_x), "y")
+    two_xy = swap(at(two_y), "x")
+    up_hops.append(ring(at(up_hops[-1]), depth))
+    params, bias_qkv, bias_up = kernel_call(
+        functools.partial(params_kernel, count, head_size, hidden_block),
+        [at(small)],
+        [WHOLE],
+        [shape_of((8, width), F32), shape_of((1, 3 * local), F32), shape_of((1, hidden_size), F32)],
+    )
+    now = (one_y, two_x, up_hops[-1], params)
+    while len(up_hops) < depth:
+        up_hops.append(ring(at(up_hops[-1]), depth))
+    down_far = far_halves(down_weight.reshape(2, hidden_block // 2, -1))
+    now = (one_xy, two_xy, up_hops[-1], *down_far)
+
+    first_arrays = [one, two, one_x, two_y, one_y, two_x, one_xy, two_xy]
+    marks = [(0, 0, 0), (1, 0, 0), (0, 1, 0), (1, 0, 1), (0, 0, 1), (1, 1, 0), (0, 1, 1), (1, 1, 1)]
+    first_parts = [
+        (n, z, half, z, x, y) for n, (half, x, y) in enumerate(marks) for z in range(depth)
     ]
-    spot = 6 * each
-    bias_qkv = small[:, spot : spot + qkv_bias.shape[0]].reshape(-1, 2, head_size)
-    spot += qkv_bias.shape[0]
-    bias_up = small[:, spot : spot + up_bias.shape[0]].reshape(-1, 2, hidden_block)
-    bias_qkv = taken(bias_qkv, core, 1).reshape(1, -1)
-    bias_up = taken(bias_up, core, 1).reshape(1, -1)
-
-    places = jnp.stack([frame_index, row_index, column_index], axis=0)
-    places = lax.ppermute(places, ("core", "y"), DIAGONAL)
-    places = jnp.concatenate([places, swap(places, "core")], axis=1).T
-    tokens_other = swap(tokens_own, "core")
-    grad_full = jnp.concatenate([grad_own, swap(grad_own, "core")])
-    turn = turn_tables(places, head_size, 2 * head_size)
-
     part_count = len(first_parts)
-    dma = pltpu.SemaphoreType.DMA
+    pair_parts = []
+    for z in range(depth):
+        pair_parts += [(z, 0, 0, z, 0, 0), (z, 1, 0, z, 1, 0), (z, 2, 1, z, 0, 0), (z, 3, 1, z, 0, 1)]
+        array = depth + 2 * (z // step)
+        k = z % step
+        pair_parts += [
+            (array, 2 * k, 0, z, 0, 1),
+            (array, 2 * k + 1, 0, z, 1, 1),
+            (array + 1, 2 * k, 1, z, 1, 0),
+            (array + 1, 2 * k + 1, 1, z, 1, 1),
+        ]
+    pair_count = len(pair_parts)
+
+    up_one, up_two = two_halves(up_hops)
+    down_hops = [doubled(down_far)]
+    up_one_x = swap(up_one, "x")
+    up_two_y = swap(up_two, "y")
+    up_one_y = swap(up_one, "y")
+    up_two_x = swap(up_two, "x")
+    down_hops.append(ring(down_hops[0], depth))
     normed, queries, keys, values = kernel_call(
         functools.partial(qkv_kernel, depth, first_parts),
-        [where, tokens_own, tokens_other, gain_one, shift_one, bias_qkv, *turn, *first_arrays],
-        [SCALARS] + [WHOLE] * 8 + [ANYWHERE] * len(first_arrays),
+        [after(tokens_own, up_one, up_two, down_hops[0]), tokens_other, params, bias_qkv, *turn, *first_arrays],
+        [WHOLE] * 7 + [ANYWHERE] * len(first_arrays),
         [shape_of((length, width), BF16)] + [shape_of((length, local), BF16)] * 3,
         scratch=[pltpu.VMEM((2, width, 3 * local // 2), BF16), dma((part_count,))],
-        flops=2 * length * width * 3 * local,
-    )
-    attended, logs = attend(queries, keys, values, head_size)
+    )
+    now = (normed, up_one_x, up_two_y, down_hops[-1])
+    up_one_xy = swap(at(up_one_x), "y")
+    up_two_xy = swap(at(up_two_y), "x")
+    up_arrays = [up_one, up_two, up_one_x, up_two_y, up_one_y, up_two_x, up_one_xy, up_two_xy]
+    down_hops.append(ring(at(down_hops[-1]), depth))
+    attended, logs = attend(at(queries), keys, values, head_size)
+    now = (attended, up_one_y, up_two_x, up_one_xy, up_two_xy, down_hops[-1])
+
+    def last_pair(group):
+        ones = join([at(group[0])] + group[1:], [(n, 0, 2) for n in range(len(group))])
+        twos = join([at(group[0])] + group[1:], [(n, 2, 2) for n in range(len(group))])
+        return ones, twos
+
+    def last_swaps(pair):
+        return [swap(at(pair[0]), "y"), swap(at(pair[1]), "x")]
+
+    while len(down_hops) < depth:
+        down_hops.append(ring(at(down_hops[-1]), depth))
+    near_pair = last_pair(down_hops[:step])
+    near = last_swaps(near_pair)
     proj_scratch = [pltpu.VMEM((2, local, width // 2), BF16), dma((part_count,))]
-    partial = [shape_of((piece, width), F32), shape_of((piece, width), BF16)]
-    kept, sent = kernel_call(
+    kept, *sent = kernel_call(
         functools.partial(proj_kernel, depth, first_parts),
-        [where, attended, *first_arrays],
-        [SCALARS, WHOLE] + [ANYWHERE] * len(first_arrays),
+        [after(attended, *near_pair), *first_arrays],
+        [WHOLE] + [ANYWHERE] * len(first_arrays),
         partial,
         scratch=proj_scratch,
-        flops=2 * length * width * local,
-    )
-    middle, second_own = kernel_call(
-        middle_kernel,
-        [tokens_own, kept, swap(sent, "core"), bias_proj, gain_two, shift_two],
-        [WHOLE] * 6,
-        partial,
-    )
-    hidden_size = bias_up.shape[1]
-    up_scratch = [pltpu.VMEM((2, width, hidden_size // 2), BF16), dma((len(up_parts),))]
+    )
+    middle, *second_own = kernel_call(
+        middle_kernel, [tokens_own, kept, params, *swap_each(sent)], [WHOLE] * (3 + SHARES), partial
+    )
+    second_other = swap_each(second_own)
+    now = (*second_own, down_hops[-1])
+    far_pair = last_pair(down_hops[step:])
+    far = last_swaps(far_pair)
+    down_arrays = down_hops + near + far
+    up_scratch = [pltpu.VMEM((2, width, hidden_size // 2), BF16), dma((part_count,))]
     second, active, slope = kernel_call(
-        functools.partial(up_kernel, depth, up_parts),
-        [where, second_own, swap(second_own, "core"), bias_up, *up_arrays],
-        [SCALARS] + [WHOLE] * 3 + [ANYWHERE] * len(up_arrays),
+        functools.partial(up_kernel, depth, first_parts),
+        [after(bias_up, *far_pair), *second_own, *second_other, *up_arrays],
+        [WHOLE] * (1 + 2 * SHARES) + [ANYWHERE] * len(up_arrays),
         [shape_of((length, width), BF16)] + [shape_of((length, hidden_size), BF16)] * 2,
         scratch=up_scratch,
-        flops=2 * length * width * hidden_size,
-        exps=length * hidden_size,
-    )
-    sends = rows_grad(where, active, grad_full, depth, hidden_block, 1)
-    down_sum = Scatter(sends, "x", "y", depth)
-    down_scratch = [pltpu.VMEM((2, hidden_size, width // 2), BF16), dma((len(down_parts),))]
-    hidden_grad, up_sums = kernel_call(
-        functools.partial(hidden_kernel, depth, down_parts),
-        [where, grad_full, after(slope, *sends), *down_arrays],
-        [SCALARS] + [WHOLE] * 2 + [ANYWHERE] * len(down_arrays),
-        [shape_of((length, hidden_size), BF16), shape_of((8, hidden_size), F32)],
-        scratch=down_scratch,
-        flops=2 * length * width * hidden_size,
-    )
-    sends = columns_grad(where, second, hidden_grad, depth, up_rows, 1)
-    up_sum = Scatter(sends, "y", "x", depth)
-    down_sum.keeps = rows_grad(where, after(active, *sends), grad_full, depth, hidden_block, 0)
-    kept, sent = kernel_call(
-        functools.partial(up_back_kernel, depth, up_parts),
-        [where, after(hidden_grad, *down_sum.keeps), *up_arrays],
-        [SCALARS, WHOLE] + [ANYWHERE] * len(up_arrays),
-        partial,
-        scratch=up_scratch,
-        flops=2 * length * width * hidden_size,
-    )
-    up_sum.keeps = columns_grad(where, after(second, sent), hidden_grad, depth, up_rows, 0)
-    gate = down_sum.hop(0, up_sum.keeps[0])
-    middle_grad, branch_own, middle_sums = kernel_call(
-        middle_back_kernel,
-        [after(kept, gate), swap(sent, "core"), middle, grad_own, gain_two],
-        [WHOLE] * 5,
-        partial + [shape_of((8, width), F32)],
-    )
-    branch_other = swap(branch_own, "core")
-    (attended_grad,) = kernel_call(
+    )
+    (down_sends,) = merged_call(
+        rows_grad(active, grad_own, grad_other, depth, hidden_block, 1)
+    )
+    down_sum = Scatter(down_sends, "x", "y", depth)
+    now = (*down_sends, *far_pair)
+    down_sum.send()
+    down_sum.send()
+    down_scratch = [pltpu.VMEM((2, hidden_size, width // 2), BF16), dma((pair_count,))]
+    hidden_grad, up_sums, *up_sends = kernel_call(
+        functools.partial(hidden_kernel, depth, pair_parts, up_rows),
+        [grad_own, grad_other, at(slope), second, *down_arrays],
+        [ANYWHERE] * 2 + [WHOLE] + [ANYWHERE] * (1 + len(down_arrays)),
+        [shape_of((length, hidden_size), BF16), shape_of((8, hidden_size), F32)]
+        + [shape_of((len(group), 2, up_rows, hidden_size // 2), BF16) for group in near_first(depth)],
+        scratch=[
+            down_scratch[0],
+            pltpu.VMEM((length, width), BF16),
+            pltpu.VMEM((length, width), BF16),
+            down_scratch[1],
+            dma((2,)),
+            dma((2 * depth,)),
+        ],
+    )
+    up_sum = Scatter(up_sends, "y", "x", depth)
+    up_sum.send()
+    up_sum.send()
+    now = tuple(up_sends)
+    (kept, *sent), down_sum.keeps = merged_call(
+        (
+            functools.partial(up_back_kernel, depth, first_parts),
+            [at(hidden_grad), *up_arrays],
+            [WHOLE] + [ANYWHERE] * len(up_arrays),
+            partial,
+            up_scratch,
+        ),
+        rows_grad(active, grad_own, grad_other, depth, hidden_block, 0),
+    )
+    sent_other = swap_each(sent)
+    gate = down_sum.hop(0, down_sum.keeps[0])
+    (middle_grad, *branch_own, middle_sums), up_sum.keeps = merged_call(
+        (
+            middle_back_kernel,
+            [after(kept, gate), middle, grad_own, params, *sent_other],
+            [WHOLE] * (4 + SHARES),
+            partial + [shape_of((8, width), F32)],
+            [],
+        ),
+        columns_grad(second, hidden_grad, depth, up_rows, 0),
+    )
+    branch_other = swap_each(branch_own)
+    attended_grad, proj_blocks = kernel_call(
         functools.partial(proj_back_kernel, depth, first_parts),
-        [where, branch_own, branch_other, *first_arrays],
-        [SCALARS] + [WHOLE] * 2 + [ANYWHERE] * len(first_arrays),
-        [shape_of((length, local), BF16)],
-        scratch=proj_scratch,
-        flops=2 * length * width * local,
-    )
-    (proj_blocks,) = kernel_call(
-        functools.partial(proj_grad_kernel, depth),
-        [where, attended, after(branch_own, attended_grad), branch_other],
-        [SCALARS] + [WHOLE] * 3,
-        [shape_of((2, 2, depth, up_rows, width // 4), BF16)],
-        scratch=[pltpu.VMEM((local, width // 2), F32)],
-        flops=2 * length * width * local,
+        [after(attended, *up_sum.keeps), *branch_own, *branch_other, *first_arrays],
+        [WHOLE] + [ANYWHERE] * (2 * SHARES + len(first_arrays)),
+        [shape_of((length, local), BF16), shape_of((2, 2, depth, up_rows, width // 4), BF16)],
+        scratch=[
+            proj_scratch[0],
+            pltpu.VMEM((local, width // 2), F32),
+            pltpu.VMEM((length, width), BF16),
+            proj_scratch[1],
+            dma((2 * SHARES,)),
+        ],
     )
     pairs = local // (2 * head_size)
-    gate = down_sum.hop(1, proj_blocks)
-    first_grads = attend_back(
-        queries, keys, values, after(attended_grad, gate), logs, turn, head_size, 0, pairs // 2
-    )
-    gate = (down_sum.hop(2, first_grads[0]), up_sum.hop(0, first_grads[0]))
-    second_grads = attend_back(
-        queries, keys, values, after(attended_grad, *gate), logs, turn, head_size, pairs // 2, pairs
-    )
-    mixed_pieces = [group[n] for n in range(3) for group in (first_grads, second_grads)]
-    mixed_sums = jnp.concatenate([first_grads[3][:3], second_grads[3][:3]], axis=1)
-
-    def mixed_weight_grad(sent_number, gate):
-        block = (2, depth, up_rows, local)
-        return kernel_call(
+    groups = []
+
+    def attend_next(*gates):
+        k = len(groups)
+        grads = after(attended_grad, *gates)
+        groups.append(attend_back(queries, keys, values, grads, logs, turn, head_size, k, k + 1))
+        return groups[-1][0]
+
+    gate = attended_grad
+    while len(groups) < pairs - 3:
+        gate = attend_next(gate)
+    gate = attend_next(down_sum.hop(1, gate))
+    gate = attend_next(gate)
+    gate = attend_next(down_sum.hop(2, gate), up_sum.arrived[0])
+    mixed_pieces = [group[n] for n in range(3) for group in groups]
+
+    def mixed_weight_grad(sent_number, *gates):
+        block = (depth, up_rows, local)
+        return (
             functools.partial(mixed_grad_kernel, depth, sent_number),
-            [where, after(normed, gate), *mixed_pieces, proj_blocks],
-            [SCALARS] + [ANYWHERE] * (1 + len(mixed_pieces)) + [WHOLE],
-            [shape_of(block, BF16)] * 2,
-            scratch=[
+            [after(normed, *gates), *mixed_pieces, proj_blocks],
+            [ANYWHERE] * (1 + len(mixed_pieces)) + [WHOLE],
+            [shape_of(block, BF16)] * 4,
+            [
                 pltpu.VMEM((length, width), BF16),
                 pltpu.VMEM((length, 3 * local), BF16),
                 dma((2 * depth,)),
                 dma((len(mixed_pieces),)),
             ],
-            flops=length * width * 3 * local,
         )
 
-    one_send, two_send = mixed_weight_grad(1, second_grads[0])
-    one_near = swap(one_send, "y")
-    two_near = swap(two_send, "x")
-    gate = (up_sum.hop(1, two_send), down_sum.finish(two_send))
-    kept, sent = kernel_call(
-        functools.partial(mixed_back_kernel, depth, first_parts, len(mixed_pieces)),
-        [where, after(mixed_pieces[0], *gate), *mixed_pieces[1:], *first_arrays],
-        [SCALARS] + [WHOLE] * len(mixed_pieces) + [ANYWHERE] * len(first_arrays),
-        partial,
-        scratch=[pltpu.VMEM((2, width, 3 * local // 2), BF16), dma((part_count,))],
-        flops=2 * length * width * 3 * local,
-    )
-    sent_other = swap(sent, "core")
-    one_keep, two_keep = mixed_weight_grad(0, sent)
-    gate = up_sum.hop(2, two_keep)
-    tokens_grad, first_sums = kernel_call(
-        tokens_back_kernel,
-        [after(kept, gate), sent_other, tokens_own, middle_grad, gain_one],
-        [WHOLE] * 5,
-        [shape_of((piece, width), BF16), shape_of((8, width), F32)],
-    )
-    one_far = add_low(after(one_keep[1], tokens_grad), one_near[1])
-    two_far = add_low(after(two_keep[1], tokens_grad), two_near[1])
-    one_last = swap(one_far, "x")
-    two_last = swap(two_far, "y")
-    kept, sent = kernel_call(
-        functools.partial(down_kernel, depth, down_parts),
-        [where, after(active, one_far, two_far), *down_arrays],
-        [SCALARS, WHOLE] + [ANYWHERE] * len(down_arrays),
-        partial,
-        scratch=down_scratch,
-        flops=2 * length * width * hidden_size,
-    )
-    up_sum.finish(sent)
-    block_out = (middle + (kept + swap(sent, "core").astype(F32)) + bias_down).astype(BF16)
-    block_out = lax.ppermute(block_out, ("core", "y"), DIAGONAL)
-    tokens_grad = lax.ppermute(tokens_grad, ("core", "y"), DIAGONAL)
-    one = add_low(one_keep[0], one_near[0], one_last)
-    two = add_low(two_keep[0], two_near[0], two_last)
-    both = jnp.stack([one, two], axis=1)
-    moving = both[1 % depth]
-    for step in range(1, depth):
-        moving = add_low(both[(step + 1) % depth], ring(moving, depth))
-    grad_first = moving
-    grad_down = down_sum.result()
-    grad_up = up_sum.result()
-
-    def spread(vector, group):
-        parts = vector.reshape(-1, 1, group)
-        pair = jnp.arange(2).reshape(1, 2, 1) == core
-        return jnp.where(pair, parts, 0.0).reshape(-1)
-
-    vectors = [
-        first_sums[0],
-        first_sums[1],
-        middle_sums[0],
-        middle_sums[1],
-        middle_sums[2],
-        middle_sums[3],
-        spread(mixed_sums[:3].reshape(-1), head_size),
-        spread(up_sums[0], hidden_block),
+    ((one_far, one_near, two_far, two_near),) = merged_call(mixed_weight_grad(1, gate))
+    now = (one_far,)
+    fars = [swap(one_far, "y"), swap(two_far, "x")]
+    gate = up_sum.hop(0, *now, down_sum.moving)
+    (kept, *sent), keeps = merged_call(
+        (
+            functools.partial(mixed_back_kernel, depth, first_parts, len(mixed_pieces)),
+            [after(mixed_pieces[0], gate, up_sum.arrived[1]), *mixed_pieces[1:], *first_arrays],
+            [ANYWHERE] * (len(mixed_pieces) + len(first_arrays)),
+            partial,
+            [
+                pltpu.VMEM((2, width, 3 * local // 2), BF16),
+                pltpu.VMEM((length, 3 * local), BF16),
+                dma((part_count,)),
+                dma((len(mixed_pieces),)),
+            ],
+        ),
+        mixed_weight_grad(0),
+    )
+    sent_other = swap_each([after(item, *fars, up_sum.moving) for item in sent])
+    now = (keeps[0], *fars, up_sum.moving)
+    fars = [add_blocks([(at(keep_one), ()), (arrived, ())]) for keep_one, arrived in zip(keeps[::2], fars)]
+    lasts = [swap(fars[0], "x"), swap(fars[1], "y")]
+    nears = [swap(after(one_near, *fars), "y"), swap(after(two_near, *fars), "x")]
+    up_sum.hop(1, *now)
+    (tokens_grad, first_sums), (kept, *sent) = merged_call(
+        (
+            tokens_back_kernel,
+            [after(kept, *fars), tokens_own, middle_grad, params, *sent_other],
+            [WHOLE] * (4 + SHARES),
+            [shape_of((piece, width), BF16), shape_of((8, width), F32)],
+            [],
+        ),
+        (
+            functools.partial(down_kernel, depth, pair_parts),
+            [active, *down_arrays],
+            [WHOLE] + [ANYWHERE] * len(down_arrays),
+            partial,
+            down_scratch,
+        ),
+    )
+    now = (tokens_grad, *lasts, *nears, up_sum.moving)
+    keeps = keeps[1::2]
+    moving = None
+
+    def first_hop(n):
+        arrays, specs = first_terms(keeps, nears, lasts, n)
+        if moving is not None:
+            arrays.append(moving)
+            specs.append(same(block_kind.shape))
+        arrays[0] = at(arrays[0])
+        (total,) = kernel_call(
+            hop_first_kernel, arrays, specs, [block_kind], grid=(1,), out_specs=[same(block_kind.shape)]
+        )
+        return total, ring(total, depth)
+
+    sent_other = swap_each([at(item) for item in sent])
+    (small,) = kernel_call(
+        functools.partial(small_kernel, count, head_size, hidden_block, len(groups)),
+        [at(first_sums), middle_sums, up_sums] + [group[3] for group in groups],
+        [WHOLE] * (3 + len(groups)),
+        [shape_of((count, ROW), F32)],
+    )
+    for n in range(1, depth):
+        total, moving = first_hop(n)
+        if n == 1:
+            small = lax.all_to_all(after(small, total), everyone, split_axis=0, concat_axis=0, tiled=True)
+            (block_out,) = kernel_call(
+                out_kernel,
+                [middle, after(kept, total, small), params, *sent_other],
+                [WHOLE] * (3 + SHARES),
+                [shape_of((piece, width), BF16)],
+            )
+            now = (moving, block_out, small)
+        elif n == 2:
+            block_traded = trade(after(block_out, total))
+            tokens_traded = trade(after(tokens_grad, total))
+            up_sum.hop(2, total)
+            now = (moving, down_sum.finish(total), tokens_traded, block_traded)
+        else:
+            tokens_out = choose(tokens_grad, after(tokens_traded, total))
+            block_done = choose(block_out, after(block_traded, total))
+            now = (moving, up_sum.finish(total), tokens_out, block_done)
+    arrays, specs = first_terms(keeps, nears, lasts, 0)
+    arrays[0] = at(arrays[0])
+    out_shapes = [
+        shape_of((shard_rows, part_qkv), F32),
+        shape_of((shard_rows, part_qkv), BF16),
+        shape_of(proj_weight.shape, F32),
     ]
-    packed = jnp.concatenate([v.reshape(count, -1) for v in vectors], axis=1)
-    packed = jnp.pad(packed, ((0, 0), (0, 512 - packed.shape[1])))
-    packed = lax.all_to_all(packed, everyone, split_axis=0, concat_axis=0, tiled=True)
-    packed = jnp.sum(packed, axis=0)
-    pieces = []
-    spot = 0
-    for v in vectors:
-        size = v.shape[0] // count
-        pieces.append(packed[spot : spot + size])
-        spot += size
-
-    def joined(body, block):
-        rows = block.shape[0] // 2
-        pair = block.reshape(2, rows, -1)
-        (whole,) = kernel_call(
-            body,
-            [cores, taken(pair, core, 0), swap(taken(pair, 1 - core, 0), "core")],
-            [SCALARS, WHOLE, WHOLE],
-            [shape_of((rows, 2 * block.shape[1]), F32)],
-        )
-        return whole
-
-    grad_proj = grad_first[1][:, part_qkv - local :].astype(F32)
-    group = grad_proj.shape[0] // 2
-    grad_proj = jnp.concatenate([grad_proj[:group], grad_proj[group:]], axis=1)
-    grad_qkv = jnp.concatenate([grad_first[0], grad_first[1][:, : part_qkv - local]], axis=1)
-    grad_qkv = joined(join_heads_kernel, grad_qkv)
-    grad_up = joined(functools.partial(join_blocks_kernel, hidden_block), grad_up)
+    mine, sent, grad_proj = kernel_call(
+        finish_first_kernel,
+        arrays + [moving],
+        specs + [same(block_kind.shape)],
+        out_shapes,
+        grid=(1,),
+        out_specs=[same(kind.shape) for kind in out_shapes],
+        scratch=[pltpu.VMEM((2 * shard_rows, part_qkv), F32)],
+    )
+    (grad_qkv,) = kernel_call(
+        join_heads_kernel,
+        [mine, swap(sent, "core")],
+        [WHOLE] * 2,
+        [shape_of(qkv_weight.shape, F32)],
+    )
+    small = jnp.sum(small, axis=0)
+
+    def rest_of(scatter):
+        arrays, specs = [], []
+        for array, prefix in scatter.rest():
+            lead = tuple(prefix) + (0,) * (array.ndim - len(prefix) - 2)
+            arrays.append(array)
+            specs.append(
+                pl.BlockSpec((1,) * len(lead) + array.shape[-2:], lambda i, lead=lead: lead + (0, 0))
+            )
+        return arrays, specs
+
+    arrays, specs = rest_of(up_sum)
+    out_shapes = [shape_of((shard_rows, part_up), F32), shape_of((shard_rows, part_up), BF16)]
+    mine, sent = kernel_call(
+        finish_up_kernel,
+        arrays,
+        specs,
+        out_shapes,
+        grid=(1,),
+        out_specs=[same(kind.shape) for kind in out_shapes],
+        scratch=[pltpu.VMEM((2 * shard_rows, part_up), F32)],
+    )
+    (grad_up,) = kernel_call(
+        functools.partial(join_blocks_kernel, hidden_block),
+        [mine, swap(sent, "core")],
+        [WHOLE] * 2,
+        [shape_of(up_weight.shape, F32)],
+    )
+    arrays, specs = rest_of(down_sum)
+    (grad_down,) = kernel_call(
+        finish_down_kernel,
+        arrays,
+        specs,
+        [shape_of(down_weight.shape, F32)],
+        grid=(1,),
+        out_specs=[same(down_weight.shape)],
+    )
+
+    def part(begin, size):
+        return small[begin : begin + size]
+
     return (
-        block_out,
-        tokens_grad,
-        pieces[0],
-        pieces[1],
+        block_done,
+        tokens_out,
+        part(0, EACH),
+        part(EACH, EACH),
         grad_qkv,
-        pieces[6],
+        part(256, 3 * EACH),
         grad_proj,
-        pieces[4],
-        pieces[2],
-        pieces[3],
+        part(4 * EACH, EACH),
+        part(2 * EACH, EACH),
+        part(3 * EACH, EACH),
         grad_up,
-        pieces[7],
-        grad_down.astype(F32),
-        pieces[5],
+        part(384, 4 * EACH),
+        grad_down,
+        part(5 * EACH, EACH),
     )
 
 

time: 448 us -> 358 us (0.80)
  local copies, waits for them, and re-layouts: 70.4 us -> 24.6 us
  other arithmetic: 46.7 us -> 4.7 us
  starting transfers between devices: 82.5 us -> 69.8 us
  blocking collectives: 0 us -> 11.6 us
    unnamed x206 -> x185, local copies, waits for them, and re-layouts: 44.2 us -> 16.8 us
    convert_element_type x17 -> x0, other arithmetic: 25.6 us -> none  [the longest x14 21.7 us: add_low(): return total.astype(BF16)]
    all_to_all x0 -> x1, blocking collectives: none -> 11.6 us  [fast_shards(): lax.all_to_all(after(small, total), everyone, split_axis=0, concat_axis=0...]
    ppermute x38 -> x43, waiting for transfers between devices: 40.2 us -> 49.9 us  [swap(): return lax.ppermute(values, axis, SWAP)]
    concatenate x9 -> x0, other arithmetic: 9.56 us -> none  [the longest x2 4.43 us: gather_single(): group = jnp.concatenate(hops[begin:begin + step])]
    slice x20 -> x3, local copies, waits for them, and re-layouts: 9.88 us -> 1.62 us  [part(): return small[begin:begin + size]]
    another operation x7 -> x0, other arithmetic: 6.14 us -> none  [the longest x2 2.86 us: fast_shards(): both = jnp.stack([one, two], axis=1)]
    all_to_all x1, starting transfers between devices: 10.7 us -> 4.75 us  [fast_shards(): lax.all_to_all(small, everyone, split_axis=0, concat_axis=0, tiled=True)]
  transfers between devices with their start and end apart: 63 -> 67, of which waited for: 18 -> 25; matrix products, arithmetic and copies ran while one was open for 17% -> 4% of each run, Pallas kernels for 29% -> 35%
where the time goes in v2:
time: 358 us; the launch traced here: 351 us
  Pallas kernels  133 us (37%)
  waiting for transfers between devices  105 us (29%)
  starting transfers between devices  69.8 us (19%)
  local copies, waits for them, and re-layouts  24.6 us (7%)
  blocking collectives  11.6 us (3%)
  other arithmetic  4.7 us (1%)
    pallas_call x55, Pallas kernels, kernel_call(): pl.pallas_call(body, in_specs=in_specs, out_specs=out_specs, out_shape=ou...  133 us
    ppermute x43, waiting for transfers between devices, swap(): return lax.ppermute(values, axis, SWAP)  49.9 us
    ppermute x18, waiting for transfers between devices, ring(): lax.ppermute(values, 'z', [(i, (i + 1) % depth) for i in range(depth)])  49.1 us
    ppermute x43, starting transfers between devices, swap(): return lax.ppermute(values, axis, SWAP)  37.1 us
    unnamed x185, local copies, waits for them, and re-layouts  16.8 us
    ppermute x5, starting transfers between devices, trade(): return lax.ppermute(values, ('core', 'y'), DIAGONAL)  16.5 us
    all_to_all x1, blocking collectives, fast_shards(): lax.all_to_all(after(small, total), everyone, split_axis=0, concat_axis=0...  11.6 us
    ppermute x18, starting transfers between devices, ring(): lax.ppermute(values, 'z', [(i, (i + 1) % depth) for i in range(depth)])  11.4 us
  transfers between devices with their start and end apart: 67, of which 25 were waited for; matrix products, arithmetic and copies ran while one was open for 4% of the time, Pallas kernels for 35%

profile of v2, /device:TPU:1, one launch (start us, length us, event | category | flops | bytes accessed | tf_op | source)
XLA Modules:
  0.0 350.9 jit_solution(15777976481422017782)
XLA Ops:
  5.0 4.5 %collective-permute-start.4 = (bf16[512,1024]{1,0:T(8,128)(2,1)}, bf16[512,1024]{1,0:T(8,128)(2,1)S(1)}, u32[]{:S(2)}, u32[]{:S(2)}) collective-permute-start(bf16[512,1024]{1,0:T(8,128)(2,1)} %own_ref), channel_id=1, source_target_pairs={{1,2},{2,1},{5,6},{6,5},{9,10},{10,9},{13,14},{14,13},{17,18},{18,... | collective-permute-start | bytes 3145736 | tf_op jit(solution)/shard_map/ppermute | solution.py:574
  10.9 5.4 %concatenate.6 = bf16[512]{0:T(512)(128)(2,1)S(1)} concatenate(bf16[32]{0:T(256)(128)(2,1)} %param.21, bf16[32]{0:T(256)(128)(2,1)} %param.22, bf16[32]{0:T(256)(128)(2,1)} %param.27, bf16[32]{0:T(256)(128)(2,1)} %param.28, bf16[32]{0:T(256)(128)(2,1)} %param.26, bf16[32]{0:T(256)(128)(2,1)} %param.32, bf16[64]{0:T(256)(128)(2,1)S(1)} %broadcast_in_dim.102, bf16[96]{0:T(256)(128)(2,1)} %param.24, ...), dimensions={0} | concatenate | bytes 2048 | tf_op jit(solution)/shard_map/concatenate | solution.py:1529
  20.6 6.9 %collective-permute-done.3.refs_2_ = bf16[2,128,512]{2,1,0:T(8,128)(2,1)S(1)} collective-permute-done((bf16[2,128,512]{2,1,0:T(8,128)(2,1)S(1)}, bf16[2,128,512]{2,1,0:T(8,128)(2,1)S(1)}, u32[]{:S(2)}, u32[]{:S(2)}) %collective-permute-start.3) | collective-permute-done | bytes 262176 | tf_op jit(solution)/shard_map/ppermute | solution.py:514
  30.9 4.7 %all-to-all-start = ((f32[32,1,512]{2,1,0:T(1,128)}), f32[32,1,512]{2,1,0:T(1,128)S(1)}, u32[]{:S(2)}, u32[]{:S(2)}) async-start(f32[32,1,512]{2,1,0:T(1,128)} %broadcast_in_dim.104), calls=%async_computation | async-start | bytes 131072 | tf_op jit(solution)/shard_map/all_to_all | solution.py:1562
  55.5 4.6 %fusion = (f32[1024,128]{1,0:T(8,128)S(1)}, f32[1024,128]{1,0:T(8,128)S(1)}, f32[1024,128]{1,0:T(8,128)S(1)}) fusion(f32[128]{0:T(128)S(1)} %fusion.4, s32[1024]{0:T(1024)S(1)} %bitcast.47, s32[1024]{0:T(1024)S(1)} %bitcast.48, s32[1024]{0:T(1024)S(1)} %bitcast.46, pred[128]{0:T(512)(128)(4,1)S(1)} %get-tuple-element.330, ...), kind=kLoop, calls=%fused_computation.4 | loop fusion | flops 1179648 | bytes 1586176 | tf_op jit(solution)/shard_map/jit(_where)/select_n | solution.py:1473
  65.0 7.5 %collective-permute-done.17.rest_4_.rest_6_.refs_16_ = bf16[4,128,512]{2,1,0:T(8,128)(2,1)S(1)} collective-permute-done((bf16[4,128,512]{2,1,0:T(8,128)(2,1)S(1)}, bf16[4,128,512]{2,1,0:T(8,128)(2,1)S(1)}, u32[]{:S(2)}, u32[]{:S(2)}) %collective-permute-start.17) | collective-permute-done | bytes 524320 | tf_op jit(solution)/shard_map/ppermute | solution.py:500
  76.0 10.6 %collective-permute-done.21 = bf16[128,512]{1,0:T(8,128)(2,1)S(1)} collective-permute-done((bf16[128,512]{1,0:T(8,128)(2,1)S(1)}, bf16[128,512]{1,0:T(8,128)(2,1)S(1)}, u32[]{:S(2)}, u32[]{:S(2)}) %collective-permute-start.21) | collective-permute-done | bytes 131104 | tf_op jit(solution)/shard_map/ppermute | solution.py:500
  93.8 5.6 %shard_map.284 = (bf16[1024,1024]{1,0:T(8,128)(2,1)S(1)}, bf16[1024,512]{1,0:T(8,128)(2,1)S(1)}, bf16[1024,512]{1,0:T(8,128)(2,1)S(1)}, bf16[1024,512]{1,0:T(8,128)(2,1)S(1)}) custom-call(bf16[512,1024]{1,0:T(8,128)(2,1)S(1)} %shard_map.275.own_ref.refs_1_, bf16[512,1024]{1,0:T(8,128)(2,1)S(1)} %collective-permute-done.6.other_ref, ...), custom_call_target="tpu_custom_call" | custom-call | bytes 13146 | tf_op jit(solution)/shard_map/pallas_call | solution.py:453
  106.4 13.9 %shard_map.285 = (bf16[1024,512]{1,0:T(8,128)(2,1)S(1)}, f32[4,2,1024]{2,1,0:T(2,128)S(1)}) custom-call(bf16[1024,512]{1,0:T(8,128)(2,1)S(1)} %get-tuple-element.203.query_ref, bf16[1024,512]{1,0:T(8,128)(2,1)S(1)} %get-tuple-element.204.key_ref, bf16[1024,512]{1,0:T(8,128)(2,1)S(1)} %get-tuple-element.205.value_ref), custom_call_target="tpu_custom_call" | custom-call | flops 8589934 | bytes 4227 | tf_op jit(solution)/shard_map/pallas_call | solution.py:453
  120.3 4.7 %collective-permute-done.27.rest_8_.refs_7_ = bf16[4,128,512]{2,1,0:T(8,128)(2,1)S(1)} collective-permute-done((bf16[4,128,512]{2,1,0:T(8,128)(2,1)S(1)}, bf16[4,128,512]{2,1,0:T(8,128)(2,1)S(1)}, u32[]{:S(2)}, u32[]{:S(2)}) %collective-permute-start.27) | collective-permute-done | bytes 524320 | tf_op jit(solution)/shard_map/ppermute | solution.py:500
  138.1 11.3 %collective-permute-done.31.refs_1_.rest_3_.refs_9_ = bf16[4,128,512]{2,1,0:T(8,128)(2,1)S(1)} collective-permute-done((bf16[4,128,512]{2,1,0:T(8,128)(2,1)S(1)}, bf16[4,128,512]{2,1,0:T(8,128)(2,1)S(1)}, u32[]{:S(2)}, u32[]{:S(2)}) %collective-permute-start.31) | collective-permute-done | bytes 524320 | tf_op jit(solution)/shard_map/ppermute | solution.py:514
  152.3 8.1 %shard_map.292 = (bf16[1024,1024]{1,0:T(8,128)(2,1)S(1)}, bf16[1024,2048]{1,0:T(8,128)(2,1)S(1)}, bf16[1024,2048]{1,0:T(8,128)(2,1)S(1)}) custom-call(f32[1,2048]{1,0:T(1,128)S(1)} %get-tuple-element.219.bias_ref, bf16[512,1024]{1,0:T(8,128)(2,1)S(1)} %get-tuple-element.216.rest_0_, bf16[512,1024]{1,0:T(8,128)(2,1)S(1)} %collective-permute-done.32.rest_1_, ...), custom_call_target="tpu_custom_call" | custom-call | bytes 16785 | tf_op jit(solution)/shard_map/pallas_call | solution.py:453
  167.7 14.6 %shard_map.294 = (bf16[1024,2048]{1,0:T(8,128)(2,1)S(1)}, f32[8,2048]{1,0:T(8,128)S(1)}, bf16[2,2,128,1024]{3,2,1,0:T(8,128)(2,1)}, bf16[2,2,128,1024]{3,2,1,0:T(8,128)(2,1)S(1)}) custom-call(bf16[512,1024]{1,0:T(8,128)(2,1)S(1)} %shard_map.277.refs_1_.own_ref.refs_10_.refs_2_, bf16[512,1024]{1,0:T(8,128)(2,1)S(1)} %collective-permute-done.13.refs_2_.other_ref.refs_11_, ...), custom_call_target="tpu_custom_call" | custom-call | bytes 18939 | tf_op jit(solution)/shard_map/pallas_call | solution.py:453
  185.9 8.2 %shard_map.295 = (f32[512,1024]{1,0:T(8,128)S(1)}, bf16[512,1024]{1,0:T(8,128)(2,1)S(1)}, bf16[2,2,256,512]{3,2,1,0:T(8,128)(2,1)S(1)}, bf16[2,2,256,512]{3,2,1,0:T(8,128)(2,1)S(1)}) custom-call(bf16[1024,2048]{1,0:T(8,128)(2,1)S(1)} %get-tuple-element.233.refs_0_.refs_6_, bf16[4,128,512]{2,1,0:T(8,128)(2,1)S(1)} %shard_map.281.rest_2_.refs_1_, ...), custom_call_target="tpu_custom_call" | custom-call | bytes 19922 | tf_op jit(solution)/shard_map/pallas_call | solution.py:453
  198.4 5.1 %shard_map.297 = (f32[512,1024]{1,0:T(8,128)S(1)}, bf16[512,1024]{1,0:T(8,128)(2,1)S(1)}, f32[8,1024]{1,0:T(8,128)S(1)}, bf16[2,2,128,1024]{3,2,1,0:T(8,128)(2,1)S(1)}, bf16[2,2,128,1024]{3,2,1,0:T(8,128)(2,1)S(1)}) custom-call(f32[512,1024]{1,0:T(8,128)S(1)} %get-tuple-element.237.refs_0_, f32[512,1024]{1,0:T(8,128)S(1)} %copy-done.11, ...), custom_call_target="tpu_custom_call" | custom-call | bytes 17891 | tf_op jit(solution)/shard_map/pallas_call | solution.py:453
  209.5 6.2 %shard_map.299 = (bf16[1024,128]{1,0:T(8,128)(2,1)S(1)}, bf16[1024,128]{1,0:T(8,128)(2,1)S(1)}, bf16[1024,128]{1,0:T(8,128)(2,1)S(1)}, f32[8,128]{1,0:T(8,128)S(1)}) custom-call(bf16[1024,512]{1,0:T(8,128)(2,1)S(1)} %get-tuple-element.203.query_ref, bf16[1024,512]{1,0:T(8,128)(2,1)S(1)} %get-tuple-element.204.key_ref, ...), custom_call_target="tpu_custom_call" | custom-call | flops 5368709 | bytes 6590 | tf_op jit(solution)/shard_map/pallas_call | solution.py:453
  219.7 6.2 %shard_map.301 = (bf16[1024,128]{1,0:T(8,128)(2,1)S(1)}, bf16[1024,128]{1,0:T(8,128)(2,1)S(1)}, bf16[1024,128]{1,0:T(8,128)(2,1)S(1)}, f32[8,128]{1,0:T(8,128)S(1)}) custom-call(bf16[1024,512]{1,0:T(8,128)(2,1)S(1)} %get-tuple-element.203.query_ref, bf16[1024,512]{1,0:T(8,128)(2,1)S(1)} %get-tuple-element.204.key_ref, ...), custom_call_target="tpu_custom_call" | custom-call | flops 5368709 | bytes 6590 | tf_op jit(solution)/shard_map/pallas_call | solution.py:453
  225.9 6.4 %shard_map.302 = (bf16[1024,128]{1,0:T(8,128)(2,1)S(1)}, bf16[1024,128]{1,0:T(8,128)(2,1)S(1)}, bf16[1024,128]{1,0:T(8,128)(2,1)S(1)}, f32[8,128]{1,0:T(8,128)S(1)}) custom-call(bf16[1024,512]{1,0:T(8,128)(2,1)S(1)} %get-tuple-element.203.query_ref, bf16[1024,512]{1,0:T(8,128)(2,1)S(1)} %get-tuple-element.204.key_ref, ...), custom_call_target="tpu_custom_call" | custom-call | flops 5368709 | bytes 6590 | tf_op jit(solution)/shard_map/pallas_call | solution.py:453
  234.2 6.2 %shard_map.304 = (bf16[1024,128]{1,0:T(8,128)(2,1)S(1)}, bf16[1024,128]{1,0:T(8,128)(2,1)S(1)}, bf16[1024,128]{1,0:T(8,128)(2,1)S(1)}, f32[8,128]{1,0:T(8,128)S(1)}) custom-call(bf16[1024,512]{1,0:T(8,128)(2,1)S(1)} %get-tuple-element.203.query_ref, bf16[1024,512]{1,0:T(8,128)(2,1)S(1)} %get-tuple-element.204.key_ref, ...), custom_call_target="tpu_custom_call" | custom-call | flops 5368709 | bytes 6590 | tf_op jit(solution)/shard_map/pallas_call | solution.py:453
  252.2 8.0 %shard_map.307 = (f32[512,1024]{1,0:T(8,128)S(1)}, bf16[512,1024]{1,0:T(8,128)(2,1)S(1)}, bf16[4,128,512]{2,1,0:T(8,128)(2,1)S(1)}, bf16[4,128,512]{2,1,0:T(8,12...) custom-call(bf16[1024,128]{1,0:T(8,128)(2,1)S(1)} %get-tuple-element.268.refs_1_.refs_0_.refs_21_, ...), custom_call_target="tpu_custom_call" | custom-call | bytes 18874 | tf_op jit(solution)/shard_map/pallas_call | solution.py:453
  268.5 12.3 %shard_map.310 = (bf16[512,1024]{1,0:T(8,128)(2,1)S(1)}, f32[8,1024]{1,0:T(8,128)S(1)}, f32[512,1024]{1,0:T(8,128)S(1)}, bf16[512,1024]{1,0:T(8,128)(2,1)S(1)}) custom-call(f32[512,1024]{1,0:T(8,128)S(1)} %get-tuple-element.275.refs_0_, bf16[512,1024]{1,0:T(8,128)(2,1)S(1)} %shard_map.275.own_ref.refs_1_, f32[512,1024]{1,0:T(8,128)S(1)} %copy-done.54, ...), custom_call_target="tpu_custom_call" | custom-call | bytes 18939 | tf_op jit(solution)/shard_map/pallas_call | solution.py:453
  280.9 9.6 %collective-permute-done.52.refs_1_ = bf16[4,128,512]{2,1,0:T(8,128)(2,1)S(1)} collective-permute-done((bf16[4,128,512]{2,1,0:T(8,128)(2,1)S(1)}, bf16[4,128,512]{2,1,0:T(8,128)(2,1)S(1)}, u32[]{:S(2)}, u32[]{:S(2)}) %collective-permute-start.52) | collective-permute-done | bytes 524320 | tf_op jit(solution)/shard_map/ppermute | solution.py:500
  292.2 11.6 %all_to_all.21 = f32[32,1,512]{2,1,0:T(1,128)S(1)} all-to-all(f32[32,1,512]{2,1,0:T(1,128)S(1)} %copy.31), channel_id=1, replica_groups=mesh['z'=4,'x'=2,'core'=2,'y'=2] {'z','x','core','y'}, dimensions={0} | all-to-all | bytes 131072 | tf_op jit(solution)/shard_map/all_to_all | solution.py:1832
  311.7 16.8 %collective-permute-done.58.refs_6_ = bf16[2,128,512]{2,1,0:T(8,128)(2,1)S(1)} collective-permute-done((bf16[2,128,512]{2,1,0:T(8,128)(2,1)S(1)}, bf16[2,128,512]{2,1,0:T(8,128)(2,1)S(1)}, u32[]{:S(2)}, u32[]{:S(2)}) %collective-permute-start.58) | collective-permute-done | bytes 262176 | tf_op jit(solution)/shard_map/ppermute | solution.py:514
  (368 shorter events, 149.3 us)
Async XLA Ops:
  5.0 22.5 %collective-permute-start.4 = (bf16[512,1024]{1,0:T(8,128)(2,1)}, bf16[512,1024]{1,0:T(8,128)(2,1)S(1)}, u32[]{:S(2)}, u32[]{:S(2)}) collective-permute-start(bf16[512,1024]{1,0:T(8,128)(2,1)} %own_ref), channel_id=1, source_target_pairs={{1,2},{2,1},{5,6},{6,5},{9,10},{10,9},{13,14},{14,13},{17,18},{18,... | collective-permute-start | bytes 3145736 | tf_op jit(solution)/shard_map/ppermute | solution.py:574
  17.7 25.0 %collective-permute-start.9 = (bf16[512,1024]{1,0:T(8,128)(2,1)}, bf16[512,1024]{1,0:T(8,128)(2,1)}, u32[]{:S(2)}, u32[]{:S(2)}) collective-permute-start(bf16[512,1024]{1,0:T(8,128)(2,1)} %own_ref.1), channel_id=1, source_target_pairs={{1,2},{2,1},{5,6},{6,5},{9,10},{10,9},{13,14},{14,13},{17,18},{18,... | collective-permute-start | bytes 3145736 | tf_op jit(solution)/shard_map/ppermute | solution.py:574
  50.3 22.3 %collective-permute-start.17 = (bf16[4,128,512]{2,1,0:T(8,128)(2,1)S(1)}, bf16[4,128,512]{2,1,0:T(8,128)(2,1)S(1)}, u32[]{:S(2)}, u32[]{:S(2)}) collective-permute-start(bf16[4,128,512]{2,1,0:T(8,128)(2,1)S(1)} %shard_map.278.rest_0_.rest_2_.refs_12_), channel_id=1, source_target_pairs={{0,1},{1,0},{2,3},{3,2},{4,5},{5,4},{6,7},{7,6},{8,9},{9,8},{10,11... | collective-permute-start | bytes 1572872 | tf_op jit(solution)/shard_map/ppermute | solution.py:500
  62.5 24.1 %collective-permute-start.14 = (bf16[4,128,512]{2,1,0:T(8,128)(2,1)S(1)}, bf16[4,128,512]{2,1,0:T(8,128)(2,1)S(1)}, u32[]{:S(2)}, u32[]{:S(2)}) collective-permute-start(bf16[4,128,512]{2,1,0:T(8,128)(2,1)S(1)} %collective-permute-done.10.rest_2_.rest_4_.refs_14_), channel_id=1, source_target_pairs={{0,1},{1,0},{2,3},{3,2},{4,5},{5,4},{6,7},{7,6},{8,9},{9,8},{10,11... | collective-permute-start | bytes 1572872 | tf_op jit(solution)/shard_map/ppermute | solution.py:500
  64.4 22.3 %collective-permute-start.15 = (bf16[4,128,512]{2,1,0:T(8,128)(2,1)S(1)}, bf16[4,128,512]{2,1,0:T(8,128)(2,1)S(1)}, u32[]{:S(2)}, u32[]{:S(2)}) collective-permute-start(bf16[4,128,512]{2,1,0:T(8,128)(2,1)S(1)} %collective-permute-done.11.rest_3_.rest_5_.refs_15_), channel_id=1, source_target_pairs={{0,4},{4,0},{1,5},{5,1},{2,6},{6,2},{3,7},{7,3},{8,12},{12,8},{9,1... | collective-permute-start | bytes 1572872 | tf_op jit(solution)/shard_map/ppermute | solution.py:500
  92.5 27.7 %collective-permute-start.25 = (bf16[4,128,512]{2,1,0:T(8,128)(2,1)S(1)}, bf16[4,128,512]{2,1,0:T(8,128)(2,1)S(1)}, u32[]{:S(2)}, u32[]{:S(2)}) collective-permute-start(bf16[4,128,512]{2,1,0:T(8,128)(2,1)S(1)} %shard_map.281.rest_2_.refs_1_), channel_id=1, source_target_pairs={{0,1},{1,0},{2,3},{3,2},{4,5},{5,4},{6,7},{7,6},{8,9},{9,8},{10,11... | collective-permute-start | bytes 1572872 | tf_op jit(solution)/shard_map/ppermute | solution.py:500
  92.6 27.7 %collective-permute-start.26 = (bf16[4,128,512]{2,1,0:T(8,128)(2,1)S(1)}, bf16[4,128,512]{2,1,0:T(8,128)(2,1)S(1)}, u32[]{:S(2)}, u32[]{:S(2)}) collective-permute-start(bf16[4,128,512]{2,1,0:T(8,128)(2,1)S(1)} %shard_map.282.rest_3_.refs_2_), channel_id=1, source_target_pairs={{0,4},{4,0},{1,5},{5,1},{2,6},{6,2},{3,7},{7,3},{8,12},{12,8},{9,1... | collective-permute-start | bytes 1572872 | tf_op jit(solution)/shard_map/ppermute | solution.py:500
  102.5 22.5 %collective-permute-start.27 = (bf16[4,128,512]{2,1,0:T(8,128)(2,1)S(1)}, bf16[4,128,512]{2,1,0:T(8,128)(2,1)S(1)}, u32[]{:S(2)}, u32[]{:S(2)}) collective-permute-start(bf16[4,128,512]{2,1,0:T(8,128)(2,1)S(1)} %collective-permute-done.22.rest_4_.refs_3_), channel_id=1, source_target_pairs={{0,1},{1,0},{2,3},{3,2},{4,5},{5,4},{6,7},{7,6},{8,9},{9,8},{10,11... | collective-permute-start | bytes 1572872 | tf_op jit(solution)/shard_map/ppermute | solution.py:500
  104.0 21.0 %collective-permute-start.28 = (bf16[4,128,512]{2,1,0:T(8,128)(2,1)S(1)}, bf16[4,128,512]{2,1,0:T(8,128)(2,1)S(1)}, u32[]{:S(2)}, u32[]{:S(2)}) collective-permute-start(bf16[4,128,512]{2,1,0:T(8,128)(2,1)S(1)} %collective-permute-done.23.rest_5_.refs_4_), channel_id=1, source_target_pairs={{0,4},{4,0},{1,5},{5,1},{2,6},{6,2},{3,7},{7,3},{8,12},{12,8},{9,1... | collective-permute-start | bytes 1572872 | tf_op jit(solution)/shard_map/ppermute | solution.py:500
  105.2 19.8 %collective-permute-start.29 = (bf16[4,128,512]{2,1,0:T(8,128)(2,1)S(1)}, bf16[4,128,512]{2,1,0:T(8,128)(2,1)S(1)}, u32[]{:S(2)}, u32[]{:S(2)}) collective-permute-start(bf16[4,128,512]{2,1,0:T(8,128)(2,1)S(1)} %collective-permute-done.24.refs_1_.rest_1_.refs_7_), channel_id=1, source_target_pairs={{0,8},{8,16},{16,24},{24,0},{1,9},{9,17},{17,25},{25,1},{2,10},{10... | collective-permute-start | bytes 1572872 | tf_op jit(solution)/shard_map/ppermute | solution.py:514
  135.5 29.3 %collective-permute-start.33 = (bf16[4,128,512]{2,1,0:T(8,128)(2,1)S(1)}, bf16[4,128,512]{2,1,0:T(8,128)(2,1)S(1)}, u32[]{:S(2)}, u32[]{:S(2)}) collective-permute-start(bf16[4,128,512]{2,1,0:T(8,128)(2,1)S(1)} %shard_map.286), channel_id=1, source_target_pairs={{0,1},{1,0},{2,3},{3,2},{4,5},{5,4},{6,7},{7,6},{8,9},{9,8},{10,11... | collective-permute-start | bytes 1572872 | tf_op jit(solution)/shard_map/ppermute | solution.py:500
  136.9 27.8 %collective-permute-start.34 = (bf16[4,128,512]{2,1,0:T(8,128)(2,1)S(1)}, bf16[4,128,512]{2,1,0:T(8,128)(2,1)S(1)}, u32[]{:S(2)}, u32[]{:S(2)}) collective-permute-start(bf16[4,128,512]{2,1,0:T(8,128)(2,1)S(1)} %shard_map.287), channel_id=1, source_target_pairs={{0,4},{4,0},{1,5},{5,1},{2,6},{6,2},{3,7},{7,3},{8,12},{12,8},{9,1... | collective-permute-start | bytes 1572872 | tf_op jit(solution)/shard_map/ppermute | solution.py:500
  164.4 31.6 %collective-permute-start.37 = (bf16[2,2,256,512]{3,2,1,0:T(8,128)(2,1)}, bf16[2,2,256,512]{3,2,1,0:T(8,128)(2,1)S(1)}, u32[]{:S(2)}, u32[]{:S(2)}) collective-permute-start(bf16[2,2,256,512]{3,2,1,0:T(8,128)(2,1)} %get-tuple-element.222), channel_id=1, source_target_pairs={{0,4},{4,0},{1,5},{5,1},{2,6},{6,2},{3,7},{7,3},{8,12},{12,8},{9,1... | collective-permute-start | bytes 3145736 | tf_op jit(solution)/shard_map/ppermute | solution.py:500
  204.0 28.4 %collective-permute-start.41 = (bf16[2,2,256,512]{3,2,1,0:T(8,128)(2,1)}, bf16[2,2,256,512]{3,2,1,0:T(8,128)(2,1)S(1)}, u32[]{:S(2)}, u32[]{:S(2)}) collective-permute-start(bf16[2,2,256,512]{3,2,1,0:T(8,128)(2,1)} %get-tuple-element.223), channel_id=1, source_target_pairs={{0,4},{4,0},{1,5},{5,1},{2,6},{6,2},{3,7},{7,3},{8,12},{12,8},{9,1... | collective-permute-start | bytes 3145736 | tf_op jit(solution)/shard_map/ppermute | solution.py:500
  205.2 29.0 %collective-permute-start.43 = (bf16[2,2,128,1024]{3,2,1,0:T(8,128)(2,1)}, bf16[2,2,128,1024]{3,2,1,0:T(8,128)(2,1)S(1)}, u32[]{:S(2)}, u32[]{:S(2)}) collective-permute-start(bf16[2,2,128,1024]{3,2,1,0:T(8,128)(2,1)} %get-tuple-element.231), channel_id=1, source_target_pairs={{0,1},{1,0},{2,3},{3,2},{4,5},{5,4},{6,7},{7,6},{8,9},{9,8},{10,11... | collective-permute-start | bytes 3145736 | tf_op jit(solution)/shard_map/ppermute | solution.py:500
  219.6 32.5 %collective-permute-start.45 = (bf16[2,2,128,1024]{3,2,1,0:T(8,128)(2,1)S(1)}, bf16[2,2,128,1024]{3,2,1,0:T(8,128)(2,1)S(1)}, u32[]{:S(2)}, u32[]{:S(2)}) collective-permute-start(bf16[2,2,128,1024]{3,2,1,0:T(8,128)(2,1)S(1)} %copy-done.88), channel_id=1, source_target_pairs={{0,1},{1,0},{2,3},{3,2},{4,5},{5,4},{6,7},{7,6},{8,9},{9,8},{10,11... | collective-permute-start | bytes 3145736 | tf_op jit(solution)/shard_map/ppermute | solution.py:500
  264.9 25.6 %collective-permute-start.50 = (bf16[4,128,512]{2,1,0:T(8,128)(2,1)S(1)}, bf16[4,128,512]{2,1,0:T(8,128)(2,1)S(1)}, u32[]{:S(2)}, u32[]{:S(2)}) collective-permute-start(bf16[4,128,512]{2,1,0:T(8,128)(2,1)S(1)} %shard_map.308), channel_id=1, source_target_pairs={{0,4},{4,0},{1,5},{5,1},{2,6},{6,2},{3,7},{7,3},{8,12},{12,8},{9,1... | collective-permute-start | bytes 1572872 | tf_op jit(solution)/shard_map/ppermute | solution.py:500
  266.0 24.6 %collective-permute-start.51 = (bf16[4,128,512]{2,1,0:T(8,128)(2,1)S(1)}, bf16[4,128,512]{2,1,0:T(8,128)(2,1)S(1)}, u32[]{:S(2)}, u32[]{:S(2)}) collective-permute-start(bf16[4,128,512]{2,1,0:T(8,128)(2,1)S(1)} %shard_map.309), channel_id=1, source_target_pairs={{0,1},{1,0},{2,3},{3,2},{4,5},{5,4},{6,7},{7,6},{8,9},{9,8},{10,11... | collective-permute-start | bytes 1572872 | tf_op jit(solution)/shard_map/ppermute | solution.py:500
  266.1 24.5 %collective-permute-start.52 = (bf16[4,128,512]{2,1,0:T(8,128)(2,1)S(1)}, bf16[4,128,512]{2,1,0:T(8,128)(2,1)S(1)}, u32[]{:S(2)}, u32[]{:S(2)}) collective-permute-start(bf16[4,128,512]{2,1,0:T(8,128)(2,1)S(1)} %get-tuple-element.283), channel_id=1, source_target_pairs={{0,1},{1,0},{2,3},{3,2},{4,5},{5,4},{6,7},{7,6},{8,9},{9,8},{10,11... | collective-permute-start | bytes 1572872 | tf_op jit(solution)/shard_map/ppermute | solution.py:500
  267.5 23.0 %collective-permute-start.53 = (bf16[4,128,512]{2,1,0:T(8,128)(2,1)S(1)}, bf16[4,128,512]{2,1,0:T(8,128)(2,1)S(1)}, u32[]{:S(2)}, u32[]{:S(2)}) collective-permute-start(bf16[4,128,512]{2,1,0:T(8,128)(2,1)S(1)} %get-tuple-element.285), channel_id=1, source_target_pairs={{0,4},{4,0},{1,5},{5,1},{2,6},{6,2},{3,7},{7,3},{8,12},{12,8},{9,1... | collective-permute-start | bytes 1572872 | tf_op jit(solution)/shard_map/ppermute | solution.py:500
  268.4 22.2 %collective-permute-start.54 = (bf16[2,128,1024]{2,1,0:T(8,128)(2,1)S(1)}, bf16[2,128,1024]{2,1,0:T(8,128)(2,1)S(1)}, u32[]{:S(2)}, u32[]{:S(2)}) collective-permute-start(bf16[2,128,1024]{2,1,0:T(8,128)(2,1)S(1)} %shard_map.311), channel_id=1, source_target_pairs={{0,8},{8,16},{16,24},{24,0},{1,9},{9,17},{17,25},{25,1},{2,10},{10... | collective-permute-start | bytes 1572872 | tf_op jit(solution)/shard_map/ppermute | solution.py:514
  304.3 24.1 %collective-permute-start.57 = (bf16[512,1024]{1,0:T(8,128)(2,1)S(1)}, bf16[512,1024]{1,0:T(8,128)(2,1)S(1)}, u32[]{:S(2)}, u32[]{:S(2)}) collective-permute-start(bf16[512,1024]{1,0:T(8,128)(2,1)S(1)} %shard_map.314.own_ref), channel_id=1, source_target_pairs={{1,2},{2,1},{5,6},{6,5},{9,10},{10,9},{13,14},{14,13},{17,18},{18,... | collective-permute-start | bytes 3145736 | tf_op jit(solution)/shard_map/ppermute | solution.py:574
  307.6 24.5 %collective-permute-start.59 = (bf16[512,1024]{1,0:T(8,128)(2,1)S(1)}, bf16[512,1024]{1,0:T(8,128)(2,1)S(1)}, u32[]{:S(2)}, u32[]{:S(2)}) collective-permute-start(bf16[512,1024]{1,0:T(8,128)(2,1)S(1)} %get-tuple-element.304.own_ref), channel_id=1, source_target_pairs={{1,2},{2,1},{5,6},{6,5},{9,10},{10,9},{13,14},{14,13},{17,18},{18,... | collective-permute-start | bytes 3145736 | tf_op jit(solution)/shard_map/ppermute | solution.py:574
  310.1 22.1 %collective-permute-start.61 = (bf16[2,128,1024]{2,1,0:T(8,128)(2,1)S(1)}, bf16[2,128,1024]{2,1,0:T(8,128)(2,1)S(1)}, u32[]{:S(2)}, u32[]{:S(2)}) collective-permute-start(bf16[2,128,1024]{2,1,0:T(8,128)(2,1)S(1)} %shard_map.320), channel_id=1, source_target_pairs={{0,8},{8,16},{16,24},{24,0},{1,9},{9,17},{17,25},{25,1},{2,10},{10... | collective-permute-start | bytes 1572872 | tf_op jit(solution)/shard_map/ppermute | solution.py:514
  (135 other events, 2208.5 us)

commit v3 on v2

--- a/solution.py
+++ b/solution.py
@@ -834,7 +834,7 @@
     out_spec = pl.BlockSpec((length, wide), lambda i: (0, i))
     whole = pl.BlockSpec((length, wide), lambda i: (0, 0))
     return kernel_call(
-        functools.partial(attend_back_kernel, block=512, scale=head_size**-0.5),
+        functools.partial(attend_back_kernel, block=1024, scale=head_size**-0.5),
         [queries, keys, values, grads, logs, *turn],
         [spec] * 4 + [pl.BlockSpec((1, 2, length), lambda i: (begin + i, 0, 0))] + [whole] * 3,
         [shape_of((length, width), BF16)] * 3 + [shape_of((8, width), F32)],

time: 358 us -> 358 us (level)
  no operation moved by 1% of the time
where the time goes in v3:
time: 358 us; the launch traced here: 351 us
  Pallas kernels  134 us (37%)
  waiting for transfers between devices  104 us (29%)
  starting transfers between devices  70 us (20%)
  local copies, waits for them, and re-layouts  24.6 us (7%)
  blocking collectives  11.6 us (3%)
  other arithmetic  4.7 us (1%)
    pallas_call x55, Pallas kernels, kernel_call(): pl.pallas_call(body, in_specs=in_specs, out_specs=out_specs, out_shape=ou...  134 us
    ppermute x43, waiting for transfers between devices, swap(): return lax.ppermute(values, axis, SWAP)  49.9 us
    ppermute x18, waiting for transfers between devices, ring(): lax.ppermute(values, 'z', [(i, (i + 1) % depth) for i in range(depth)])  48.2 us
    ppermute x43, starting transfers between devices, swap(): return lax.ppermute(values, axis, SWAP)  37.6 us
    unnamed x185, local copies, waits for them, and re-layouts  16.8 us
    ppermute x5, starting transfers between devices, trade(): return lax.ppermute(values, ('core', 'y'), DIAGONAL)  16.5 us
    all_to_all x1, blocking collectives, fast_shards(): lax.all_to_all(after(small, total), everyone, split_axis=0, concat_axis=0...  11.6 us
    ppermute x18, starting transfers between devices, ring(): lax.ppermute(values, 'z', [(i, (i + 1) % depth) for i in range(depth)])  11.2 us
  transfers between devices with their start and end apart: 67, of which 25 were waited for; matrix products, arithmetic and copies ran while one was open for 4% of the time, Pallas kernels for 35%

profile of v3, /device:TPU:1, one launch (start us, length us, event | category | flops | bytes accessed | tf_op | source)
XLA Modules:
  0.0 350.9 jit_solution(11535159928127810744)
XLA Ops:
  5.0 4.5 %collective-permute-start.4 = (bf16[512,1024]{1,0:T(8,128)(2,1)}, bf16[512,1024]{1,0:T(8,128)(2,1)S(1)}, u32[]{:S(2)}, u32[]{:S(2)}) collective-permute-start(bf16[512,1024]{1,0:T(8,128)(2,1)} %own_ref), channel_id=1, source_target_pairs={{1,2},{2,1},{5,6},{6,5},{9,10},{10,9},{13,14},{14,13},{17,18},{18,... | collective-permute-start | bytes 3145736 | tf_op jit(solution)/shard_map/ppermute | solution.py:574
  10.9 5.4 %concatenate.6 = bf16[512]{0:T(512)(128)(2,1)S(1)} concatenate(bf16[32]{0:T(256)(128)(2,1)} %param.21, bf16[32]{0:T(256)(128)(2,1)} %param.22, bf16[32]{0:T(256)(128)(2,1)} %param.27, bf16[32]{0:T(256)(128)(2,1)} %param.28, bf16[32]{0:T(256)(128)(2,1)} %param.26, bf16[32]{0:T(256)(128)(2,1)} %param.32, bf16[64]{0:T(256)(128)(2,1)S(1)} %broadcast_in_dim.102, bf16[96]{0:T(256)(128)(2,1)} %param.24, ...), dimensions={0} | concatenate | bytes 2048 | tf_op jit(solution)/shard_map/concatenate | solution.py:1529
  20.6 6.9 %collective-permute-done.3.refs_2_ = bf16[2,128,512]{2,1,0:T(8,128)(2,1)S(1)} collective-permute-done((bf16[2,128,512]{2,1,0:T(8,128)(2,1)S(1)}, bf16[2,128,512]{2,1,0:T(8,128)(2,1)S(1)}, u32[]{:S(2)}, u32[]{:S(2)}) %collective-permute-start.3) | collective-permute-done | bytes 262176 | tf_op jit(solution)/shard_map/ppermute | solution.py:514
  30.9 4.7 %all-to-all-start = ((f32[32,1,512]{2,1,0:T(1,128)}), f32[32,1,512]{2,1,0:T(1,128)S(1)}, u32[]{:S(2)}, u32[]{:S(2)}) async-start(f32[32,1,512]{2,1,0:T(1,128)} %broadcast_in_dim.104), calls=%async_computation | async-start | bytes 131072 | tf_op jit(solution)/shard_map/all_to_all | solution.py:1562
  55.5 4.6 %fusion = (f32[1024,128]{1,0:T(8,128)S(1)}, f32[1024,128]{1,0:T(8,128)S(1)}, f32[1024,128]{1,0:T(8,128)S(1)}) fusion(f32[128]{0:T(128)S(1)} %fusion.4, s32[1024]{0:T(1024)S(1)} %bitcast.47, s32[1024]{0:T(1024)S(1)} %bitcast.48, s32[1024]{0:T(1024)S(1)} %bitcast.46, pred[128]{0:T(512)(128)(4,1)S(1)} %get-tuple-element.330, ...), kind=kLoop, calls=%fused_computation.4 | loop fusion | flops 1179648 | bytes 1586176 | tf_op jit(solution)/shard_map/jit(_where)/select_n | solution.py:1473
  65.0 7.5 %collective-permute-done.17.rest_4_.rest_6_.refs_16_ = bf16[4,128,512]{2,1,0:T(8,128)(2,1)S(1)} collective-permute-done((bf16[4,128,512]{2,1,0:T(8,128)(2,1)S(1)}, bf16[4,128,512]{2,1,0:T(8,128)(2,1)S(1)}, u32[]{:S(2)}, u32[]{:S(2)}) %collective-permute-start.17) | collective-permute-done | bytes 524320 | tf_op jit(solution)/shard_map/ppermute | solution.py:500
  76.0 10.6 %collective-permute-done.21 = bf16[128,512]{1,0:T(8,128)(2,1)S(1)} collective-permute-done((bf16[128,512]{1,0:T(8,128)(2,1)S(1)}, bf16[128,512]{1,0:T(8,128)(2,1)S(1)}, u32[]{:S(2)}, u32[]{:S(2)}) %collective-permute-start.21) | collective-permute-done | bytes 131104 | tf_op jit(solution)/shard_map/ppermute | solution.py:500
  93.8 5.6 %shard_map.284 = (bf16[1024,1024]{1,0:T(8,128)(2,1)S(1)}, bf16[1024,512]{1,0:T(8,128)(2,1)S(1)}, bf16[1024,512]{1,0:T(8,128)(2,1)S(1)}, bf16[1024,512]{1,0:T(8,128)(2,1)S(1)}) custom-call(bf16[512,1024]{1,0:T(8,128)(2,1)S(1)} %shard_map.275.own_ref.refs_1_, bf16[512,1024]{1,0:T(8,128)(2,1)S(1)} %collective-permute-done.6.other_ref, ...), custom_call_target="tpu_custom_call" | custom-call | bytes 13146 | tf_op jit(solution)/shard_map/pallas_call | solution.py:453
  106.4 13.9 %shard_map.285 = (bf16[1024,512]{1,0:T(8,128)(2,1)S(1)}, f32[4,2,1024]{2,1,0:T(2,128)S(1)}) custom-call(bf16[1024,512]{1,0:T(8,128)(2,1)S(1)} %get-tuple-element.203.query_ref, bf16[1024,512]{1,0:T(8,128)(2,1)S(1)} %get-tuple-element.204.key_ref, bf16[1024,512]{1,0:T(8,128)(2,1)S(1)} %get-tuple-element.205.value_ref), custom_call_target="tpu_custom_call" | custom-call | flops 8589934 | bytes 4227 | tf_op jit(solution)/shard_map/pallas_call | solution.py:453
  120.3 4.7 %collective-permute-done.27.rest_8_.refs_7_ = bf16[4,128,512]{2,1,0:T(8,128)(2,1)S(1)} collective-permute-done((bf16[4,128,512]{2,1,0:T(8,128)(2,1)S(1)}, bf16[4,128,512]{2,1,0:T(8,128)(2,1)S(1)}, u32[]{:S(2)}, u32[]{:S(2)}) %collective-permute-start.27) | collective-permute-done | bytes 524320 | tf_op jit(solution)/shard_map/ppermute | solution.py:500
  138.1 11.3 %collective-permute-done.31.refs_1_.rest_3_.refs_9_ = bf16[4,128,512]{2,1,0:T(8,128)(2,1)S(1)} collective-permute-done((bf16[4,128,512]{2,1,0:T(8,128)(2,1)S(1)}, bf16[4,128,512]{2,1,0:T(8,128)(2,1)S(1)}, u32[]{:S(2)}, u32[]{:S(2)}) %collective-permute-start.31) | collective-permute-done | bytes 524320 | tf_op jit(solution)/shard_map/ppermute | solution.py:514
  152.3 8.1 %shard_map.292 = (bf16[1024,1024]{1,0:T(8,128)(2,1)S(1)}, bf16[1024,2048]{1,0:T(8,128)(2,1)S(1)}, bf16[1024,2048]{1,0:T(8,128)(2,1)S(1)}) custom-call(f32[1,2048]{1,0:T(1,128)S(1)} %get-tuple-element.219.bias_ref, bf16[512,1024]{1,0:T(8,128)(2,1)S(1)} %get-tuple-element.216.rest_0_, bf16[512,1024]{1,0:T(8,128)(2,1)S(1)} %collective-permute-done.32.rest_1_, ...), custom_call_target="tpu_custom_call" | custom-call | bytes 16785 | tf_op jit(solution)/shard_map/pallas_call | solution.py:453
  167.7 14.6 %shard_map.294 = (bf16[1024,2048]{1,0:T(8,128)(2,1)S(1)}, f32[8,2048]{1,0:T(8,128)S(1)}, bf16[2,2,128,1024]{3,2,1,0:T(8,128)(2,1)}, bf16[2,2,128,1024]{3,2,1,0:T(8,128)(2,1)S(1)}) custom-call(bf16[512,1024]{1,0:T(8,128)(2,1)S(1)} %shard_map.277.refs_1_.own_ref.refs_10_.refs_2_, bf16[512,1024]{1,0:T(8,128)(2,1)S(1)} %collective-permute-done.13.refs_2_.other_ref.refs_11_, ...), custom_call_target="tpu_custom_call" | custom-call | bytes 18939 | tf_op jit(solution)/shard_map/pallas_call | solution.py:453
  185.9 8.2 %shard_map.295 = (f32[512,1024]{1,0:T(8,128)S(1)}, bf16[512,1024]{1,0:T(8,128)(2,1)S(1)}, bf16[2,2,256,512]{3,2,1,0:T(8,128)(2,1)S(1)}, bf16[2,2,256,512]{3,2,1,0:T(8,128)(2,1)S(1)}) custom-call(bf16[1024,2048]{1,0:T(8,128)(2,1)S(1)} %get-tuple-element.233.refs_0_.refs_6_, bf16[4,128,512]{2,1,0:T(8,128)(2,1)S(1)} %shard_map.281.rest_2_.refs_1_, ...), custom_call_target="tpu_custom_call" | custom-call | bytes 19922 | tf_op jit(solution)/shard_map/pallas_call | solution.py:453
  198.4 5.1 %shard_map.297 = (f32[512,1024]{1,0:T(8,128)S(1)}, bf16[512,1024]{1,0:T(8,128)(2,1)S(1)}, f32[8,1024]{1,0:T(8,128)S(1)}, bf16[2,2,128,1024]{3,2,1,0:T(8,128)(2,1)S(1)}, bf16[2,2,128,1024]{3,2,1,0:T(8,128)(2,1)S(1)}) custom-call(f32[512,1024]{1,0:T(8,128)S(1)} %get-tuple-element.237.refs_0_, f32[512,1024]{1,0:T(8,128)S(1)} %copy-done.11, ...), custom_call_target="tpu_custom_call" | custom-call | bytes 17891 | tf_op jit(solution)/shard_map/pallas_call | solution.py:453
  209.5 6.4 %shard_map.299 = (bf16[1024,128]{1,0:T(8,128)(2,1)S(1)}, bf16[1024,128]{1,0:T(8,128)(2,1)S(1)}, bf16[1024,128]{1,0:T(8,128)(2,1)S(1)}, f32[8,128]{1,0:T(8,128)S(1)}) custom-call(bf16[1024,512]{1,0:T(8,128)(2,1)S(1)} %get-tuple-element.203.query_ref, bf16[1024,512]{1,0:T(8,128)(2,1)S(1)} %get-tuple-element.204.key_ref, ...), custom_call_target="tpu_custom_call" | custom-call | flops 5368709 | bytes 6590 | tf_op jit(solution)/shard_map/pallas_call | solution.py:453
  219.7 6.4 %shard_map.301 = (bf16[1024,128]{1,0:T(8,128)(2,1)S(1)}, bf16[1024,128]{1,0:T(8,128)(2,1)S(1)}, bf16[1024,128]{1,0:T(8,128)(2,1)S(1)}, f32[8,128]{1,0:T(8,128)S(1)}) custom-call(bf16[1024,512]{1,0:T(8,128)(2,1)S(1)} %get-tuple-element.203.query_ref, bf16[1024,512]{1,0:T(8,128)(2,1)S(1)} %get-tuple-element.204.key_ref, ...), custom_call_target="tpu_custom_call" | custom-call | flops 5368709 | bytes 6590 | tf_op jit(solution)/shard_map/pallas_call | solution.py:453
  226.1 6.6 %shard_map.302 = (bf16[1024,128]{1,0:T(8,128)(2,1)S(1)}, bf16[1024,128]{1,0:T(8,128)(2,1)S(1)}, bf16[1024,128]{1,0:T(8,128)(2,1)S(1)}, f32[8,128]{1,0:T(8,128)S(1)}) custom-call(bf16[1024,512]{1,0:T(8,128)(2,1)S(1)} %get-tuple-element.203.query_ref, bf16[1024,512]{1,0:T(8,128)(2,1)S(1)} %get-tuple-element.204.key_ref, ...), custom_call_target="tpu_custom_call" | custom-call | flops 5368709 | bytes 6590 | tf_op jit(solution)/shard_map/pallas_call | solution.py:453
  234.2 6.4 %shard_map.304 = (bf16[1024,128]{1,0:T(8,128)(2,1)S(1)}, bf16[1024,128]{1,0:T(8,128)(2,1)S(1)}, bf16[1024,128]{1,0:T(8,128)(2,1)S(1)}, f32[8,128]{1,0:T(8,128)S(1)}) custom-call(bf16[1024,512]{1,0:T(8,128)(2,1)S(1)} %get-tuple-element.203.query_ref, bf16[1024,512]{1,0:T(8,128)(2,1)S(1)} %get-tuple-element.204.key_ref, ...), custom_call_target="tpu_custom_call" | custom-call | flops 5368709 | bytes 6590 | tf_op jit(solution)/shard_map/pallas_call | solution.py:453
  252.2 8.0 %shard_map.307 = (f32[512,1024]{1,0:T(8,128)S(1)}, bf16[512,1024]{1,0:T(8,128)(2,1)S(1)}, bf16[4,128,512]{2,1,0:T(8,128)(2,1)S(1)}, bf16[4,128,512]{2,1,0:T(8,12...) custom-call(bf16[1024,128]{1,0:T(8,128)(2,1)S(1)} %get-tuple-element.268.refs_1_.refs_0_.refs_21_, ...), custom_call_target="tpu_custom_call" | custom-call | bytes 18874 | tf_op jit(solution)/shard_map/pallas_call | solution.py:453
  268.5 12.3 %shard_map.310 = (bf16[512,1024]{1,0:T(8,128)(2,1)S(1)}, f32[8,1024]{1,0:T(8,128)S(1)}, f32[512,1024]{1,0:T(8,128)S(1)}, bf16[512,1024]{1,0:T(8,128)(2,1)S(1)}) custom-call(f32[512,1024]{1,0:T(8,128)S(1)} %get-tuple-element.275.refs_0_, bf16[512,1024]{1,0:T(8,128)(2,1)S(1)} %shard_map.275.own_ref.refs_1_, f32[512,1024]{1,0:T(8,128)S(1)} %copy-done.54, ...), custom_call_target="tpu_custom_call" | custom-call | bytes 18939 | tf_op jit(solution)/shard_map/pallas_call | solution.py:453
  280.9 9.6 %collective-permute-done.52.refs_1_ = bf16[4,128,512]{2,1,0:T(8,128)(2,1)S(1)} collective-permute-done((bf16[4,128,512]{2,1,0:T(8,128)(2,1)S(1)}, bf16[4,128,512]{2,1,0:T(8,128)(2,1)S(1)}, u32[]{:S(2)}, u32[]{:S(2)}) %collective-permute-start.52) | collective-permute-done | bytes 524320 | tf_op jit(solution)/shard_map/ppermute | solution.py:500
  292.2 11.6 %all_to_all.21 = f32[32,1,512]{2,1,0:T(1,128)S(1)} all-to-all(f32[32,1,512]{2,1,0:T(1,128)S(1)} %copy.31), channel_id=1, replica_groups=mesh['z'=4,'x'=2,'core'=2,'y'=2] {'z','x','core','y'}, dimensions={0} | all-to-all | bytes 131072 | tf_op jit(solution)/shard_map/all_to_all | solution.py:1832
  311.7 16.8 %collective-permute-done.58.refs_6_ = bf16[2,128,512]{2,1,0:T(8,128)(2,1)S(1)} collective-permute-done((bf16[2,128,512]{2,1,0:T(8,128)(2,1)S(1)}, bf16[2,128,512]{2,1,0:T(8,128)(2,1)S(1)}, u32[]{:S(2)}, u32[]{:S(2)}) %collective-permute-start.58) | collective-permute-done | bytes 262176 | tf_op jit(solution)/shard_map/ppermute | solution.py:514
  (368 shorter events, 148.7 us)
Async XLA Ops:
  5.0 22.5 %collective-permute-start.4 = (bf16[512,1024]{1,0:T(8,128)(2,1)}, bf16[512,1024]{1,0:T(8,128)(2,1)S(1)}, u32[]{:S(2)}, u32[]{:S(2)}) collective-permute-start(bf16[512,1024]{1,0:T(8,128)(2,1)} %own_ref), channel_id=1, source_target_pairs={{1,2},{2,1},{5,6},{6,5},{9,10},{10,9},{13,14},{14,13},{17,18},{18,... | collective-permute-start | bytes 3145736 | tf_op jit(solution)/shard_map/ppermute | solution.py:574
  17.7 25.0 %collective-permute-start.9 = (bf16[512,1024]{1,0:T(8,128)(2,1)}, bf16[512,1024]{1,0:T(8,128)(2,1)}, u32[]{:S(2)}, u32[]{:S(2)}) collective-permute-start(bf16[512,1024]{1,0:T(8,128)(2,1)} %own_ref.1), channel_id=1, source_target_pairs={{1,2},{2,1},{5,6},{6,5},{9,10},{10,9},{13,14},{14,13},{17,18},{18,... | collective-permute-start | bytes 3145736 | tf_op jit(solution)/shard_map/ppermute | solution.py:574
  50.3 22.3 %collective-permute-start.17 = (bf16[4,128,512]{2,1,0:T(8,128)(2,1)S(1)}, bf16[4,128,512]{2,1,0:T(8,128)(2,1)S(1)}, u32[]{:S(2)}, u32[]{:S(2)}) collective-permute-start(bf16[4,128,512]{2,1,0:T(8,128)(2,1)S(1)} %shard_map.278.rest_0_.rest_2_.refs_12_), channel_id=1, source_target_pairs={{0,1},{1,0},{2,3},{3,2},{4,5},{5,4},{6,7},{7,6},{8,9},{9,8},{10,11... | collective-permute-start | bytes 1572872 | tf_op jit(solution)/shard_map/ppermute | solution.py:500
  62.5 24.1 %collective-permute-start.14 = (bf16[4,128,512]{2,1,0:T(8,128)(2,1)S(1)}, bf16[4,128,512]{2,1,0:T(8,128)(2,1)S(1)}, u32[]{:S(2)}, u32[]{:S(2)}) collective-permute-start(bf16[4,128,512]{2,1,0:T(8,128)(2,1)S(1)} %collective-permute-done.10.rest_2_.rest_4_.refs_14_), channel_id=1, source_target_pairs={{0,1},{1,0},{2,3},{3,2},{4,5},{5,4},{6,7},{7,6},{8,9},{9,8},{10,11... | collective-permute-start | bytes 1572872 | tf_op jit(solution)/shard_map/ppermute | solution.py:500
  64.4 22.3 %collective-permute-start.15 = (bf16[4,128,512]{2,1,0:T(8,128)(2,1)S(1)}, bf16[4,128,512]{2,1,0:T(8,128)(2,1)S(1)}, u32[]{:S(2)}, u32[]{:S(2)}) collective-permute-start(bf16[4,128,512]{2,1,0:T(8,128)(2,1)S(1)} %collective-permute-done.11.rest_3_.rest_5_.refs_15_), channel_id=1, source_target_pairs={{0,4},{4,0},{1,5},{5,1},{2,6},{6,2},{3,7},{7,3},{8,12},{12,8},{9,1... | collective-permute-start | bytes 1572872 | tf_op jit(solution)/shard_map/ppermute | solution.py:500
  92.5 27.7 %collective-permute-start.25 = (bf16[4,128,512]{2,1,0:T(8,128)(2,1)S(1)}, bf16[4,128,512]{2,1,0:T(8,128)(2,1)S(1)}, u32[]{:S(2)}, u32[]{:S(2)}) collective-permute-start(bf16[4,128,512]{2,1,0:T(8,128)(2,1)S(1)} %shard_map.281.rest_2_.refs_1_), channel_id=1, source_target_pairs={{0,1},{1,0},{2,3},{3,2},{4,5},{5,4},{6,7},{7,6},{8,9},{9,8},{10,11... | collective-permute-start | bytes 1572872 | tf_op jit(solution)/shard_map/ppermute | solution.py:500
  92.6 27.7 %collective-permute-start.26 = (bf16[4,128,512]{2,1,0:T(8,128)(2,1)S(1)}, bf16[4,128,512]{2,1,0:T(8,128)(2,1)S(1)}, u32[]{:S(2)}, u32[]{:S(2)}) collective-permute-start(bf16[4,128,512]{2,1,0:T(8,128)(2,1)S(1)} %shard_map.282.rest_3_.refs_2_), channel_id=1, source_target_pairs={{0,4},{4,0},{1,5},{5,1},{2,6},{6,2},{3,7},{7,3},{8,12},{12,8},{9,1... | collective-permute-start | bytes 1572872 | tf_op jit(solution)/shard_map/ppermute | solution.py:500
  102.5 22.5 %collective-permute-start.27 = (bf16[4,128,512]{2,1,0:T(8,128)(2,1)S(1)}, bf16[4,128,512]{2,1,0:T(8,128)(2,1)S(1)}, u32[]{:S(2)}, u32[]{:S(2)}) collective-permute-start(bf16[4,128,512]{2,1,0:T(8,128)(2,1)S(1)} %collective-permute-done.22.rest_4_.refs_3_), channel_id=1, source_target_pairs={{0,1},{1,0},{2,3},{3,2},{4,5},{5,4},{6,7},{7,6},{8,9},{9,8},{10,11... | collective-permute-start | bytes 1572872 | tf_op jit(solution)/shard_map/ppermute | solution.py:500
  104.0 21.0 %collective-permute-start.28 = (bf16[4,128,512]{2,1,0:T(8,128)(2,1)S(1)}, bf16[4,128,512]{2,1,0:T(8,128)(2,1)S(1)}, u32[]{:S(2)}, u32[]{:S(2)}) collective-permute-start(bf16[4,128,512]{2,1,0:T(8,128)(2,1)S(1)} %collective-permute-done.23.rest_5_.refs_4_), channel_id=1, source_target_pairs={{0,4},{4,0},{1,5},{5,1},{2,6},{6,2},{3,7},{7,3},{8,12},{12,8},{9,1... | collective-permute-start | bytes 1572872 | tf_op jit(solution)/shard_map/ppermute | solution.py:500
  105.2 19.8 %collective-permute-start.29 = (bf16[4,128,512]{2,1,0:T(8,128)(2,1)S(1)}, bf16[4,128,512]{2,1,0:T(8,128)(2,1)S(1)}, u32[]{:S(2)}, u32[]{:S(2)}) collective-permute-start(bf16[4,128,512]{2,1,0:T(8,128)(2,1)S(1)} %collective-permute-done.24.refs_1_.rest_1_.refs_7_), channel_id=1, source_target_pairs={{0,8},{8,16},{16,24},{24,0},{1,9},{9,17},{17,25},{25,1},{2,10},{10... | collective-permute-start | bytes 1572872 | tf_op jit(solution)/shard_map/ppermute | solution.py:514
  135.5 29.3 %collective-permute-start.33 = (bf16[4,128,512]{2,1,0:T(8,128)(2,1)S(1)}, bf16[4,128,512]{2,1,0:T(8,128)(2,1)S(1)}, u32[]{:S(2)}, u32[]{:S(2)}) collective-permute-start(bf16[4,128,512]{2,1,0:T(8,128)(2,1)S(1)} %shard_map.286), channel_id=1, source_target_pairs={{0,1},{1,0},{2,3},{3,2},{4,5},{5,4},{6,7},{7,6},{8,9},{9,8},{10,11... | collective-permute-start | bytes 1572872 | tf_op jit(solution)/shard_map/ppermute | solution.py:500
  136.9 27.8 %collective-permute-start.34 = (bf16[4,128,512]{2,1,0:T(8,128)(2,1)S(1)}, bf16[4,128,512]{2,1,0:T(8,128)(2,1)S(1)}, u32[]{:S(2)}, u32[]{:S(2)}) collective-permute-start(bf16[4,128,512]{2,1,0:T(8,128)(2,1)S(1)} %shard_map.287), channel_id=1, source_target_pairs={{0,4},{4,0},{1,5},{5,1},{2,6},{6,2},{3,7},{7,3},{8,12},{12,8},{9,1... | collective-permute-start | bytes 1572872 | tf_op jit(solution)/shard_map/ppermute | solution.py:500
  164.4 31.6 %collective-permute-start.37 = (bf16[2,2,256,512]{3,2,1,0:T(8,128)(2,1)}, bf16[2,2,256,512]{3,2,1,0:T(8,128)(2,1)S(1)}, u32[]{:S(2)}, u32[]{:S(2)}) collective-permute-start(bf16[2,2,256,512]{3,2,1,0:T(8,128)(2,1)} %get-tuple-element.222), channel_id=1, source_target_pairs={{0,4},{4,0},{1,5},{5,1},{2,6},{6,2},{3,7},{7,3},{8,12},{12,8},{9,1... | collective-permute-start | bytes 3145736 | tf_op jit(solution)/shard_map/ppermute | solution.py:500
  204.0 28.7 %collective-permute-start.41 = (bf16[2,2,256,512]{3,2,1,0:T(8,128)(2,1)}, bf16[2,2,256,512]{3,2,1,0:T(8,128)(2,1)S(1)}, u32[]{:S(2)}, u32[]{:S(2)}) collective-permute-start(bf16[2,2,256,512]{3,2,1,0:T(8,128)(2,1)} %get-tuple-element.223), channel_id=1, source_target_pairs={{0,4},{4,0},{1,5},{5,1},{2,6},{6,2},{3,7},{7,3},{8,12},{12,8},{9,1... | collective-permute-start | bytes 3145736 | tf_op jit(solution)/shard_map/ppermute | solution.py:500
  205.2 29.0 %collective-permute-start.43 = (bf16[2,2,128,1024]{3,2,1,0:T(8,128)(2,1)}, bf16[2,2,128,1024]{3,2,1,0:T(8,128)(2,1)S(1)}, u32[]{:S(2)}, u32[]{:S(2)}) collective-permute-start(bf16[2,2,128,1024]{3,2,1,0:T(8,128)(2,1)} %get-tuple-element.231), channel_id=1, source_target_pairs={{0,1},{1,0},{2,3},{3,2},{4,5},{5,4},{6,7},{7,6},{8,9},{9,8},{10,11... | collective-permute-start | bytes 3145736 | tf_op jit(solution)/shard_map/ppermute | solution.py:500
  219.6 32.5 %collective-permute-start.45 = (bf16[2,2,128,1024]{3,2,1,0:T(8,128)(2,1)S(1)}, bf16[2,2,128,1024]{3,2,1,0:T(8,128)(2,1)S(1)}, u32[]{:S(2)}, u32[]{:S(2)}) collective-permute-start(bf16[2,2,128,1024]{3,2,1,0:T(8,128)(2,1)S(1)} %copy-done.88), channel_id=1, source_target_pairs={{0,1},{1,0},{2,3},{3,2},{4,5},{5,4},{6,7},{7,6},{8,9},{9,8},{10,11... | collective-permute-start | bytes 3145736 | tf_op jit(solution)/shard_map/ppermute | solution.py:500
  264.9 25.6 %collective-permute-start.50 = (bf16[4,128,512]{2,1,0:T(8,128)(2,1)S(1)}, bf16[4,128,512]{2,1,0:T(8,128)(2,1)S(1)}, u32[]{:S(2)}, u32[]{:S(2)}) collective-permute-start(bf16[4,128,512]{2,1,0:T(8,128)(2,1)S(1)} %shard_map.308), channel_id=1, source_target_pairs={{0,4},{4,0},{1,5},{5,1},{2,6},{6,2},{3,7},{7,3},{8,12},{12,8},{9,1... | collective-permute-start | bytes 1572872 | tf_op jit(solution)/shard_map/ppermute | solution.py:500
  266.0 24.6 %collective-permute-start.51 = (bf16[4,128,512]{2,1,0:T(8,128)(2,1)S(1)}, bf16[4,128,512]{2,1,0:T(8,128)(2,1)S(1)}, u32[]{:S(2)}, u32[]{:S(2)}) collective-permute-start(bf16[4,128,512]{2,1,0:T(8,128)(2,1)S(1)} %shard_map.309), channel_id=1, source_target_pairs={{0,1},{1,0},{2,3},{3,2},{4,5},{5,4},{6,7},{7,6},{8,9},{9,8},{10,11... | collective-permute-start | bytes 1572872 | tf_op jit(solution)/shard_map/ppermute | solution.py:500
  266.6 23.9 %collective-permute-start.52 = (bf16[4,128,512]{2,1,0:T(8,128)(2,1)S(1)}, bf16[4,128,512]{2,1,0:T(8,128)(2,1)S(1)}, u32[]{:S(2)}, u32[]{:S(2)}) collective-permute-start(bf16[4,128,512]{2,1,0:T(8,128)(2,1)S(1)} %get-tuple-element.283), channel_id=1, source_target_pairs={{0,1},{1,0},{2,3},{3,2},{4,5},{5,4},{6,7},{7,6},{8,9},{9,8},{10,11... | collective-permute-start | bytes 1572872 | tf_op jit(solution)/shard_map/ppermute | solution.py:500
  267.5 23.0 %collective-permute-start.53 = (bf16[4,128,512]{2,1,0:T(8,128)(2,1)S(1)}, bf16[4,128,512]{2,1,0:T(8,128)(2,1)S(1)}, u32[]{:S(2)}, u32[]{:S(2)}) collective-permute-start(bf16[4,128,512]{2,1,0:T(8,128)(2,1)S(1)} %get-tuple-element.285), channel_id=1, source_target_pairs={{0,4},{4,0},{1,5},{5,1},{2,6},{6,2},{3,7},{7,3},{8,12},{12,8},{9,1... | collective-permute-start | bytes 1572872 | tf_op jit(solution)/shard_map/ppermute | solution.py:500
  268.4 22.2 %collective-permute-start.54 = (bf16[2,128,1024]{2,1,0:T(8,128)(2,1)S(1)}, bf16[2,128,1024]{2,1,0:T(8,128)(2,1)S(1)}, u32[]{:S(2)}, u32[]{:S(2)}) collective-permute-start(bf16[2,128,1024]{2,1,0:T(8,128)(2,1)S(1)} %shard_map.311), channel_id=1, source_target_pairs={{0,8},{8,16},{16,24},{24,0},{1,9},{9,17},{17,25},{25,1},{2,10},{10... | collective-permute-start | bytes 1572872 | tf_op jit(solution)/shard_map/ppermute | solution.py:514
  304.3 24.1 %collective-permute-start.57 = (bf16[512,1024]{1,0:T(8,128)(2,1)S(1)}, bf16[512,1024]{1,0:T(8,128)(2,1)S(1)}, u32[]{:S(2)}, u32[]{:S(2)}) collective-permute-start(bf16[512,1024]{1,0:T(8,128)(2,1)S(1)} %shard_map.314.own_ref), channel_id=1, source_target_pairs={{1,2},{2,1},{5,6},{6,5},{9,10},{10,9},{13,14},{14,13},{17,18},{18,... | collective-permute-start | bytes 3145736 | tf_op jit(solution)/shard_map/ppermute | solution.py:574
  307.6 24.5 %collective-permute-start.59 = (bf16[512,1024]{1,0:T(8,128)(2,1)S(1)}, bf16[512,1024]{1,0:T(8,128)(2,1)S(1)}, u32[]{:S(2)}, u32[]{:S(2)}) collective-permute-start(bf16[512,1024]{1,0:T(8,128)(2,1)S(1)} %get-tuple-element.304.own_ref), channel_id=1, source_target_pairs={{1,2},{2,1},{5,6},{6,5},{9,10},{10,9},{13,14},{14,13},{17,18},{18,... | collective-permute-start | bytes 3145736 | tf_op jit(solution)/shard_map/ppermute | solution.py:574
  310.1 22.1 %collective-permute-start.61 = (bf16[2,128,1024]{2,1,0:T(8,128)(2,1)S(1)}, bf16[2,128,1024]{2,1,0:T(8,128)(2,1)S(1)}, u32[]{:S(2)}, u32[]{:S(2)}) collective-permute-start(bf16[2,128,1024]{2,1,0:T(8,128)(2,1)S(1)} %shard_map.320), channel_id=1, source_target_pairs={{0,8},{8,16},{16,24},{24,0},{1,9},{9,17},{17,25},{25,1},{2,10},{10... | collective-permute-start | bytes 1572872 | tf_op jit(solution)/shard_map/ppermute | solution.py:514
  (135 other events, 2207.9 us)
